TPU v7x, 32 devices: a whole 2x2x4 slice. The times are simulated.
32 devices in a mesh: slab: 8 (over z, x), ctrl: 4 (over y, core).
Axes of the slice: x: 2, y: 2, z: 4, core: 2. Of those that a mesh axis runs over, the one named last changes fastest.
Arguments:
- face_pressure: float32 [131072], P(('slab', 'ctrl')), may hold values from 0 to 18
- face_area: float32 [3, 131072], P(None, ('slab', 'ctrl')), may hold values from -0.015625 to 0.015625
- face_center: float32 [3, 131072], P(None, ('slab', 'ctrl')), may hold values from -6 to 6
- motion: float32 [6], replicated, may hold values from -1 to 1
- inverse_mass: float32 [6], replicated, may hold values from 0.5 to 2
- control_points: float32 [3, 8192], P(None, ('slab', 'ctrl')), may hold values from -4 to 4
- control_modes: float32 [18, 8192], P(None, ('slab', 'ctrl')), may hold values from -0.25 to 0.25
- node_points: float32 [3, 64, 32, 128], P(None, 'slab', 'ctrl'), may hold values from -5 to 5
- tile_list: int32 [64, 32, 16], P('slab', 'ctrl'), may hold values from 0 to 63, as said below
- tile_count: int32 [64, 32], P('slab', 'ctrl'), may hold values from 0 to 16, as said below
Outputs:
- node_shift: float32 [3, 64, 32, 128], P(None, 'slab', 'ctrl')
- cell_volume: float32 [64, 32, 128], P('slab', 'ctrl')
- volume_change: float32 [64, 32, 128], P('slab', 'ctrl')
- new_state: float32 [6], replicated
Inputs may be any that keep to these rules, and one draw needn't show every extreme that they name: `tile_list`: the entries of one line are distinct tile numbers; only the first tile_count entries of a line are live, the others are to be ignored. `tile_count`: every line in the planes x with 192 <= 8 x < 320 has 16 live entries; every other line has at most 4.
All inputs are finite; a program needn't handle non-finite values.
Results may differ from a plain program's by a relative error of at most 0.0003.
Values sent between devices are 32-bit elements; how exact they have to be, the bound alone decides.
No kernel may reach another device: no remote copies, remote signals or barrier semaphores. Data moves between devices by JAX's collectives and lax.ppermute only.
A program may use at most 64 MiB of HBM per device.

v0:
```python
import jax
import jax.numpy as jnp
from jax import lax
from jax.sharding import PartitionSpec as P

TILE = 128


TIME_STEP = 0.5
RADIUS = 4.0
GRAVITY = (0.0, 0.0, -0.5, 0.0, 0.0, 0.0)


def from_behind(value, axis, steps):
    count = lax.axis_size(axis)
    pairs = [(source, (source + steps) % count) for source in range(count)]
    return lax.ppermute(value, axis, pairs)


def shifted(value, axis, by):
    devices = lax.axis_size(axis)
    pairs = [(i, i + by) for i in range(devices) if 0 <= i + by < devices]
    return lax.ppermute(value, axis, pairs)


def surface_loads(pressure, area, center):
    pushed = pressure[None, :] * area
    forces = jnp.sum(pushed, axis=1)
    moment_x = jnp.sum(center[1] * pushed[2] - center[2] * pushed[1])
    moment_y = jnp.sum(center[2] * pushed[0] - center[0] * pushed[2])
    moment_z = jnp.sum(center[0] * pushed[1] - center[1] * pushed[0])
    return jnp.concatenate([forces, jnp.stack([moment_x, moment_y, moment_z])])


def advance(total_loads, motion, inverse_mass):
    acceleration = inverse_mass * total_loads + jnp.array(GRAVITY, dtype=jnp.float32)
    new_state = motion + TIME_STEP * acceleration
    rigid_step = TIME_STEP * motion + 0.5 * TIME_STEP * TIME_STEP * acceleration
    return (new_state, rigid_step)


def mode_mix(rigid_step, modes):
    shaped = modes.reshape(6, 3, modes.shape[1])
    return jnp.einsum("k,kcj->cj", rigid_step, shaped, precision=lax.Precision.HIGHEST)


def kernel_sum(points, tile_ids, counts, center_tiles, coeff_tiles):
    longest = jnp.max(counts)

    def accumulate(entry_id, running):
        picked = jnp.take(tile_ids, entry_id, axis=1)
        centers = jnp.take(center_tiles, picked, axis=1)
        coeffs = jnp.take(coeff_tiles, picked, axis=1)
        square = jnp.zeros((points.shape[1], points.shape[2], centers.shape[2]), jnp.float32)
        for axis_id in range(3):
            offset = points[axis_id][:, :, None] - centers[axis_id][:, None, :]
            square = square + offset * offset
        radial = jnp.sqrt(square) / RADIUS
        falloff = jnp.maximum(1.0 - radial, 0.0)
        fourth = falloff * falloff
        fourth = fourth * fourth
        kernel = fourth * (4.0 * radial + 1.0)
        alive_mask = (entry_id < counts)[:, None, None]
        kernel = jnp.where(alive_mask, kernel, 0.0)
        return running + jnp.einsum("lnj,clj->cln", kernel, coeffs, precision=lax.Precision.HIGHEST)

    start = jnp.zeros((3, points.shape[1], points.shape[2]), jnp.float32)
    return lax.fori_loop(0, longest, accumulate, start)


def cell_volumes(lattice):
    span_x = lattice.shape[-3] - 1
    span_y = lattice.shape[-2] - 1
    corners = {}
    for shift_x in range(2):
        for shift_y in range(2):
            for shift_z in range(2):
                sliced = lattice[..., shift_x : shift_x + span_x, shift_y : shift_y + span_y, :]
                if shift_z == 1:
                    sliced = jnp.concatenate(
                        [sliced[..., 1:], jnp.zeros_like(sliced[..., :1])], axis=-1
                    )
                corners[shift_x, shift_y, shift_z] = sliced
    edge_x = 0.0
    edge_y = 0.0
    edge_z = 0.0
    for first in range(2):
        for second in range(2):
            edge_x = edge_x + corners[1, first, second] - corners[0, first, second]
            edge_y = edge_y + corners[first, 1, second] - corners[first, 0, second]
            edge_z = edge_z + corners[first, second, 1] - corners[first, second, 0]
    edge_x = 0.25 * edge_x
    edge_y = 0.25 * edge_y
    edge_z = 0.25 * edge_z
    ex0, ex1, ex2 = (edge_x[..., 0, :, :, :], edge_x[..., 1, :, :, :], edge_x[..., 2, :, :, :])
    ey0, ey1, ey2 = (edge_y[..., 0, :, :, :], edge_y[..., 1, :, :, :], edge_y[..., 2, :, :, :])
    ez0, ez1, ez2 = (edge_z[..., 0, :, :, :], edge_z[..., 1, :, :, :], edge_z[..., 2, :, :, :])
    return (
        ex0 * (ey1 * ez2 - ey2 * ez1)
        + ex1 * (ey2 * ez0 - ey0 * ez2)
        + ex2 * (ey0 * ez1 - ey1 * ez0)
    )


def local(
    face_pressure,
    face_area,
    face_center,
    motion,
    inverse_mass,
    control_points,
    control_modes,
    node_points,
    tile_list,
    tile_count,
):
    local_loads = surface_loads(face_pressure, face_area, face_center)
    centers_all, modes_all = (
        lax.all_gather(control_points, ("slab", "ctrl"), axis=1, tiled=True),
        lax.all_gather(control_modes, ("slab", "ctrl"), axis=1, tiled=True),
    )
    total_loads = lax.psum(local_loads, ("slab", "ctrl"))
    new_state, rigid_step = advance(total_loads, motion, inverse_mass)
    coeffs_all = mode_mix(rigid_step, modes_all)
    center_tiles = centers_all.reshape(3, -1, TILE)
    coeff_tiles = coeffs_all.reshape(3, -1, TILE)
    plane_count = node_points.shape[1]
    row_count = node_points.shape[2]
    line_nodes = node_points.shape[3]
    slots = tile_list.shape[2]
    half_rows = row_count // 2
    half_slab = lax.axis_size("slab") // 2
    kept_points = node_points[:, :, :half_rows].reshape(3, -1, line_nodes)
    kept_ids = tile_list[:, :half_rows].reshape(-1, slots)
    kept_counts = tile_count[:, :half_rows].reshape(-1)
    sent_points = node_points[:, :, half_rows:].reshape(3, -1, line_nodes)
    sent_ids = tile_list[:, half_rows:].reshape(-1, slots)
    sent_counts = tile_count[:, half_rows:].reshape(-1)
    got_points, got_ids, got_counts = from_behind(
        (sent_points, sent_ids, sent_counts), "slab", half_slab
    )
    own_part = kernel_sum(kept_points, kept_ids, kept_counts, center_tiles, coeff_tiles)
    lent_part = kernel_sum(got_points, got_ids, got_counts, center_tiles, coeff_tiles)
    came_back = from_behind(lent_part, "slab", half_slab)
    node_shift = jnp.concatenate(
        [
            own_part.reshape(3, plane_count, half_rows, line_nodes),
            came_back.reshape(3, plane_count, row_count - half_rows, line_nodes),
        ],
        axis=2,
    )
    displaced = node_points + node_shift
    stacked = jnp.stack([node_points, displaced])
    next_plane = shifted(stacked[:, :, :1], "slab", -1)
    widened = jnp.concatenate([stacked, next_plane], axis=2)
    next_row = shifted(widened[:, :, :, :1], "ctrl", -1)
    extended = jnp.concatenate([widened, next_row], axis=3)
    volumes = cell_volumes(extended)
    plane_total = plane_count * lax.axis_size("slab")
    row_total = row_count * lax.axis_size("ctrl")
    plane_ids = lax.axis_index("slab") * plane_count + jnp.arange(plane_count, dtype=jnp.int32)
    row_ids = lax.axis_index("ctrl") * row_count + jnp.arange(row_count, dtype=jnp.int32)
    depth_ids = jnp.arange(line_nodes, dtype=jnp.int32)
    inside = (plane_ids < plane_total - 1)[:, None, None]
    inside = inside & (row_ids < row_total - 1)[None, :, None]
    inside = inside & (depth_ids < line_nodes - 1)[None, None, :]
    volumes = jnp.where(inside[None], volumes, 0.0)
    return (node_shift, volumes[1], volumes[1] - volumes[0], new_state)


def solution(mesh):
    placed = (
        P(("slab", "ctrl")),
        P(None, ("slab", "ctrl")),
        P(None, ("slab", "ctrl")),
        P(),
        P(),
        P(None, ("slab", "ctrl")),
        P(None, ("slab", "ctrl")),
        P(None, "slab", "ctrl", None),
        P("slab", "ctrl", None),
        P("slab", "ctrl"),
    )
    return jax.shard_map(
        local,
        mesh=mesh,
        in_specs=placed,
        out_specs=(
            P(None, "slab", "ctrl", None),
            P("slab", "ctrl", None),
            P("slab", "ctrl", None),
            P(),
        ),
        check_vma=False,
    )
```

profile of v0, /device:TPU:0, one launch (start us, length us, event | category | flops | bytes accessed | tf_op | source)
XLA Modules:
  0.0 303.0 jit_solution(9148817950466568534)
XLA Ops:
  0.6 1.5 fusion.109
  2.2 4.0 %collective-permute-start = (s32[32]{0:T(128)S(1)}, s32[32]{0:T(128)S(1)}, u32[]{:S(2)}, u32[]{:S(2)}) collective-permute-start(s32[32]{0:T(128)S(1)} %reshape.142), channel_id=1, source_target_pairs={{0,16},{4,20},{8,24},{12,28},{16,0},{20,4},{24,8},{28,12},{1,17},{... | collective-permute-start | bytes 392 | tf_op jit(solution)/shard_map/ppermute | solution.py:17
  6.2 0.8 fusion.108
  7.1 1.0 fusion.107
  8.1 3.0 collective-permute-start.2
  11.1 41.9 %all_gather.6 = f32[18,8192]{1,0:T(8,128)S(1)} all-gather(f32[18,256]{1,0:T(8,128)} %param.25), channel_id=1, replica_groups=mesh['slab'=8,'ctrl'=4] {'slab','ctrl'}, dimensions={1}, use_global_device_ids=true | all-gather | bytes 608256 | tf_op jit(solution)/shard_map/all_gather | solution.py:120
  53.9 0.7 subtract_reduce_fusion.2
  54.7 2.0 pad_maximum_fusion.5
  57.1 36.9 %psum.7 = f32[6]{0:T(128)S(1)} all-reduce(f32[6]{0:T(128)S(1)} %pad_maximum_fusion.5), channel_id=1, replica_groups=mesh['slab'=8,'ctrl'=4] {'slab','ctrl'}, use_global_device_ids=true, to_apply=%region_5.0 | all-reduce | flops 6 | bytes 48 | tf_op jit(solution)/shard_map/psum | solution.py:122
  94.0 1.1 fusion.86
  95.2 40.5 %all_gather.7 = f32[3,8192]{1,0:T(4,128)S(1)} all-gather(f32[3,256]{1,0:T(4,128)S(1)} %copy-done.4), channel_id=1, replica_groups=mesh['slab'=8,'ctrl'=4] {'slab','ctrl'}, dimensions={1}, use_global_device_ids=true | all-gather | bytes 101376 | tf_op jit(solution)/shard_map/all_gather | solution.py:119
  135.9 30.4 %while.25 = (s32[]{:T(128)}, f32[3,32,128]{2,0,1:T(4,128)S(1)}, s32[]{:T(128)}, s32[32,16]{0,1:T(8,128)S(1)}, f32[3,64,128]{2,0,1:T(4,128)S(1)}, /*index=5*/s32[...) while((s32[]{:T(128)}, f32[3,32,128]{2,0,1:T(4,128)S(1)}, ...), condition=%wide.region_7.10_spmd, body=%wide.region_6.9_spmd.sunk | while | flops 27301128 | bytes 742493 | solution.py:68
  138.0 5.3 %fusion.121 = f32[3,32,128]{2,0,1:T(4,128)S(1)} fusion(f32[3,32,128]{2,0,1:T(4,128)S(1)} %get-tuple-element.500, f32[32,128]{1,0:T(8,128)S(1)} %bitcast.121, f32[32,128]{1,0:T(8,128)S(1)} %get-tuple-element.428, f32[32,128]{1,0:T(8,128)S(1)} %bitcast.122, f32[32,128]{1,0:T(8,128)S(1)} %get-tuple-element.430, f32[32,128]{1,0:T(8,128)S(1)} %bitcast.120, ...), kind=kOutput, calls=%fused_computation.23.clone.1 | convolution fusion | flops 27287552 | bytes 245824 | tf_op jit(solution)/shard_map/while/body/lnj,clj->cln/dot_general | solution.py:65
  144.1 0.6 gather_fusion
  144.8 0.6 gather_fusion.1
  145.5 5.3 %fusion.121 = f32[3,32,128]{2,0,1:T(4,128)S(1)} fusion(f32[3,32,128]{2,0,1:T(4,128)S(1)} %get-tuple-element.500, f32[32,128]{1,0:T(8,128)S(1)} %bitcast.121, f32[32,128]{1,0:T(8,128)S(1)} %get-tuple-element.428, f32[32,128]{1,0:T(8,128)S(1)} %bitcast.122, f32[32,128]{1,0:T(8,128)S(1)} %get-tuple-element.430, f32[32,128]{1,0:T(8,128)S(1)} %bitcast.120, ...), kind=kOutput, calls=%fused_computation.23.clone.1 | convolution fusion | flops 27287552 | bytes 245824 | tf_op jit(solution)/shard_map/while/body/lnj,clj->cln/dot_general | solution.py:65
  152.9 5.3 %fusion.121 = f32[3,32,128]{2,0,1:T(4,128)S(1)} fusion(f32[3,32,128]{2,0,1:T(4,128)S(1)} %get-tuple-element.500, f32[32,128]{1,0:T(8,128)S(1)} %bitcast.121, f32[32,128]{1,0:T(8,128)S(1)} %get-tuple-element.428, f32[32,128]{1,0:T(8,128)S(1)} %bitcast.122, f32[32,128]{1,0:T(8,128)S(1)} %get-tuple-element.430, f32[32,128]{1,0:T(8,128)S(1)} %bitcast.120, ...), kind=kOutput, calls=%fused_computation.23.clone.1 | convolution fusion | flops 27287552 | bytes 245824 | tf_op jit(solution)/shard_map/while/body/lnj,clj->cln/dot_general | solution.py:65
  158.9 0.6 gather_fusion
  160.3 5.3 %fusion.121 = f32[3,32,128]{2,0,1:T(4,128)S(1)} fusion(f32[3,32,128]{2,0,1:T(4,128)S(1)} %get-tuple-element.500, f32[32,128]{1,0:T(8,128)S(1)} %bitcast.121, f32[32,128]{1,0:T(8,128)S(1)} %get-tuple-element.428, f32[32,128]{1,0:T(8,128)S(1)} %bitcast.122, f32[32,128]{1,0:T(8,128)S(1)} %get-tuple-element.430, f32[32,128]{1,0:T(8,128)S(1)} %bitcast.120, ...), kind=kOutput, calls=%fused_computation.23.clone.1 | convolution fusion | flops 27287552 | bytes 245824 | tf_op jit(solution)/shard_map/while/body/lnj,clj->cln/dot_general | solution.py:65
  166.5 0.6 reduce_max.19
  167.3 119.7 %while.26 = (s32[]{:T(128)}, f32[3,32,128]{2,0,1:T(4,128)S(1)}, s32[]{:T(128)}, s32[32,16]{0,1:T(8,128)S(1)}, f32[3,64,128]{2,0,1:T(4,128)S(1)}, /*index=5*/s32[...) while((s32[]{:T(128)}, f32[3,32,128]{2,0,1:T(4,128)S(1)}, ...), condition=%wide.region_10.13_spmd, body=%wide.region_9.12_spmd.sunk | while | flops 27301128 | bytes 742493 | solution.py:68
  169.4 5.3 %fusion.125 = f32[3,32,128]{2,0,1:T(4,128)S(1)} fusion(f32[3,32,128]{2,0,1:T(4,128)S(1)} %get-tuple-element.464, f32[32,128]{1,0:T(8,128)S(1)} %bitcast.124, f32[32,128]{1,0:T(8,128)S(1)} %get-tuple-element.445, f32[32,128]{1,0:T(8,128)S(1)} %bitcast.125, f32[32,128]{1,0:T(8,128)S(1)} %get-tuple-element.447, f32[32,128]{1,0:T(8,128)S(1)} %bitcast.123, ...), kind=kOutput, calls=%fused_computation.71.clone.1 | convolution fusion | flops 27287552 | bytes 245824 | tf_op jit(solution)/shard_map/while/body/lnj,clj->cln/dot_general | solution.py:65
  175.4 0.6 gather_fusion.2
  176.2 0.6 gather_fusion.3
  176.8 5.3 %fusion.125 = f32[3,32,128]{2,0,1:T(4,128)S(1)} fusion(f32[3,32,128]{2,0,1:T(4,128)S(1)} %get-tuple-element.464, f32[32,128]{1,0:T(8,128)S(1)} %bitcast.124, f32[32,128]{1,0:T(8,128)S(1)} %get-tuple-element.445, f32[32,128]{1,0:T(8,128)S(1)} %bitcast.125, f32[32,128]{1,0:T(8,128)S(1)} %get-tuple-element.447, f32[32,128]{1,0:T(8,128)S(1)} %bitcast.123, ...), kind=kOutput, calls=%fused_computation.71.clone.1 | convolution fusion | flops 27287552 | bytes 245824 | tf_op jit(solution)/shard_map/while/body/lnj,clj->cln/dot_general | solution.py:65
  182.9 0.6 gather_fusion.2
  183.6 0.6 gather_fusion.3
  184.3 5.3 %fusion.125 = f32[3,32,128]{2,0,1:T(4,128)S(1)} fusion(f32[3,32,128]{2,0,1:T(4,128)S(1)} %get-tuple-element.464, f32[32,128]{1,0:T(8,128)S(1)} %bitcast.124, f32[32,128]{1,0:T(8,128)S(1)} %get-tuple-element.445, f32[32,128]{1,0:T(8,128)S(1)} %bitcast.125, f32[32,128]{1,0:T(8,128)S(1)} %get-tuple-element.447, f32[32,128]{1,0:T(8,128)S(1)} %bitcast.123, ...), kind=kOutput, calls=%fused_computation.71.clone.1 | convolution fusion | flops 27287552 | bytes 245824 | tf_op jit(solution)/shard_map/while/body/lnj,clj->cln/dot_general | solution.py:65
  190.3 0.6 gather_fusion.2
  191.1 0.6 gather_fusion.3
  191.7 5.3 %fusion.125 = f32[3,32,128]{2,0,1:T(4,128)S(1)} fusion(f32[3,32,128]{2,0,1:T(4,128)S(1)} %get-tuple-element.464, f32[32,128]{1,0:T(8,128)S(1)} %bitcast.124, f32[32,128]{1,0:T(8,128)S(1)} %get-tuple-element.445, f32[32,128]{1,0:T(8,128)S(1)} %bitcast.125, f32[32,128]{1,0:T(8,128)S(1)} %get-tuple-element.447, f32[32,128]{1,0:T(8,128)S(1)} %bitcast.123, ...), kind=kOutput, calls=%fused_computation.71.clone.1 | convolution fusion | flops 27287552 | bytes 245824 | tf_op jit(solution)/shard_map/while/body/lnj,clj->cln/dot_general | solution.py:65
  197.8 0.6 gather_fusion.2
  198.5 0.6 gather_fusion.3
  199.1 5.3 %fusion.125 = f32[3,32,128]{2,0,1:T(4,128)S(1)} fusion(f32[3,32,128]{2,0,1:T(4,128)S(1)} %get-tuple-element.464, f32[32,128]{1,0:T(8,128)S(1)} %bitcast.124, f32[32,128]{1,0:T(8,128)S(1)} %get-tuple-element.445, f32[32,128]{1,0:T(8,128)S(1)} %bitcast.125, f32[32,128]{1,0:T(8,128)S(1)} %get-tuple-element.447, f32[32,128]{1,0:T(8,128)S(1)} %bitcast.123, ...), kind=kOutput, calls=%fused_computation.71.clone.1 | convolution fusion | flops 27287552 | bytes 245824 | tf_op jit(solution)/shard_map/while/body/lnj,clj->cln/dot_general | solution.py:65
  206.6 5.3 %fusion.125 = f32[3,32,128]{2,0,1:T(4,128)S(1)} fusion(f32[3,32,128]{2,0,1:T(4,128)S(1)} %get-tuple-element.464, f32[32,128]{1,0:T(8,128)S(1)} %bitcast.124, f32[32,128]{1,0:T(8,128)S(1)} %get-tuple-element.445, f32[32,128]{1,0:T(8,128)S(1)} %bitcast.125, f32[32,128]{1,0:T(8,128)S(1)} %get-tuple-element.447, f32[32,128]{1,0:T(8,128)S(1)} %bitcast.123, ...), kind=kOutput, calls=%fused_computation.71.clone.1 | convolution fusion | flops 27287552 | bytes 245824 | tf_op jit(solution)/shard_map/while/body/lnj,clj->cln/dot_general | solution.py:65
  212.6 0.6 gather_fusion.2
  213.4 0.6 gather_fusion.3
  214.0 5.3 %fusion.125 = f32[3,32,128]{2,0,1:T(4,128)S(1)} fusion(f32[3,32,128]{2,0,1:T(4,128)S(1)} %get-tuple-element.464, f32[32,128]{1,0:T(8,128)S(1)} %bitcast.124, f32[32,128]{1,0:T(8,128)S(1)} %get-tuple-element.445, f32[32,128]{1,0:T(8,128)S(1)} %bitcast.125, f32[32,128]{1,0:T(8,128)S(1)} %get-tuple-element.447, f32[32,128]{1,0:T(8,128)S(1)} %bitcast.123, ...), kind=kOutput, calls=%fused_computation.71.clone.1 | convolution fusion | flops 27287552 | bytes 245824 | tf_op jit(solution)/shard_map/while/body/lnj,clj->cln/dot_general | solution.py:65
  221.5 5.3 %fusion.125 = f32[3,32,128]{2,0,1:T(4,128)S(1)} fusion(f32[3,32,128]{2,0,1:T(4,128)S(1)} %get-tuple-element.464, f32[32,128]{1,0:T(8,128)S(1)} %bitcast.124, f32[32,128]{1,0:T(8,128)S(1)} %get-tuple-element.445, f32[32,128]{1,0:T(8,128)S(1)} %bitcast.125, f32[32,128]{1,0:T(8,128)S(1)} %get-tuple-element.447, f32[32,128]{1,0:T(8,128)S(1)} %bitcast.123, ...), kind=kOutput, calls=%fused_computation.71.clone.1 | convolution fusion | flops 27287552 | bytes 245824 | tf_op jit(solution)/shard_map/while/body/lnj,clj->cln/dot_general | solution.py:65
  227.5 0.6 gather_fusion.2
  228.3 0.6 gather_fusion.3
  228.9 5.3 %fusion.125 = f32[3,32,128]{2,0,1:T(4,128)S(1)} fusion(f32[3,32,128]{2,0,1:T(4,128)S(1)} %get-tuple-element.464, f32[32,128]{1,0:T(8,128)S(1)} %bitcast.124, f32[32,128]{1,0:T(8,128)S(1)} %get-tuple-element.445, f32[32,128]{1,0:T(8,128)S(1)} %bitcast.125, f32[32,128]{1,0:T(8,128)S(1)} %get-tuple-element.447, f32[32,128]{1,0:T(8,128)S(1)} %bitcast.123, ...), kind=kOutput, calls=%fused_computation.71.clone.1 | convolution fusion | flops 27287552 | bytes 245824 | tf_op jit(solution)/shard_map/while/body/lnj,clj->cln/dot_general | solution.py:65
  236.3 5.3 %fusion.125 = f32[3,32,128]{2,0,1:T(4,128)S(1)} fusion(f32[3,32,128]{2,0,1:T(4,128)S(1)} %get-tuple-element.464, f32[32,128]{1,0:T(8,128)S(1)} %bitcast.124, f32[32,128]{1,0:T(8,128)S(1)} %get-tuple-element.445, f32[32,128]{1,0:T(8,128)S(1)} %bitcast.125, f32[32,128]{1,0:T(8,128)S(1)} %get-tuple-element.447, f32[32,128]{1,0:T(8,128)S(1)} %bitcast.123, ...), kind=kOutput, calls=%fused_computation.71.clone.1 | convolution fusion | flops 27287552 | bytes 245824 | tf_op jit(solution)/shard_map/while/body/lnj,clj->cln/dot_general | solution.py:65
  243.8 5.3 %fusion.125 = f32[3,32,128]{2,0,1:T(4,128)S(1)} fusion(f32[3,32,128]{2,0,1:T(4,128)S(1)} %get-tuple-element.464, f32[32,128]{1,0:T(8,128)S(1)} %bitcast.124, f32[32,128]{1,0:T(8,128)S(1)} %get-tuple-element.445, f32[32,128]{1,0:T(8,128)S(1)} %bitcast.125, f32[32,128]{1,0:T(8,128)S(1)} %get-tuple-element.447, f32[32,128]{1,0:T(8,128)S(1)} %bitcast.123, ...), kind=kOutput, calls=%fused_computation.71.clone.1 | convolution fusion | flops 27287552 | bytes 245824 | tf_op jit(solution)/shard_map/while/body/lnj,clj->cln/dot_general | solution.py:65
  249.8 0.6 gather_fusion.2
  250.6 0.6 gather_fusion.3
  251.2 5.3 %fusion.125 = f32[3,32,128]{2,0,1:T(4,128)S(1)} fusion(f32[3,32,128]{2,0,1:T(4,128)S(1)} %get-tuple-element.464, f32[32,128]{1,0:T(8,128)S(1)} %bitcast.124, f32[32,128]{1,0:T(8,128)S(1)} %get-tuple-element.445, f32[32,128]{1,0:T(8,128)S(1)} %bitcast.125, f32[32,128]{1,0:T(8,128)S(1)} %get-tuple-element.447, f32[32,128]{1,0:T(8,128)S(1)} %bitcast.123, ...), kind=kOutput, calls=%fused_computation.71.clone.1 | convolution fusion | flops 27287552 | bytes 245824 | tf_op jit(solution)/shard_map/while/body/lnj,clj->cln/dot_general | solution.py:65
  257.3 0.6 gather_fusion.2
  258.0 0.6 gather_fusion.3
  258.7 5.3 %fusion.125 = f32[3,32,128]{2,0,1:T(4,128)S(1)} fusion(f32[3,32,128]{2,0,1:T(4,128)S(1)} %get-tuple-element.464, f32[32,128]{1,0:T(8,128)S(1)} %bitcast.124, f32[32,128]{1,0:T(8,128)S(1)} %get-tuple-element.445, f32[32,128]{1,0:T(8,128)S(1)} %bitcast.125, f32[32,128]{1,0:T(8,128)S(1)} %get-tuple-element.447, f32[32,128]{1,0:T(8,128)S(1)} %bitcast.123, ...), kind=kOutput, calls=%fused_computation.71.clone.1 | convolution fusion | flops 27287552 | bytes 245824 | tf_op jit(solution)/shard_map/while/body/lnj,clj->cln/dot_general | solution.py:65
  264.7 0.6 gather_fusion.2
  265.5 0.6 gather_fusion.3
  266.1 5.3 %fusion.125 = f32[3,32,128]{2,0,1:T(4,128)S(1)} fusion(f32[3,32,128]{2,0,1:T(4,128)S(1)} %get-tuple-element.464, f32[32,128]{1,0:T(8,128)S(1)} %bitcast.124, f32[32,128]{1,0:T(8,128)S(1)} %get-tuple-element.445, f32[32,128]{1,0:T(8,128)S(1)} %bitcast.125, f32[32,128]{1,0:T(8,128)S(1)} %get-tuple-element.447, f32[32,128]{1,0:T(8,128)S(1)} %bitcast.123, ...), kind=kOutput, calls=%fused_computation.71.clone.1 | convolution fusion | flops 27287552 | bytes 245824 | tf_op jit(solution)/shard_map/while/body/lnj,clj->cln/dot_general | solution.py:65
  273.5 5.3 %fusion.125 = f32[3,32,128]{2,0,1:T(4,128)S(1)} fusion(f32[3,32,128]{2,0,1:T(4,128)S(1)} %get-tuple-element.464, f32[32,128]{1,0:T(8,128)S(1)} %bitcast.124, f32[32,128]{1,0:T(8,128)S(1)} %get-tuple-element.445, f32[32,128]{1,0:T(8,128)S(1)} %bitcast.125, f32[32,128]{1,0:T(8,128)S(1)} %get-tuple-element.447, f32[32,128]{1,0:T(8,128)S(1)} %bitcast.123, ...), kind=kOutput, calls=%fused_computation.71.clone.1 | convolution fusion | flops 27287552 | bytes 245824 | tf_op jit(solution)/shard_map/while/body/lnj,clj->cln/dot_general | solution.py:65
  279.6 0.6 gather_fusion.2
  280.4 0.6 gather_fusion.3
  281.0 5.3 %fusion.125 = f32[3,32,128]{2,0,1:T(4,128)S(1)} fusion(f32[3,32,128]{2,0,1:T(4,128)S(1)} %get-tuple-element.464, f32[32,128]{1,0:T(8,128)S(1)} %bitcast.124, f32[32,128]{1,0:T(8,128)S(1)} %get-tuple-element.445, f32[32,128]{1,0:T(8,128)S(1)} %bitcast.125, f32[32,128]{1,0:T(8,128)S(1)} %get-tuple-element.447, f32[32,128]{1,0:T(8,128)S(1)} %bitcast.123, ...), kind=kOutput, calls=%fused_computation.71.clone.1 | convolution fusion | flops 27287552 | bytes 245824 | tf_op jit(solution)/shard_map/while/body/lnj,clj->cln/dot_general | solution.py:65
  287.6 4.7 %collective-permute-done.3 = f32[3,32,128]{2,0,1:T(4,128)S(1)} collective-permute-done((f32[3,32,128]{2,0,1:T(4,128)S(1)}, f32[3,32,128]{2,0,1:T(4,128)S(1)}, u32[]{:S(2)}, u32[]{:S(2)}) %collective-permute-start.3) | collective-permute-done | bytes 49184 | tf_op jit(solution)/shard_map/ppermute | solution.py:17
  292.3 0.7 add_bitcast_fusion
  293.0 1.3 collective-permute-start.4
  294.4 4.3 %collective-permute-done.4 = f32[2,3,1,8,128]{4,3,2,0,1:T(8,128)S(1)} collective-permute-done((f32[2,3,1,8,128]{4,3,2,0,1:T(8,128)S(1)}, f32[2,3,1,8,128]{4,3,2,0,1:T(8,128)S(1)}, u32[]{:S(2)}, u32[]{:S(2)}) %collective-permute-start.4) | collective-permute-done | bytes 24608 | tf_op jit(solution)/shard_map/ppermute | solution.py:23
  298.7 1.3 collective-permute-start.5
  300.1 1.7 collective-permute-done.5
  302.3 0.6 fusion.93
  (165 shorter events, 17.1 us)
Async XLA Ops:
  2.2 164.3 %collective-permute-start = (s32[32]{0:T(128)S(1)}, s32[32]{0:T(128)S(1)}, u32[]{:S(2)}, u32[]{:S(2)}) collective-permute-start(s32[32]{0:T(128)S(1)} %reshape.142), channel_id=1, source_target_pairs={{0,16},{4,20},{8,24},{12,28},{16,0},{20,4},{24,8},{28,12},{1,17},{... | collective-permute-start | bytes 392 | tf_op jit(solution)/shard_map/ppermute | solution.py:17
  7.1 160.1 %collective-permute-start.1 = (s32[32,16]{1,0:T(8,128)S(1)}, s32[32,16]{1,0:T(8,128)S(1)}, u32[]{:S(2)}, u32[]{:S(2)}) collective-permute-start(s32[32,16]{1,0:T(8,128)S(1)} %bitcast.130), channel_id=1, source_target_pairs={{0,16},{4,20},{8,24},{12,28},{16,0},{20,4},{24,8},{28,12},{1,17},{... | collective-permute-start | bytes 6152 | tf_op jit(solution)/shard_map/ppermute | solution.py:17
  8.1 159.1 %collective-permute-start.2 = (f32[3,32,128]{2,1,0:T(8,128)S(1)}, f32[3,32,128]{2,1,0:T(8,128)S(1)}, u32[]{:S(2)}, u32[]{:S(2)}) collective-permute-start(f32[3,32,128]{2,1,0:T(8,128)S(1)} %bitcast.129), channel_id=1, source_target_pairs={{0,16},{4,20},{8,24},{12,28},{16,0},{20,4},{24,8},{28,12},{1,17},{... | collective-permute-start | bytes 147464 | tf_op jit(solution)/shard_map/ppermute | solution.py:17
  52.9 0.8 copy-start.1
  52.9 0.8 copy-start.3
  52.9 1.0 copy-start.2
  53.8 40.3 %copy-start.5 = (f32[6]{0:T(128)S(1)}, f32[6]{0:T(128)}, u32[]{:S(2)}) copy-start(f32[6]{0:T(128)} %param.22) | copy-start | bytes 76
  53.8 40.3 %copy-start.6 = (f32[6]{0:T(128)S(1)}, f32[6]{0:T(128)}, u32[]{:S(2)}) copy-start(f32[6]{0:T(128)} %param.23) | copy-start | bytes 76
  53.8 40.3 %copy-start.7 = (f32[6]{0:T(128)S(1)}, f32[6]{0:T(128)}, u32[]{:S(2)}) copy-start(f32[6]{0:T(128)} %constant.108.clone) | copy-start | bytes 76
  57.1 38.1 %copy-start.4 = (f32[3,256]{1,0:T(4,128)S(1)}, f32[3,256]{1,0:T(4,128)}, u32[]{:S(2)}) copy-start(f32[3,256]{1,0:T(4,128)} %param.24) | copy-start | bytes 9220
  167.2 125.0 %copy-start = (f32[3,8,8,128]{3,2,1,0:T(8,128)S(1)}, f32[3,8,8,128]{3,2,1,0:T(8,128)}, u32[]{:S(2)}) copy-start(f32[3,8,8,128]{3,2,1,0:T(8,128)} %param.26) | copy-start | bytes 294916
  287.0 5.3 %collective-permute-start.3 = (f32[3,32,128]{2,0,1:T(4,128)S(1)}, f32[3,32,128]{2,0,1:T(4,128)S(1)}, u32[]{:S(2)}, u32[]{:S(2)}) collective-permute-start(f32[3,32,128]{2,0,1:T(4,128)S(1)} %get-tuple-element.215), channel_id=1, source_target_pairs={{0,16},{4,20},{8,24},{12,28},{16,0},{20,4},{24,8},{28,12},{1,17},{... | collective-permute-start | bytes 147464 | tf_op jit(solution)/shard_map/ppermute | solution.py:17
  293.0 5.7 %collective-permute-start.4 = (f32[2,3,1,8,128]{4,3,2,0,1:T(8,128)S(1)}, f32[2,3,1,8,128]{4,3,2,0,1:T(8,128)S(1)}, u32[]{:S(2)}, u32[]{:S(2)}) collective-permute-start(f32[2,3,1,8,128]{4,3,2,0,1:T(8,128)S(1)} %fusion.94), channel_id=1, source_target_pairs={{4,0},{8,4},{12,8},{16,12},{20,16},{24,20},{28,24},{5,1},{9,5},{13... | collective-permute-start | bytes 73736 | tf_op jit(solution)/shard_map/ppermute | solution.py:23
  298.7 3.1 %collective-permute-start.5 = (f32[2,3,9,1,128]{4,3,2,0,1:T(1,128)S(1)}, f32[2,3,9,1,128]{4,3,2,0,1:T(1,128)S(1)}, u32[]{:S(2)}, u32[]{:S(2)}) collective-permute-start(f32[2,3,9,1,128]{4,3,2,0,1:T(1,128)S(1)} %pad_maximum_fusion.4), channel_id=1, source_target_pairs={{1,0},{2,1},{3,2},{5,4},{6,5},{7,6},{9,8},{10,9},{11,10},{13,12},{... | collective-permute-start | bytes 82952 | tf_op jit(solution)/shard_map/ppermute | solution.py:23
where the time goes:
time: 304 us; the launch traced here: 303 us
  blocking collectives  119 us (39%)
  matrix products  108 us (36%)
  local copies, waits for them, and re-layouts  29 us (10%)
  loops' own time  15.9 us (5%)
  waiting for transfers between devices  10.7 us (4%)
  other arithmetic  9.94 us (3%)
  starting transfers between devices  9.69 us (3%)
    dot_general x20, matrix products, accumulate(): jnp.einsum('lnj,clj->cln', kernel, coeffs, precision=lax.Precision.HIGHEST)  107 us
    all_gather x1, blocking collectives, local(): lax.all_gather(control_modes, ('slab', 'ctrl'), axis=1, tiled=True)  41.9 us
    all_gather x1, blocking collectives, local(): lax.all_gather(control_points, ('slab', 'ctrl'), axis=1, tiled=True)  40.5 us
    psum x1, blocking collectives, local(): total_loads = lax.psum(local_loads, ('slab', 'ctrl'))  36.9 us
    another operation x2, loops' own time, kernel_sum(): return lax.fori_loop(0, longest, accumulate, start)  15.9 us
    gather x20, local copies, waits for them, and re-layouts, accumulate(): centers = jnp.take(center_tiles, picked, axis=1)  12.2 us
    gather x20, local copies, waits for them, and re-layouts, accumulate(): coeffs = jnp.take(coeff_tiles, picked, axis=1)  12.2 us
    ppermute x4, starting transfers between devices, from_behind(): return lax.ppermute(value, axis, pairs)  7.12 us
  transfers between devices with their start and end apart: 6, of which 3 were waited for; matrix products, arithmetic and copies ran while one was open for 12% of the time, Pallas kernels for 0%

commit v1 on v0

v1 whole, which is shorter than its diff:
```python
import functools
import jax
import jax.numpy as jnp
from jax import lax
from jax.experimental import pallas as pl
from jax.experimental.pallas import tpu as pltpu
from jax.sharding import PartitionSpec as P

TILE = 128
TIME_STEP = 0.5
RADIUS = 4.0
GRAVITY = (0.0, 0.0, -0.5, 0.0, 0.0, 0.0)
ROWS = 24
FEATS = 32
UNROLL = 4
TINY = 1e-30
F32 = jnp.float32
BF16 = jnp.bfloat16


def vmem():
    return pl.BlockSpec(memory_space=pltpu.VMEM)


def smem():
    return pl.BlockSpec(memory_space=pltpu.SMEM)


def swapped(value, slab_bit, ctrl_bit):
    slabs, ctrls = lax.axis_size("slab"), lax.axis_size("ctrl")
    pairs = [
        (s * ctrls + c, (s ^ slab_bit) * ctrls + (c ^ ctrl_bit))
        for s in range(slabs)
        for c in range(ctrls)
    ]
    return lax.ppermute(value, ("slab", "ctrl"), pairs)


def shifted_back(value, axis):
    return lax.ppermute(value, axis, [(i, i - 1) for i in range(1, lax.axis_size(axis))])


def load_rows(pressure, area, center):
    pushed = pressure * area

    def turned(value, by):
        return jnp.concatenate([value[by:3], value[0:by]], axis=0)

    moment = turned(center, 1) * turned(pushed, 2) - turned(center, 2) * turned(pushed, 1)
    sums = [jnp.sum(pushed, axis=1, keepdims=True), jnp.sum(moment, axis=1, keepdims=True)]
    lane = lax.broadcasted_iota(jnp.int32, (1, 128), 1)
    row = jnp.zeros((1, 128), F32)
    for k in range(6):
        row = jnp.where(lane == k, sums[k // 3][k % 3 : k % 3 + 1, :], row)
    return row


def pack_kernel(pressure, area, center, points, modes, out):
    row = load_rows(pressure[...], area[...], center[...])
    for t in range(out.shape[0] // ROWS):
        span = slice(t * TILE, (t + 1) * TILE)
        base = t * ROWS
        for c in range(3):
            out[base + 8 * c : base + 8 * c + 1, :] = points[c : c + 1, span]
            for k in range(6):
                at = base + 8 * c + 1 + k
                out[at : at + 1, :] = modes[3 * k + c : 3 * k + c + 1, span]
            at = base + 8 * c + 7
            out[at : at + 1, :] = row if (t == 0 and c == 0) else jnp.zeros((1, 128), F32)


def loads_kernel(pressure, area, center, out):
    out[...] = load_rows(pressure[...], area[...], center[...])


def list_kernel(lines, slots, dummy, codes, counts, items, total):
    lead = 2 * UNROLL
    for e in range(lead):
        items[e] = dummy

    def one(line, at):
        for e in range(slots):
            items[at + e] = codes[line * slots + e]
        return at + counts[line]

    end = lax.fori_loop(0, lines, one, jnp.int32(lead))
    for e in range(4 * UNROLL):
        items[end + e] = dummy
    total[0] = end - lead


def split3(value):
    first = value.astype(BF16).astype(F32)
    rest = value - first
    second = rest.astype(BF16).astype(F32)
    return first, second, rest - second


def shift_kernel(
    own, lent, bits, items, total, table, points, extra, motion, inverse, gravity,
    out_own, out_extra, out_state, out_row, out_plane,
    tile_raw, line_raw, coef_raw, tile_feat, line_feat, coefs, acc, *stages,
):
    squares, phis = stages[:UNROLL], stages[UNROLL:]
    tiles = table.shape[0] // ROWS
    lines = own + lent

    loads = jnp.sum(table[pl.ds(7, tiles, stride=ROWS), :], axis=0, keepdims=True)
    acceleration = inverse[...] * loads + gravity[...]
    out_state[...] = motion[...] + TIME_STEP * acceleration
    step = TIME_STEP * motion[...] + 0.5 * TIME_STEP * TIME_STEP * acceleration

    one = jnp.ones((tiles, 128), F32)
    zero = jnp.zeros((tiles, 128), F32)
    norm = zero
    for c in range(3):
        place = table[pl.ds(8 * c, tiles, stride=ROWS), :] * (1.0 / RADIUS)
        norm = norm + place * place
        b1, b2, b3 = split3(-2.0 * place)
        for f, value in enumerate((b1, b1, b2, b2, b1, b3, b2, b3)):
            tile_raw[pl.ds(8 * c + f, tiles, stride=FEATS), :] = value
        coef = zero
        for k in range(6):
            coef = coef + step[:, k : k + 1] * table[pl.ds(8 * c + 1 + k, tiles, stride=ROWS), :]
        for f, value in enumerate(split3(4.0 * coef)):
            coef_raw[pl.ds(3 * f + c, tiles, stride=16), :] = value
    for f in range(9, 16):
        coef_raw[pl.ds(f, tiles, stride=16), :] = zero
    for f, value in enumerate(split3(norm) + (one, one, one, zero, zero)):
        tile_raw[pl.ds(24 + f, tiles, stride=FEATS), :] = value

    packed = coef_raw[...].astype(BF16)
    coefs[:, 0:128] = packed
    coefs[:, 128:256] = packed

    def turn(t, carry):
        block = tile_raw[pl.ds(pl.multiple_of(t * FEATS, FEATS), FEATS), :]
        tile_feat[pl.ds(pl.multiple_of(t * TILE, TILE), TILE), :] = block.T.astype(BF16)
        return carry

    lax.fori_loop(0, tiles, turn, 0, unroll=4)

    def features(ref, count, first):
        norm = jnp.zeros((count, 128), F32)
        for c in range(3):
            place = ref[c * count : (c + 1) * count, :] * (1.0 / RADIUS)
            norm = norm + place * place
            a1, a2, a3 = split3(place)
            for f, value in enumerate((a1, a2, a1, a2, a3, a1, a3, a2)):
                line_raw[pl.ds(first * FEATS + 8 * c + f, count, stride=FEATS), :] = value
        one = jnp.ones((count, 128), F32)
        zero = jnp.zeros((count, 128), F32)
        for f, value in enumerate((one, one, one) + split3(norm) + (zero, zero)):
            line_raw[pl.ds(first * FEATS + 24 + f, count, stride=FEATS), :] = value

    features(points, own, 0)
    if lent:
        features(extra, lent, own)
    line_raw[lines * FEATS :, :] = jnp.zeros((FEATS, 128), F32)
    line_feat[...] = line_raw[...].astype(BF16)
    acc[...] = jnp.zeros(acc.shape, F32)

    mask = (1 << bits) - 1

    def body(j, carry):
        base = j * UNROLL
        for u in range(UNROLL):
            code = items[base + u]
            line, tile = lax.shift_right_logical(code, bits), code & mask
            got = jnp.dot(
                coefs[pl.ds(pl.multiple_of(tile * 16, 16), 16), :],
                phis[u][...],
                preferred_element_type=F32,
            )
            at = pl.ds(pl.multiple_of(line * 16, 16), 16)
            acc[at, :] = acc[at, :] + got
        for u in range(UNROLL):
            square = jnp.maximum(squares[u][...], TINY)
            near = jnp.maximum(1.0 - square * lax.rsqrt(square), 0.0)
            fourth = near * near
            fourth = fourth * fourth
            phi = fourth * (1.25 - near)
            high = phi.astype(BF16)
            phis[u][0:128, :] = high
            phis[u][128:256, :] = (phi - high.astype(F32)).astype(BF16)
        for u in range(UNROLL):
            code = items[base + 2 * UNROLL + u]
            line, tile = lax.shift_right_logical(code, bits), code & mask
            squares[u][...] = jnp.dot(
                tile_feat[pl.ds(pl.multiple_of(tile * TILE, TILE), TILE), :],
                line_feat[pl.ds(pl.multiple_of(line * FEATS, FEATS), FEATS), :],
                preferred_element_type=F32,
            )
        return carry

    groups = lax.div(total[0] + (UNROLL - 1), jnp.int32(UNROLL))
    lax.fori_loop(0, groups + 2, body, 0)

    rows = out_row.shape[1] // 3
    wide = out_plane.shape[1] // 3
    for c in range(3):
        def sums(first, count):
            value = acc[pl.ds(first * 16 + c, count, stride=16), :]
            for f in (1, 2):
                value = value + acc[pl.ds(first * 16 + 3 * f + c, count, stride=16), :]
            return value

        value = sums(0, own)
        out_own[c * own : (c + 1) * own, :] = value
        if lent:
            out_extra[c * lent : (c + 1) * lent, :] = sums(own, lent)
        out_plane[0, c * wide : (c + 1) * wide, :] = points[c * own : c * own + wide, :]
        out_plane[1, c * wide : (c + 1) * wide, :] = (
            points[c * own : c * own + wide, :] + value[0:wide, :]
        )
        old_row = points[pl.ds(c * own, rows, stride=wide), :]
        out_row[0, c * rows : (c + 1) * rows, :] = old_row
        out_row[1, c * rows : (c + 1) * rows, :] = (
            old_row + out_own[pl.ds(c * own, rows, stride=wide), :]
        )


def volume_kernel(
    keep, has_lent, points, shift, back, row_halo, plane_halo,
    out_shift, out_volume, out_change,
):
    planes, rows, depth = points.shape[1:]
    slab, ctrl = lax.axis_index("slab"), lax.axis_index("ctrl")
    slabs, ctrls = lax.axis_size("slab"), lax.axis_size("ctrl")
    row_id = lax.broadcasted_iota(jnp.int32, (rows, depth), 0)
    lane = lax.broadcasted_iota(jnp.int32, (rows, depth), 1)
    inside = (lane < depth - 1) & (row_id + ctrl * rows < ctrls * rows - 1)
    if has_lent:
        from_helper = (row_id >= 1) & is_heavy(slab, slabs)
    last_row = row_id == rows - 1

    def next_row(value, edge):
        return jnp.where(last_row, edge, pltpu.roll(value, rows - 1, 0))

    def next_depth(value):
        return pltpu.roll(value, depth - 1, 1)

    def level(x):
        found = []
        for field in range(2):
            parts = []
            for c in range(3):
                if x == planes:
                    here = plane_halo[field, c, 0:rows, :]
                    edge = plane_halo[field, c, rows : rows + 1, :]
                else:
                    here = points[c, x]
                    if field == 1:
                        moved = shift[c, x]
                        if has_lent and x >= keep:
                            moved = jnp.where(from_helper, back[c, x - keep], moved)
                        out_shift[c, x] = moved
                        here = here + moved
                    edge = row_halo[field, c, x : x + 1, :]
                there = next_row(here, edge)
                parts.append((here + there, there - here))
            found.append(parts)
        return found

    before = level(0)
    for x in range(planes):
        after = level(x + 1)
        volumes = []
        for field in range(2):
            edges = []
            for c in range(3):
                both0, step0 = before[field][c]
                both1, step1 = after[field][c]
                along, across, total = both1 - both0, step0 + step1, both0 + both1
                edges.append(
                    (
                        0.25 * (along + next_depth(along)),
                        0.25 * (across + next_depth(across)),
                        0.25 * (next_depth(total) - total),
                    )
                )
            ex, ey, ez = zip(*edges)
            volumes.append(
                ex[0] * (ey[1] * ez[2] - ey[2] * ez[1])
                + ex[1] * (ey[2] * ez[0] - ey[0] * ez[2])
                + ex[2] * (ey[0] * ez[1] - ey[1] * ez[0])
            )
        live = inside & (slab * planes + x < slabs * planes - 1)
        out_volume[x] = jnp.where(live, volumes[1], 0.0)
        out_change[x] = jnp.where(live, volumes[1] - volumes[0], 0.0)
        before = after


def is_heavy(slab, slabs):
    return (8 * slab >= 3 * slabs) & (8 * slab < 5 * slabs)


def local(
    face_pressure,
    face_area,
    face_center,
    motion,
    inverse_mass,
    control_points,
    control_modes,
    node_points,
    tile_list,
    tile_count,
):
    slabs, ctrls = lax.axis_size("slab"), lax.axis_size("ctrl")
    slab, ctrl = lax.axis_index("slab"), lax.axis_index("ctrl")
    _, planes, rows, depth = node_points.shape
    slots = tile_list.shape[2]
    own = planes * rows
    columns = control_points.shape[1]
    tiles = columns * slabs * ctrls // TILE
    bits = max(1, (tiles - 1).bit_length())
    pressure = face_pressure.reshape(1, -1)

    lend = slabs % 8 == 0 and slabs & (slabs - 1) == 0 and planes % 2 == 0
    unit = slabs // 8
    keep = planes // 2
    lent = (planes - keep) * rows if lend else 0
    heavy = [s for s in range(slabs) if is_heavy(s, slabs)]

    if lend:
        listed = jnp.concatenate(
            [tile_list[keep:], tile_count[keep:, :, None]], axis=2
        ).astype(F32)
        listed = jnp.pad(listed, ((0, 0), (0, 0), (0, TILE - slots - 1)))
        sent = jnp.concatenate(
            [node_points[:, keep:].reshape(-1, depth), listed.reshape(-1, TILE)], axis=0
        )

    direct = columns % TILE == 0 and slabs & (slabs - 1) == 0 and ctrls & (ctrls - 1) == 0
    own_tiles = columns // TILE
    device = slab * ctrls + ctrl
    got = None
    if direct:
        table = pl.pallas_call(
            pack_kernel,
            out_shape=jax.ShapeDtypeStruct((own_tiles * ROWS, TILE), F32),
            in_specs=[vmem()] * 5,
            out_specs=vmem(),
        )(pressure, face_area, face_center, control_points, control_modes)
        place = jnp.zeros(tile_list.shape, jnp.int32)
        bit = slabs // 2
        order = []
        while bit:
            order.append((bit, 0))
            bit //= 2
        bit = ctrls // 2
        while bit:
            order.append((0, bit))
            bit //= 2
        for slab_bit, ctrl_bit in order:
            size = table.shape[0]
            if lend and slab_bit == unit:
                reply = swapped(jnp.concatenate([table, sent], axis=0), slab_bit, ctrl_bit)
                got = reply[size:]
                reply = reply[:size]
            else:
                reply = swapped(table, slab_bit, ctrl_bit)
            table = jnp.concatenate([table, reply], axis=0)

        def placed(number):
            apart = (number // own_tiles) ^ device
            at = jnp.zeros(number.shape, jnp.int32)
            for turn, (slab_bit, ctrl_bit) in enumerate(order):
                flag = slab_bit * ctrls + ctrl_bit
                at = at + jnp.where((apart & flag) != 0, 1 << turn, 0)
            return at * own_tiles + number % own_tiles
    else:
        loads = pl.pallas_call(
            loads_kernel,
            out_shape=jax.ShapeDtypeStruct((1, TILE), F32),
            in_specs=[vmem()] * 3,
            out_specs=vmem(),
        )(pressure, face_area, face_center)
        loads = lax.psum(loads, ("slab", "ctrl"))
        whole = jnp.concatenate([control_points, control_modes], axis=0)
        whole = lax.all_gather(whole, ("slab", "ctrl"), axis=1, tiled=True)
        whole = whole.reshape(7, 3, tiles, TILE).transpose(2, 1, 0, 3)
        spare = jnp.zeros((tiles, 3, 1, TILE), F32).at[0, 0, 0, :].set(loads[0])
        table = jnp.concatenate([whole, spare], axis=2).reshape(tiles * ROWS, TILE)

        def placed(number):
            return number

    if lend and got is None:
        got = swapped(sent, unit, 0)

    numbers = tile_list.reshape(own, slots)
    counts = tile_count
    extra = None
    if lend:
        mine_heavy = is_heavy(slab, slabs)
        helper = is_heavy(slab ^ unit, slabs) & jnp.logical_not(mine_heavy)
        plane_id = lax.broadcasted_iota(jnp.int32, (planes, rows), 0)
        row_id = lax.broadcasted_iota(jnp.int32, (planes, rows), 1)
        counts = jnp.where(mine_heavy & (plane_id >= keep) & (row_id >= 1), 0, counts)
        extra = got[: 3 * lent]
        listed = got[3 * lent :, : slots + 1].astype(jnp.int32)
        numbers = jnp.concatenate([numbers, listed[:, :slots]], axis=0)
        lent_row = lax.broadcasted_iota(jnp.int32, (planes - keep, rows), 1).reshape(-1)
        lent_counts = jnp.where(helper & (lent_row >= 1), listed[:, slots], 0)
        counts = jnp.concatenate([counts.reshape(-1), lent_counts])
    else:
        counts = counts.reshape(-1)
    lines = own + lent
    codes = (jnp.arange(lines, dtype=jnp.int32)[:, None] << bits) + placed(numbers)
    length = lines * slots + 6 * UNROLL + slots
    items, total = pl.pallas_call(
        functools.partial(list_kernel, lines, slots, lines << bits),
        out_shape=(
            jax.ShapeDtypeStruct((length,), jnp.int32),
            jax.ShapeDtypeStruct((1,), jnp.int32),
        ),
        in_specs=[smem()] * 2,
        out_specs=(smem(), smem()),
        cost_estimate=pl.CostEstimate(flops=0, bytes_accessed=4_000_000, transcendentals=0),
    )(codes.reshape(-1), counts)

    def wide(value):
        return jnp.pad(value, (0, TILE - value.shape[0])).reshape(1, TILE)

    outs = pl.pallas_call(
        functools.partial(shift_kernel, own, lent, bits),
        out_shape=(
            jax.ShapeDtypeStruct((3 * own, depth), F32),
            jax.ShapeDtypeStruct((3 * max(lent, 8), depth), F32),
            jax.ShapeDtypeStruct((1, TILE), F32),
            jax.ShapeDtypeStruct((2, 3 * planes, depth), F32),
            jax.ShapeDtypeStruct((2, 3 * rows, depth), F32),
        ),
        in_specs=[smem()] * 2 + [vmem()] * 6,
        out_specs=(vmem(),) * 5,
        scratch_shapes=[
            pltpu.VMEM((tiles * FEATS, TILE), F32),
            pltpu.VMEM(((lines + 1) * FEATS, depth), F32),
            pltpu.VMEM((tiles * 16, TILE), F32),
            pltpu.VMEM((tiles * TILE, FEATS), BF16),
            pltpu.VMEM(((lines + 1) * FEATS, depth), BF16),
            pltpu.VMEM((tiles * 16, 2 * TILE), BF16),
            pltpu.VMEM(((lines + 1) * 16, depth), F32),
        ]
        + [pltpu.VMEM((TILE, depth), F32)] * UNROLL
        + [pltpu.VMEM((2 * TILE, depth), BF16)] * UNROLL,
        compiler_params=pltpu.CompilerParams(vmem_limit_bytes=32 << 20),
    )(
        items, total, table, node_points.reshape(3 * own, depth),
        extra if lend else jnp.zeros((24, depth), F32),
        wide(motion), wide(inverse_mass), wide(jnp.array(GRAVITY, F32)),
    )
    shift, lent_shift, state, row_sent, plane_sent = outs

    if lend:
        back = lax.ppermute(lent_shift, "slab", [(h ^ unit, h) for h in heavy])
        back = back.reshape(3, planes - keep, rows, depth)
    else:
        back = jnp.zeros((3, 1, rows, depth), F32)
    row_halo = shifted_back(row_sent, "ctrl").reshape(2, 3, planes, depth)
    plane_sent = plane_sent.reshape(2, 3, rows, depth)
    plane_halo = shifted_back(
        jnp.concatenate([plane_sent, row_halo[:, :, :1]], axis=2), "slab"
    )
    node_shift, volume, change = pl.pallas_call(
        functools.partial(volume_kernel, keep, lend),
        out_shape=(
            jax.ShapeDtypeStruct(node_points.shape, F32),
            jax.ShapeDtypeStruct(node_points.shape[1:], F32),
            jax.ShapeDtypeStruct(node_points.shape[1:], F32),
        ),
        in_specs=[vmem()] * 5,
        out_specs=(vmem(),) * 3,
    )(node_points, shift.reshape(3, planes, rows, depth), back, row_halo, plane_halo)
    return node_shift, volume, change, state[0, : motion.shape[0]]


def solution(mesh):
    placed = (
        P(("slab", "ctrl")),
        P(None, ("slab", "ctrl")),
        P(None, ("slab", "ctrl")),
        P(),
        P(),
        P(None, ("slab", "ctrl")),
        P(None, ("slab", "ctrl")),
        P(None, "slab", "ctrl", None),
        P("slab", "ctrl", None),
        P("slab", "ctrl"),
    )
    return jax.shard_map(
        local,
        mesh=mesh,
        in_specs=placed,
        out_specs=(
            P(None, "slab", "ctrl", None),
            P("slab", "ctrl", None),
            P("slab", "ctrl", None),
            P(),
        ),
        check_vma=False,
    )
```

time: 304 us -> 84.4 us (0.28)
  the two profiles are of different devices: /device:TPU:0 before, /device:TPU:19 now
where the time goes in v1:
time: 84.4 us; the launch traced here: 83.8 us
  Pallas kernels  46.4 us (55%)
  waiting for transfers between devices  14.7 us (17%)
  starting transfers between devices  13.6 us (16%)
  local copies, waits for them, and re-layouts  6.93 us (8%)
  other arithmetic  1.42 us (2%)
    pallas_call x1, Pallas kernels, local(): pl.pallas_call(functools.partial(shift_kernel, own, lent, bits), out_shap...  39.3 us
    ppermute x5, waiting for transfers between devices, swapped(): return lax.ppermute(value, ('slab', 'ctrl'), pairs)  9.46 us
    ppermute x5, starting transfers between devices, swapped(): return lax.ppermute(value, ('slab', 'ctrl'), pairs)  8.51 us
    ppermute x2, waiting for transfers between devices, shifted_back(): lax.ppermute(value, axis, [(i, i - 1) for i in range(1, lax.axis_size(axi...  5.2 us
    unnamed x29, local copies, waits for them, and re-layouts  4.16 us
    ppermute x2, starting transfers between devices, shifted_back(): lax.ppermute(value, axis, [(i, i - 1) for i in range(1, lax.axis_size(axi...  3.82 us
    pallas_call x1, Pallas kernels, local(): pl.pallas_call(functools.partial(list_kernel, lines, slots, lines << bits...  3.58 us
    pallas_call x1, Pallas kernels, local(): pl.pallas_call(functools.partial(volume_kernel, keep, lend), out_shape=(j...  1.82 us
  transfers between devices with their start and end apart: 8, of which 6 were waited for; matrix products, arithmetic and copies ran while one was open for 4% of the time, Pallas kernels for 4%

profile of v1, /device:TPU:19, one launch (start us, length us, event | category | flops | bytes accessed | tf_op | source)
XLA Modules:
  0.0 83.8 jit_solution(7659548179706154757)
XLA Ops:
  0.6 1.7 %shard_map.138 = f32[48,128]{1,0:T(8,128)} custom-call(f32[1,4096]{1,0:T(1,128)} %bitcast.28, f32[3,4096]{1,0:T(4,128)} %area.1, f32[3,4096]{1,0:T(4,128)} %center.1, f32[3,256]{1,0:T(4,128)} %points.2, f32[18,256]{1,0:T(8,128)} %modes.1), custom_call_target="tpu_custom_call" | custom-call | tf_op jit(solution)/shard_map/pallas_call | solution.py:340
  2.3 0.0 copy-start.9
  2.3 0.1 collective-permute-start
  2.4 0.8 constant_dynamic-update-slice_fusion.9
  3.2 0.0 copy-done.9
  3.2 0.1 copy.25
  3.3 0.0 slice-start.1
  3.3 0.7 slice-done.1
  4.0 0.1 add_convert_fusion
  4.1 0.1 and_select_fusion
  4.1 0.0 copy-start.4
  4.1 2.0 %collective-permute-done = f32[48,128]{1,0:T(8,128)S(1)} collective-permute-done((f32[48,128]{1,0:T(8,128)}, f32[48,128]{1,0:T(8,128)S(1)}, u32[]{:S(2)}, u32[]{:S(2)}) %collective-permute-start) | collective-permute-done | bytes 24608 | tf_op jit(solution)/shard_map/ppermute | solution.py:36
  6.1 0.0 copy-done.4
  6.1 1.5 %collective-permute-start.1 = (f32[96,128]{1,0:T(8,128)S(1)}, f32[96,128]{1,0:T(8,128)S(1)}, u32[]{:S(2)}, u32[]{:S(2)}) collective-permute-start(f32[96,128]{1,0:T(8,128)S(1)} %pad_maximum_fusion.1), channel_id=1, source_target_pairs={{0,8},{1,9},{2,10},{3,11},{4,12},{5,13},{6,14},{7,15},{8,0},{9,1},... | collective-permute-start | bytes 147464 | tf_op jit(solution)/shard_map/ppermute | solution.py:36
  7.6 1.5 %collective-permute-done.1 = f32[96,128]{1,0:T(8,128)S(1)} collective-permute-done((f32[96,128]{1,0:T(8,128)S(1)}, f32[96,128]{1,0:T(8,128)S(1)}, u32[]{:S(2)}, u32[]{:S(2)}) %collective-permute-start.1) | collective-permute-done | bytes 49184 | tf_op jit(solution)/shard_map/ppermute | solution.py:36
  9.1 0.0 slice-start
  9.2 0.8 slice-done
  10.0 0.3 collective-permute-start.2
  10.3 0.1 and.91
  10.4 0.1 reshape.64
  10.4 0.1 add.51
  10.5 0.1 add.52
  10.6 0.0 copy-start.10
  10.6 0.0 copy-start.11
  10.6 0.6 copy-done.10
  11.3 0.0 copy-done.11
  11.3 2.9 %collective-permute-done.2 = f32[320,128]{1,0:T(8,128)S(1)} collective-permute-done((f32[320,128]{1,0:T(8,128)S(1)}, f32[320,128]{1,0:T(8,128)S(1)}, u32[]{:S(2)}, u32[]{:S(2)}) %collective-permute-start.2) | collective-permute-done | bytes 163872 | tf_op jit(solution)/shard_map/ppermute | solution.py:36
  14.2 1.3 %collective-permute-start.3 = (f32[384,128]{1,0:T(8,128)S(1)}, f32[384,128]{1,0:T(8,128)S(1)}, u32[]{:S(2)}, u32[]{:S(2)}) collective-permute-start(f32[384,128]{1,0:T(8,128)S(1)} %pad_maximum_fusion), channel_id=1, source_target_pairs={{0,2},{1,3},{2,0},{3,1},{4,6},{5,7},{6,4},{7,5},{8,10},{9,11},{10,... | collective-permute-start | bytes 589832 | tf_op jit(solution)/shard_map/ppermute | solution.py:36
  15.5 0.2 slice_reduce_fusion
  15.7 3.1 %collective-permute-done.3 = f32[384,128]{1,0:T(8,128)S(1)} collective-permute-done((f32[384,128]{1,0:T(8,128)S(1)}, f32[384,128]{1,0:T(8,128)S(1)}, u32[]{:S(2)}, u32[]{:S(2)}) %collective-permute-start.3) | collective-permute-done | bytes 196640 | tf_op jit(solution)/shard_map/ppermute | solution.py:36
  18.8 0.0 copy-start.5
  18.9 5.3 %collective-permute-start.4 = (f32[768,128]{1,0:T(8,128)S(1)}, f32[768,128]{1,0:T(8,128)S(1)}, u32[]{:S(2)}, u32[]{:S(2)}) collective-permute-start(f32[768,128]{1,0:T(8,128)S(1)} %get-tuple-element.24), channel_id=1, source_target_pairs={{0,1},{1,0},{2,3},{3,2},{4,5},{5,4},{6,7},{7,6},{8,9},{9,8},{10,11... | collective-permute-start | bytes 1179656 | tf_op jit(solution)/shard_map/ppermute | solution.py:36
  24.2 0.0 copy-done.5
  24.2 0.1 concatenate.39
  24.3 0.6 pad_add_fusion.1.counts
  24.9 0.6 fusion.2.codes
  25.5 3.6 %shard_map.139 = (s32[1576]{0:T(1024)}, s32[1]{0:T(128)}) custom-call(s32[1536]{0:T(1024)} %fusion.2.codes, s32[96]{0:T(128)} %pad_add_fusion.1.counts), custom_call_target="tpu_custom_call" | custom-call | bytes 4000000 | tf_op jit(solution)/shard_map/pallas_call | solution.py:413
  29.1 0.0 collective-permute-done.4
  29.1 0.0 copy-start
  29.1 0.0 copy-start.2
  29.2 0.0 copy-start.3
  29.2 0.8 copy-done
  30.0 0.0 copy-done.2
  30.0 0.0 copy-done.3
  30.0 39.3 %shard_map.140 = (f32[192,128]{1,0:T(8,128)S(1)}, f32[96,128]{1,0:T(8,128)S(1)}, f32[1,128]{1,0:T(1,128)S(1)}, f32[2,24,128]{2,1,0:T(8,128)S(1)}, f32[2,24,128]{2,1,0:T(8,128)S(1)}) custom-call(s32[1576]{0:T(1024)S(1)} %copy-done.2, s32[1]{0:T(128)} %get-tuple-element.15.total, f32[1536,128]{1,0:T(8,128)S(1)} %constant_dynamic-update-slice_fusion.10.table, ...), custom_call_target="tpu_custom_call" | custom-call | tf_op jit(solution)/shard_map/pallas_call | solution.py:427
  69.3 0.0 copy-start.1
  69.3 0.6 copy-done.1
  70.0 1.9 %collective-permute-start.6 = (f32[2,24,128]{2,1,0:T(8,128)S(1)}, f32[2,24,128]{2,1,0:T(8,128)S(1)}, u32[]{:S(2)}, u32[]{:S(2)}) collective-permute-start(f32[2,24,128]{2,1,0:T(8,128)S(1)} %get-tuple-element.18), channel_id=1, source_target_pairs={{1,0},{2,1},{3,2},{5,4},{6,5},{7,6},{9,8},{10,9},{11,10},{13,12},{... | collective-permute-start | bytes 73736 | tf_op jit(solution)/shard_map/ppermute | solution.py:40
  71.9 1.3 %collective-permute-start.5 = (f32[96,128]{1,0:T(8,128)S(1)}, f32[96,128]{1,0:T(8,128)S(1)}, u32[]{:S(2)}, u32[]{:S(2)}) collective-permute-start(f32[96,128]{1,0:T(8,128)S(1)} %get-tuple-element.17), channel_id=1, source_target_pairs={{8,12},{20,16},{9,13},{21,17},{10,14},{22,18},{11,15},{23,19}} | collective-permute-start | bytes 147464 | tf_op jit(solution)/shard_map/ppermute | solution.py:458
  73.2 1.9 %collective-permute-done.6 = f32[2,24,128]{2,1,0:T(8,128)S(1)} collective-permute-done((f32[2,24,128]{2,1,0:T(8,128)S(1)}, f32[2,24,128]{2,1,0:T(8,128)S(1)}, u32[]{:S(2)}, u32[]{:S(2)}) %collective-permute-start.6) | collective-permute-done | bytes 24608 | tf_op jit(solution)/shard_map/ppermute | solution.py:40
  75.1 0.0 copy-start.8
  75.1 0.6 copy-done.8
  75.7 1.9 %collective-permute-start.7 = (f32[2,3,9,128]{3,2,1,0:T(8,128)S(1)}, f32[2,3,9,128]{3,2,1,0:T(8,128)S(1)}, u32[]{:S(2)}, u32[]{:S(2)}) collective-permute-start(f32[2,3,9,128]{3,2,1,0:T(8,128)S(1)} %pad_maximum_fusion.2), channel_id=1, source_target_pairs={{4,0},{8,4},{12,8},{16,12},{20,16},{24,20},{28,24},{5,1},{9,5},{13... | collective-permute-start | bytes 82952 | tf_op jit(solution)/shard_map/ppermute | solution.py:40
  77.6 0.5 slice_bitcast_fusion.1
  78.1 0.0 collective-permute-done.5
  78.1 0.0 copy-start.6
  78.1 3.3 %collective-permute-done.7.plane_halo = f32[2,3,9,128]{3,2,1,0:T(8,128)S(1)} collective-permute-done((f32[2,3,9,128]{3,2,1,0:T(8,128)S(1)}, f32[2,3,9,128]{3,2,1,0:T(8,128)S(1)}, u32[]{:S(2)}, u32[]{:S(2)}) %collective-permute-start.7) | collective-permute-done | bytes 27680 | tf_op jit(solution)/shard_map/ppermute | solution.py:40
  81.4 0.0 copy-start.7
  81.4 0.0 copy-done.6
  81.4 0.6 copy-done.7
  82.0 1.8 %shard_map.141 = (f32[3,8,8,128]{3,2,1,0:T(8,128)}, f32[8,8,128]{2,1,0:T(8,128)}, f32[8,8,128]{2,1,0:T(8,128)}) custom-call(f32[3,8,8,128]{3,2,1,0:T(8,128)} %points.3, f32[3,8,8,128]{3,2,1,0:T(8,128)} %bitcast.21, f32[3,4,8,128]{3,2,1,0:T(8,128)} %bitcast.25, f32[2,3,8,128]{3,2,1,0:T(8,128)} %bitcast.27, f32[2,3,9,128]{3,2,1,0:T(8,128)} %copy-done.7), custom_call_target="tpu_custom_call" | custom-call | tf_op jit(solution)/shard_map/pallas_call | solution.py:467
  (20 shorter events, 0.2 us)
Async XLA Ops:
  2.3 0.8 copy-start.9
  2.3 3.8 %collective-permute-start = (f32[48,128]{1,0:T(8,128)}, f32[48,128]{1,0:T(8,128)S(1)}, u32[]{:S(2)}, u32[]{:S(2)}) collective-permute-start(f32[48,128]{1,0:T(8,128)} %shard_map.138), channel_id=1, source_target_pairs={{0,16},{1,17},{2,18},{3,19},{4,20},{5,21},{6,22},{7,23},{8,24},{9,... | collective-permute-start | bytes 73736 | tf_op jit(solution)/shard_map/ppermute | solution.py:36
  3.3 0.7 slice-start.1
  4.1 2.0 %copy-start.4 = (f32[48,128]{1,0:T(8,128)S(1)}, f32[48,128]{1,0:T(8,128)}, u32[]{:S(2)}) copy-start(f32[48,128]{1,0:T(8,128)} %shard_map.138) | copy-start | bytes 73732
  6.1 3.0 %collective-permute-start.1 = (f32[96,128]{1,0:T(8,128)S(1)}, f32[96,128]{1,0:T(8,128)S(1)}, u32[]{:S(2)}, u32[]{:S(2)}) collective-permute-start(f32[96,128]{1,0:T(8,128)S(1)} %pad_maximum_fusion.1), channel_id=1, source_target_pairs={{0,8},{1,9},{2,10},{3,11},{4,12},{5,13},{6,14},{7,15},{8,0},{9,1},... | collective-permute-start | bytes 147464 | tf_op jit(solution)/shard_map/ppermute | solution.py:36
  9.1 0.8 slice-start
  10.0 4.2 %collective-permute-start.2 = (f32[320,128]{1,0:T(8,128)S(1)}, f32[320,128]{1,0:T(8,128)S(1)}, u32[]{:S(2)}, u32[]{:S(2)}) collective-permute-start(f32[320,128]{1,0:T(8,128)S(1)} %constant_dynamic-update-slice_fusion), channel_id=1, source_target_pairs={{0,4},{1,5},{2,6},{3,7},{4,0},{5,1},{6,2},{7,3},{8,12},{9,13},{10,... | collective-permute-start | bytes 491528 | tf_op jit(solution)/shard_map/ppermute | solution.py:36
  10.6 0.7 copy-start.10
  10.6 0.7 copy-start.11
  14.2 4.6 %collective-permute-start.3 = (f32[384,128]{1,0:T(8,128)S(1)}, f32[384,128]{1,0:T(8,128)S(1)}, u32[]{:S(2)}, u32[]{:S(2)}) collective-permute-start(f32[384,128]{1,0:T(8,128)S(1)} %pad_maximum_fusion), channel_id=1, source_target_pairs={{0,2},{1,3},{2,0},{3,1},{4,6},{5,7},{6,4},{7,5},{8,10},{9,11},{10,... | collective-permute-start | bytes 589832 | tf_op jit(solution)/shard_map/ppermute | solution.py:36
  18.8 5.4 %copy-start.5 = (s32[8,8,16]{2,1,0:T(8,128)S(1)}, s32[8,8,16]{2,1,0:T(8,128)}, u32[]{:S(2)}) copy-start(s32[8,8,16]{2,1,0:T(8,128)} %param.19) | copy-start | bytes 12292
  18.9 10.2 %collective-permute-start.4 = (f32[768,128]{1,0:T(8,128)S(1)}, f32[768,128]{1,0:T(8,128)S(1)}, u32[]{:S(2)}, u32[]{:S(2)}) collective-permute-start(f32[768,128]{1,0:T(8,128)S(1)} %get-tuple-element.24), channel_id=1, source_target_pairs={{0,1},{1,0},{2,3},{3,2},{4,5},{5,4},{6,7},{7,6},{8,9},{9,8},{10,11... | collective-permute-start | bytes 1179656 | tf_op jit(solution)/shard_map/ppermute | solution.py:36
  29.1 0.9 %copy-start = (f32[3,8,8,128]{3,2,1,0:T(8,128)S(1)}, f32[3,8,8,128]{3,2,1,0:T(8,128)}, u32[]{:S(2)}) copy-start(f32[3,8,8,128]{3,2,1,0:T(8,128)} %points.3) | copy-start | bytes 294916
  29.1 0.8 %copy-start.2 = (s32[1576]{0:T(1024)S(1)}, s32[1576]{0:T(1024)}, u32[]{:S(2)}) copy-start(s32[1576]{0:T(1024)} %get-tuple-element.14.items) | copy-start | bytes 18916
  29.2 0.8 %copy-start.3 = (f32[1,128]{1,0:T(1,128)S(1)}, f32[1,128]{1,0:T(1,128)}, u32[]{:S(2)}) copy-start(f32[1,128]{1,0:T(1,128)} %constant.72.gravity) | copy-start | bytes 1540
  69.3 0.6 copy-start.1
  70.0 5.1 %collective-permute-start.6 = (f32[2,24,128]{2,1,0:T(8,128)S(1)}, f32[2,24,128]{2,1,0:T(8,128)S(1)}, u32[]{:S(2)}, u32[]{:S(2)}) collective-permute-start(f32[2,24,128]{2,1,0:T(8,128)S(1)} %get-tuple-element.18), channel_id=1, source_target_pairs={{1,0},{2,1},{3,2},{5,4},{6,5},{7,6},{9,8},{10,9},{11,10},{13,12},{... | collective-permute-start | bytes 73736 | tf_op jit(solution)/shard_map/ppermute | solution.py:40
  71.9 6.2 %collective-permute-start.5 = (f32[96,128]{1,0:T(8,128)S(1)}, f32[96,128]{1,0:T(8,128)S(1)}, u32[]{:S(2)}, u32[]{:S(2)}) collective-permute-start(f32[96,128]{1,0:T(8,128)S(1)} %get-tuple-element.17), channel_id=1, source_target_pairs={{8,12},{20,16},{9,13},{21,17},{10,14},{22,18},{11,15},{23,19}} | collective-permute-start | bytes 147464 | tf_op jit(solution)/shard_map/ppermute | solution.py:458
  75.1 0.6 copy-start.8
  75.7 5.7 %collective-permute-start.7 = (f32[2,3,9,128]{3,2,1,0:T(8,128)S(1)}, f32[2,3,9,128]{3,2,1,0:T(8,128)S(1)}, u32[]{:S(2)}, u32[]{:S(2)}) collective-permute-start(f32[2,3,9,128]{3,2,1,0:T(8,128)S(1)} %pad_maximum_fusion.2), channel_id=1, source_target_pairs={{4,0},{8,4},{12,8},{16,12},{20,16},{24,20},{28,24},{5,1},{9,5},{13... | collective-permute-start | bytes 82952 | tf_op jit(solution)/shard_map/ppermute | solution.py:40
  78.1 3.3 %copy-start.6 = (f32[96,128]{1,0:T(8,128)}, f32[96,128]{1,0:T(8,128)S(1)}, u32[]{:S(2)}) copy-start(f32[96,128]{1,0:T(8,128)S(1)} %collective-permute-done.5) | copy-start | bytes 147460
  81.4 0.6 copy-start.7

commit v2 on v1

v2 whole, which is shorter than its diff:
```python
import functools
import jax
import jax.numpy as jnp
from jax import lax
from jax.experimental import pallas as pl
from jax.experimental.pallas import tpu as pltpu
from jax.sharding import PartitionSpec as P

TILE = 128
TIME_STEP = 0.5
RADIUS = 4.0
GRAVITY = (0.0, 0.0, -0.5, 0.0, 0.0, 0.0)
ROWS = 24
FEATS = 32
UNROLL = 16
MIX = 48
TINY = 1e-30
F32 = jnp.float32
BF16 = jnp.bfloat16


def vmem():
    return pl.BlockSpec(memory_space=pltpu.VMEM)


def smem():
    return pl.BlockSpec(memory_space=pltpu.SMEM)


def swapped(value, slab_bit, ctrl_bit):
    slabs, ctrls = lax.axis_size("slab"), lax.axis_size("ctrl")
    pairs = [
        (s * ctrls + c, (s ^ slab_bit) * ctrls + (c ^ ctrl_bit))
        for s in range(slabs)
        for c in range(ctrls)
    ]
    return lax.ppermute(value, ("slab", "ctrl"), pairs)


def shifted_back(value, axis):
    return lax.ppermute(value, axis, [(i, i - 1) for i in range(1, lax.axis_size(axis))])


def load_rows(pressure, area, center):
    pushed = pressure * area

    def turned(value, by):
        return jnp.concatenate([value[by:3], value[0:by]], axis=0)

    moment = turned(center, 1) * turned(pushed, 2) - turned(center, 2) * turned(pushed, 1)
    sums = [jnp.sum(pushed, axis=1, keepdims=True), jnp.sum(moment, axis=1, keepdims=True)]
    lane = lax.broadcasted_iota(jnp.int32, (1, 128), 1)
    row = jnp.zeros((1, 128), F32)
    for k in range(6):
        row = jnp.where(lane == k, sums[k // 3][k % 3 : k % 3 + 1, :], row)
    return row


def pack_kernel(pressure, area, center, points, modes, out):
    row = load_rows(pressure[...], area[...], center[...])
    for t in range(out.shape[0] // ROWS):
        span = slice(t * TILE, (t + 1) * TILE)
        base = t * ROWS
        for c in range(3):
            out[base + 8 * c : base + 8 * c + 1, :] = points[c : c + 1, span]
            for k in range(6):
                at = base + 8 * c + 1 + k
                out[at : at + 1, :] = modes[3 * k + c : 3 * k + c + 1, span]
            at = base + 8 * c + 7
            out[at : at + 1, :] = row if (t == 0 and c == 0) else jnp.zeros((1, 128), F32)


def loads_kernel(pressure, area, center, out):
    out[...] = load_rows(pressure[...], area[...], center[...])


def split3(value):
    first = value.astype(BF16).astype(F32)
    rest = value - first
    second = rest.astype(BF16).astype(F32)
    return first, second, rest - second


def spread(ref, at):
    return jnp.broadcast_to(ref[pl.ds(at, 1), :], (8, ref.shape[1]))


def products(rows, scale, order, ends):
    row = lax.broadcasted_iota(jnp.int32, rows[0].shape, 0)
    norm = jnp.zeros(rows[0].shape, F32)
    blocks = []
    for value in rows:
        place = value * (1.0 / RADIUS)
        norm = norm + place * place
        first, second, third = split3(place * scale)
        low = jnp.where((row & 1) == 1, order[1](first, second, third, row), order[0](first, second, third, row))
        blocks.append(low)
    first, second, third = split3(norm)
    blocks.append(ends(first, second, third, row))
    return jnp.concatenate(blocks, axis=0)


def tile_block(rows):
    return products(
        rows,
        -2.0,
        (
            lambda a, b, c, row: jnp.where((row == 2) | (row == 6), b, a),
            lambda a, b, c, row: jnp.where(row == 1, a, jnp.where(row == 3, b, c)),
        ),
        lambda a, b, c, row: jnp.where(
            row == 0, a, jnp.where(row == 1, b, jnp.where(row == 2, c, jnp.where(row < 6, 1.0, 0.0)))
        ),
    )


def line_block(rows):
    return products(
        rows,
        1.0,
        (
            lambda a, b, c, row: jnp.where(row < 4, a, c),
            lambda a, b, c, row: jnp.where(row == 5, a, b),
        ),
        lambda a, b, c, row: jnp.where(
            row < 3, 1.0, jnp.where(row == 3, a, jnp.where(row == 4, b, jnp.where(row == 5, c, 0.0)))
        ),
    )


def lend_kernel(keep, points, numbers, counts, out):
    _, planes, rows, _ = points.shape
    slots = numbers.shape[2]
    lent = (planes - keep) * rows
    row = lax.broadcasted_iota(jnp.int32, (rows, rows), 0)
    lane = lax.broadcasted_iota(jnp.int32, (rows, rows), 1)
    wide = lax.broadcasted_iota(jnp.int32, (rows, out.shape[1]), 1)
    for x in range(keep, planes):
        at = (x - keep) * rows
        for c in range(3):
            out[c * lent + at : c * lent + at + rows, :] = points[c, x]
        many = jnp.broadcast_to(counts[x : x + 1, :].astype(F32), (rows, rows))
        column = jnp.sum(jnp.where(row == lane, many, 0.0), axis=1, keepdims=True)
        at = at + 3 * lent
        out[at : at + rows, :] = jnp.where(wide == slots, column, 0.0)
        out[at : at + rows, 0:slots] = numbers[x].astype(F32)


def prepare_kernel(
    first, slots, bits, placed, counted, numbers, counts, points,
    items_a, items_b, totals, line_feat, codes, listed, sem,
):
    lines = numbers.shape[0]
    number = numbers[:, 0:slots].astype(jnp.int32)
    count = counted(counts[...].astype(jnp.int32))
    row = lax.broadcasted_iota(jnp.int32, (lines, slots), 0)
    slot = lax.broadcasted_iota(jnp.int32, (lines, slots), 1)
    code = lax.shift_left(row + first, jnp.full_like(row, bits)) + placed(number)
    codes[:, 0:slots] = jnp.where(slot < count, code, -1)
    codes[:, slots : slots + 1] = count
    copy = pltpu.make_async_copy(codes, listed, sem)
    copy.start()

    def block(l, carry):
        rows = [spread(points, c * lines + l) for c in range(3)]
        at = pl.ds(pl.multiple_of(l * FEATS, FEATS), FEATS)
        line_feat[at, :] = line_block(rows).astype(BF16)
        return carry

    lax.fori_loop(0, lines, block, 0, unroll=4)
    copy.wait()
    step = 4

    def one(line, ends):
        def some(g, ends):
            end_a, end_b = ends
            for e in range(step):
                code = listed[line, g * step + e]
                live = 1 + lax.shift_right_arithmetic(code, 31)
                late = live & lax.shift_right_logical(code, bits - 1)
                items_a[end_a] = code
                items_b[end_b] = code
                end_a, end_b = end_a + (live - late), end_b + late
            return end_a, end_b

        groups = lax.shift_right_logical(listed[line, slots] + (step - 1), 2)
        return lax.fori_loop(0, groups, some, ends)

    end_a, end_b = lax.fori_loop(0, lines, one, (jnp.int32(0), jnp.int32(0)))
    dummy = (first + lines) << bits
    for e in range(2 * UNROLL):
        items_a[end_a + e] = dummy
        items_b[end_b + e] = dummy
    totals[0] = end_a
    totals[1] = end_b


def prepared(first, slots, bits, placed, counted, numbers, counts, points):
    lines, depth = numbers.shape[0], points.shape[1]
    length = lines * slots + 2 * UNROLL
    return pl.pallas_call(
        functools.partial(prepare_kernel, first, slots, bits, placed, counted),
        out_shape=(
            jax.ShapeDtypeStruct((length,), jnp.int32),
            jax.ShapeDtypeStruct((length,), jnp.int32),
            jax.ShapeDtypeStruct((2,), jnp.int32),
            jax.ShapeDtypeStruct((lines * FEATS, depth), BF16),
        ),
        in_specs=[vmem()] * 3,
        out_specs=(smem(), smem(), smem(), vmem()),
        scratch_shapes=[
            pltpu.VMEM((lines, TILE), jnp.int32),
            pltpu.SMEM((lines, TILE), jnp.int32),
            pltpu.SemaphoreType.DMA,
        ],
        cost_estimate=pl.CostEstimate(flops=0, bytes_accessed=8_000_000, transcendentals=0),
    )(numbers, counts, points)


def add_items(bits, half, lists, table, feats, line_feat, tile_feat, modes, acc, squares):
    tiles = table.shape[0] // ROWS
    at = 0
    for feat in feats:
        line_feat[at : at + feat.shape[0], :] = feat[...]
        at += feat.shape[0]
    line_feat[at:, :] = jnp.zeros((line_feat.shape[0] - at, line_feat.shape[1]), BF16)
    first = lists[0][1][half]
    count = sum(total[half] for _, total in lists)

    def build(t, carry):
        base = pl.multiple_of(t * ROWS, 8)
        rows = [spread(table, base + 8 * c) for c in range(3)]
        block = tile_block(rows)
        tile_feat[pl.ds(pl.multiple_of(t * TILE, TILE), TILE), :] = block.T.astype(BF16)
        value = 4.0 * table[pl.ds(base, ROWS), :]
        high = value.astype(BF16)
        low = (value - high.astype(F32)).astype(BF16)
        at = pl.ds(pl.multiple_of(t * MIX, 16), MIX)
        modes[at, :] = jnp.concatenate([high, low], axis=0)
        return carry

    lax.fori_loop(0, tiles, build, 0, unroll=4)
    mask = tiles - 1

    def unpack(at):
        code = lists[0][0][jnp.minimum(at, first)]
        if len(lists) > 1:
            code = jnp.where(at < first, code, lists[1][0][jnp.maximum(at - first, 0)])
        return lax.shift_right_logical(code, bits), code & mask

    def distances(u, at):
        line, tile = unpack(at)
        squares[u][...] = jnp.dot(
            tile_feat[pl.ds(pl.multiple_of(tile * TILE, TILE), TILE), :],
            line_feat[pl.ds(pl.multiple_of(line * FEATS, FEATS), FEATS), :],
            preferred_element_type=F32,
        )

    def gather(u, at):
        line, tile = unpack(at)
        square = jnp.maximum(squares[u][...], TINY)
        near = jnp.maximum(1.0 - square * lax.rsqrt(square), 0.0)
        fourth = near * near
        fourth = fourth * fourth
        phi = fourth * (1.25 - near)
        high = phi.astype(BF16)
        low = (phi - high.astype(F32)).astype(BF16)
        mode = modes[pl.ds(pl.multiple_of(tile * MIX, 16), MIX), :]
        got = jnp.dot(
            jnp.concatenate([mode, mode], axis=1),
            jnp.concatenate([high, low], axis=0),
            preferred_element_type=F32,
        )
        where = pl.ds(pl.multiple_of(line * ROWS, 8), ROWS)
        acc[where, :] = acc[where, :] + (got[0:ROWS] + got[ROWS:MIX])

    def body(j, carry):
        base = j * UNROLL
        for u in range(UNROLL):
            gather(u, base + u)
            distances(u, base + UNROLL + u)
        return carry

    for u in range(UNROLL):
        distances(u, u)
    lax.fori_loop(0, lax.div(count + (UNROLL - 1), jnp.int32(UNROLL)), body, 0)


def load_sum(table):
    tiles = table.shape[0] // ROWS
    return jnp.sum(table[pl.ds(7, tiles, stride=ROWS), :], axis=0, keepdims=True)


def early_kernel(parts, bits, *refs):
    lists = [(refs[i], refs[i + 1]) for i in range(0, 2 * parts, 2)]
    feats = refs[2 * parts : 3 * parts]
    table, acc, loads, line_feat, tile_feat, modes, *squares = refs[3 * parts :]
    acc[...] = jnp.zeros(acc.shape, F32)
    loads[...] = load_sum(table)
    add_items(bits, 0, lists, table, feats, line_feat, tile_feat, modes, acc, squares)


def late_kernel(own, lent, parts, bits, *refs):
    lists = [(refs[i], refs[i + 1]) for i in range(0, 2 * parts, 2)]
    feats = refs[2 * parts : 3 * parts]
    table, early, loads, points, motion, inverse, gravity, *rest = refs[3 * parts :]
    out_own, out_extra, out_state, out_row, out_plane, *rest = rest
    line_feat, tile_feat, modes, acc, *squares = rest
    total = loads[...] + load_sum(table)
    acceleration = inverse[...] * total + gravity[...]
    out_state[...] = motion[...] + TIME_STEP * acceleration
    step = TIME_STEP * motion[...] + 0.5 * TIME_STEP * TIME_STEP * acceleration
    row = lax.broadcasted_iota(jnp.int32, (8, 128), 0)
    lane = lax.broadcasted_iota(jnp.int32, (8, 128), 1)
    chosen = jnp.where((lane == row - 1) & (lane < 6), jnp.broadcast_to(step, (8, 128)), 0.0)
    weight = jnp.broadcast_to(jnp.sum(chosen, axis=1, keepdims=True), (8, 128))

    acc[...] = early[...]
    add_items(bits, 1, lists, table, feats, line_feat, tile_feat, modes, acc, squares)

    def finish(count, first, out):
        def one(l, carry):
            base = pl.multiple_of((first + l) * ROWS, 8)
            for c in range(3):
                value = jnp.sum(weight * acc[pl.ds(base + 8 * c, 8), :], axis=0, keepdims=True)
                out[pl.ds(c * count + l, 1), :] = value
            return carry

        lax.fori_loop(0, count, one, 0, unroll=4)

    finish(own, 0, out_own)
    if lent:
        finish(lent, own, out_extra)
    rows = out_row.shape[1] // 3
    wide = out_plane.shape[1] // 3
    for c in range(3):
        old = points[c * own : c * own + wide, :]
        out_plane[0, c * wide : (c + 1) * wide, :] = old
        out_plane[1, c * wide : (c + 1) * wide, :] = old + out_own[c * own : c * own + wide, :]
        old = points[pl.ds(c * own, rows, stride=wide), :]
        out_row[0, c * rows : (c + 1) * rows, :] = old
        out_row[1, c * rows : (c + 1) * rows, :] = (
            old + out_own[pl.ds(c * own, rows, stride=wide), :]
        )


def volume_kernel(
    keep, has_lent, points, shift, back, row_halo, plane_halo,
    out_shift, out_volume, out_change,
):
    planes, rows, depth = points.shape[1:]
    slab, ctrl = lax.axis_index("slab"), lax.axis_index("ctrl")
    slabs, ctrls = lax.axis_size("slab"), lax.axis_size("ctrl")
    row_id = lax.broadcasted_iota(jnp.int32, (rows, depth), 0)
    lane = lax.broadcasted_iota(jnp.int32, (rows, depth), 1)
    inside = (lane < depth - 1) & (row_id + ctrl * rows < ctrls * rows - 1)
    if has_lent:
        from_helper = (row_id >= 1) & is_heavy(slab, slabs)
    last_row = row_id == rows - 1

    def next_row(value, edge):
        return jnp.where(last_row, edge, pltpu.roll(value, rows - 1, 0))

    def next_depth(value):
        return pltpu.roll(value, depth - 1, 1)

    def level(x):
        found = []
        for field in range(2):
            parts = []
            for c in range(3):
                if x == planes:
                    here = plane_halo[field, c, 0:rows, :]
                    edge = plane_halo[field, c, rows : rows + 1, :]
                else:
                    here = points[c, x]
                    if field == 1:
                        moved = shift[c, x]
                        if has_lent and x >= keep:
                            moved = jnp.where(from_helper, back[c, x - keep], moved)
                        out_shift[c, x] = moved
                        here = here + moved
                    edge = row_halo[field, c, x : x + 1, :]
                there = next_row(here, edge)
                parts.append((here + there, there - here))
            found.append(parts)
        return found

    before = level(0)
    for x in range(planes):
        after = level(x + 1)
        volumes = []
        for field in range(2):
            edges = []
            for c in range(3):
                both0, step0 = before[field][c]
                both1, step1 = after[field][c]
                along, across, total = both1 - both0, step0 + step1, both0 + both1
                edges.append(
                    (
                        0.25 * (along + next_depth(along)),
                        0.25 * (across + next_depth(across)),
                        0.25 * (next_depth(total) - total),
                    )
                )
            ex, ey, ez = zip(*edges)
            volumes.append(
                ex[0] * (ey[1] * ez[2] - ey[2] * ez[1])
                + ex[1] * (ey[2] * ez[0] - ey[0] * ez[2])
                + ex[2] * (ey[0] * ez[1] - ey[1] * ez[0])
            )
        live = inside & (slab * planes + x < slabs * planes - 1)
        out_volume[x] = jnp.where(live, volumes[1], 0.0)
        out_change[x] = jnp.where(live, volumes[1] - volumes[0], 0.0)
        before = after


def is_heavy(slab, slabs):
    return (8 * slab >= 3 * slabs) & (8 * slab < 5 * slabs)


def local(
    face_pressure,
    face_area,
    face_center,
    motion,
    inverse_mass,
    control_points,
    control_modes,
    node_points,
    tile_list,
    tile_count,
):
    slabs, ctrls = lax.axis_size("slab"), lax.axis_size("ctrl")
    slab, ctrl = lax.axis_index("slab"), lax.axis_index("ctrl")
    _, planes, rows, depth = node_points.shape
    slots = tile_list.shape[2]
    own = planes * rows
    columns = control_points.shape[1]
    tiles = columns * slabs * ctrls // TILE
    bits = max(1, (tiles - 1).bit_length())
    pressure = face_pressure.reshape(1, -1)

    lend = slabs % 8 == 0 and slabs & (slabs - 1) == 0 and planes % 2 == 0
    unit = slabs // 8 * 2
    keep = planes // 2
    lent = (planes - keep) * rows if lend else 0
    heavy = [s for s in range(slabs) if is_heavy(s, slabs)]

    if lend:
        sent = pl.pallas_call(
            functools.partial(lend_kernel, keep),
            out_shape=jax.ShapeDtypeStruct((4 * lent, TILE), F32),
            in_specs=[vmem()] * 3,
            out_specs=vmem(),
            cost_estimate=pl.CostEstimate(flops=0, bytes_accessed=2_000_000, transcendentals=0),
        )(node_points, tile_list, tile_count)

    direct = columns % TILE == 0 and slabs & (slabs - 1) == 0 and ctrls & (ctrls - 1) == 0
    direct = direct and ctrls > 1 and (columns // TILE) & (columns // TILE - 1) == 0
    own_tiles = columns // TILE
    got = None
    order = []
    bit = slabs // 2
    while bit:
        order.append((bit, 0))
        bit //= 2
    bit = 1
    while bit < ctrls:
        order.append((0, bit))
        bit *= 2

    def placed(number):
        if not direct:
            return number
        device = lax.axis_index("slab") * ctrls + lax.axis_index("ctrl")
        apart = (number >> (own_tiles.bit_length() - 1)) ^ device
        at = jnp.zeros(number.shape, jnp.int32)
        for turn, (slab_bit, ctrl_bit) in enumerate(order):
            flag = slab_bit * ctrls + ctrl_bit
            at = at + jnp.where((apart & flag) != 0, own_tiles << turn, 0)
        return at + (number & (own_tiles - 1))

    plane_id = lax.broadcasted_iota(jnp.int32, (planes, rows), 0)
    row_id = lax.broadcasted_iota(jnp.int32, (planes, rows), 1)
    counts = tile_count
    if lend:
        lends = is_heavy(slab, slabs) & (plane_id >= keep) & (row_id >= 1)
        counts = jnp.where(lends, 0, counts)
    flat_points = node_points.reshape(3 * own, depth)
    own_lists = prepared(
        0, slots, bits, placed, lambda count: count,
        tile_list.reshape(own, slots), counts.reshape(own, 1), flat_points,
    )

    def borrowed(got):
        def counted(count):
            at = lax.axis_index("slab")
            helper = is_heavy(at ^ unit, slabs) & jnp.logical_not(is_heavy(at, slabs))
            line = lax.broadcasted_iota(jnp.int32, count.shape, 0)
            return jnp.where(helper & (line % rows >= 1), count, 0)

        listed = got[3 * lent :]
        return prepared(
            own, slots, bits, placed, counted, listed, listed[:, slots : slots + 1], got[: 3 * lent]
        )

    if direct:
        early = pl.pallas_call(
            pack_kernel,
            out_shape=jax.ShapeDtypeStruct((own_tiles * ROWS, TILE), F32),
            in_specs=[vmem()] * 5,
            out_specs=vmem(),
        )(pressure, face_area, face_center, control_points, control_modes)
        own_ready, lent_ready = False, False
        for slab_bit, ctrl_bit in order[:-1]:
            size = early.shape[0]
            if got is not None and not own_ready:
                early, own_lists = lax.optimization_barrier((early, own_lists))
                own_ready = True
            elif own_ready and not lent_ready:
                early, lent_lists = lax.optimization_barrier((early, lent_lists))
                lent_ready = True
            if lend and slab_bit == unit:
                reply = swapped(jnp.concatenate([early, sent], axis=0), slab_bit, ctrl_bit)
                got = reply[size:]
                reply = reply[:size]
                lent_lists = borrowed(got)
            else:
                reply = swapped(early, slab_bit, ctrl_bit)
            early = jnp.concatenate([early, reply], axis=0)
        late = swapped(early, *order[-1])
    else:
        loads = pl.pallas_call(
            loads_kernel,
            out_shape=jax.ShapeDtypeStruct((1, TILE), F32),
            in_specs=[vmem()] * 3,
            out_specs=vmem(),
        )(pressure, face_area, face_center)
        loads = lax.psum(loads, ("slab", "ctrl"))
        whole = jnp.concatenate([control_points, control_modes], axis=0)
        whole = lax.all_gather(whole, ("slab", "ctrl"), axis=1, tiled=True)
        whole = whole.reshape(7, 3, tiles, TILE).transpose(2, 1, 0, 3)
        spare = jnp.zeros((tiles, 3, 1, TILE), F32).at[0, 0, 0, :].set(loads[0])
        table = jnp.concatenate([whole, spare], axis=2).reshape(tiles * ROWS, TILE)
        early, late = table[: tiles // 2 * ROWS], table[tiles // 2 * ROWS :]

    if lend and got is None:
        lent_lists = borrowed(swapped(sent, unit, 0))
    groups = [own_lists] + ([lent_lists] if lend else [])
    lines = own + lent

    def wide(value):
        return jnp.pad(value, (0, TILE - value.shape[0])).reshape(1, TILE)

    half = tiles // 2
    parts = len(groups)
    early_items = [ref for group in groups for ref in (group[0], group[2])]
    late_items = [ref for group in groups for ref in (group[1], group[2])]
    feats = [group[3] for group in groups]
    list_specs = [smem()] * (2 * parts) + [vmem()] * parts
    scratch = [
        pltpu.VMEM(((lines + 1) * FEATS, depth), BF16),
        pltpu.VMEM((half * TILE, FEATS), BF16),
        pltpu.VMEM((half * MIX, TILE), BF16),
    ]
    squares = [pltpu.VMEM((TILE, depth), F32)] * UNROLL
    partial, part_loads = pl.pallas_call(
        functools.partial(early_kernel, parts, bits),
        out_shape=(
            jax.ShapeDtypeStruct(((lines + 1) * ROWS, depth), F32),
            jax.ShapeDtypeStruct((1, TILE), F32),
        ),
        in_specs=list_specs + [vmem()],
        out_specs=(vmem(), vmem()),
        scratch_shapes=scratch + squares,
        compiler_params=pltpu.CompilerParams(vmem_limit_bytes=32 << 20),
        cost_estimate=pl.CostEstimate(flops=0, bytes_accessed=30_000_000, transcendentals=0),
    )(*early_items, *feats, early)
    outs = pl.pallas_call(
        functools.partial(late_kernel, own, lent, parts, bits),
        out_shape=(
            jax.ShapeDtypeStruct((3 * own, depth), F32),
            jax.ShapeDtypeStruct((3 * max(lent, 8), depth), F32),
            jax.ShapeDtypeStruct((1, TILE), F32),
            jax.ShapeDtypeStruct((2, 3 * planes, depth), F32),
            jax.ShapeDtypeStruct((2, 3 * rows, depth), F32),
        ),
        in_specs=list_specs + [vmem()] * 7,
        out_specs=(vmem(),) * 5,
        scratch_shapes=scratch + [pltpu.VMEM(((lines + 1) * ROWS, depth), F32)] + squares,
        compiler_params=pltpu.CompilerParams(vmem_limit_bytes=32 << 20),
    )(
        *late_items, *feats, late, partial, part_loads, flat_points,
        wide(motion), wide(inverse_mass), wide(jnp.array(GRAVITY, F32)),
    )
    shift, lent_shift, state, row_sent, plane_sent = outs

    if lend:
        back = lax.ppermute(lent_shift, "slab", [(h ^ unit, h) for h in heavy])
        back = back.reshape(3, planes - keep, rows, depth)
    else:
        back = jnp.zeros((3, 1, rows, depth), F32)
    row_halo = shifted_back(row_sent, "ctrl").reshape(2, 3, planes, depth)
    plane_sent = plane_sent.reshape(2, 3, rows, depth)
    plane_halo = shifted_back(
        jnp.concatenate([plane_sent, row_halo[:, :, :1]], axis=2), "slab"
    )
    node_shift, volume, change = pl.pallas_call(
        functools.partial(volume_kernel, keep, lend),
        out_shape=(
            jax.ShapeDtypeStruct(node_points.shape, F32),
            jax.ShapeDtypeStruct(node_points.shape[1:], F32),
            jax.ShapeDtypeStruct(node_points.shape[1:], F32),
        ),
        in_specs=[vmem()] * 5,
        out_specs=(vmem(),) * 3,
    )(node_points, shift.reshape(3, planes, rows, depth), back, row_halo, plane_halo)
    return node_shift, volume, change, state[0, : motion.shape[0]]


def solution(mesh):
    placed = (
        P(("slab", "ctrl")),
        P(None, ("slab", "ctrl")),
        P(None, ("slab", "ctrl")),
        P(),
        P(),
        P(None, ("slab", "ctrl")),
        P(None, ("slab", "ctrl")),
        P(None, "slab", "ctrl", None),
        P("slab", "ctrl", None),
        P("slab", "ctrl"),
    )
    return jax.shard_map(
        local,
        mesh=mesh,
        in_specs=placed,
        out_specs=(
            P(None, "slab", "ctrl", None),
            P("slab", "ctrl", None),
            P("slab", "ctrl", None),
            P(),
        ),
        check_vma=False,
    )
```

time: 84.4 us -> 71.6 us (0.85)
  the two profiles are of different devices: /device:TPU:19 before, /device:TPU:0 now
where the time goes in v2:
time: 71.6 us; the launch traced here: 70.8 us
  waiting for transfers between devices  26.4 us (37%)
  Pallas kernels  23.6 us (33%)
  starting transfers between devices  12.5 us (17%)
  local copies, waits for them, and re-layouts  5.12 us (7%)
  other arithmetic  2.38 us (3%)
  between operations  0.91 us (1%)
    ppermute x2, waiting for transfers between devices, shifted_back(): lax.ppermute(value, axis, [(i, i - 1) for i in range(1, lax.axis_size(axi...  20.4 us
    ppermute x5, starting transfers between devices, swapped(): return lax.ppermute(value, ('slab', 'ctrl'), pairs)  9.22 us
    pallas_call x2, Pallas kernels, prepared(): pl.pallas_call(functools.partial(prepare_kernel, first, slots, bits, plac...  7.97 us
    ppermute x5, waiting for transfers between devices, swapped(): return lax.ppermute(value, ('slab', 'ctrl'), pairs)  5.94 us
    pallas_call x1, Pallas kernels, local(): pl.pallas_call(functools.partial(late_kernel, own, lent, parts, bits), ou...  5.75 us
    pallas_call x1, Pallas kernels, local(): pl.pallas_call(functools.partial(early_kernel, parts, bits), out_shape=(j...  4.71 us
    ppermute x2, starting transfers between devices, shifted_back(): lax.ppermute(value, axis, [(i, i - 1) for i in range(1, lax.axis_size(axi...  2.57 us
    unnamed x35, local copies, waits for them, and re-layouts  1.98 us
  transfers between devices with their start and end apart: 8, of which 5 were waited for; matrix products, arithmetic and copies ran while one was open for 5% of the time, Pallas kernels for 20%

profile of v2, /device:TPU:0, one launch (start us, length us, event | category | flops | bytes accessed | tf_op | source)
XLA Modules:
  0.0 70.8 jit_solution(17581657452414815937)
XLA Ops:
  0.6 1.7 %shard_map.138 = f32[48,128]{1,0:T(8,128)} custom-call(f32[1,4096]{1,0:T(1,128)} %bitcast.21, f32[3,4096]{1,0:T(4,128)} %area.1, f32[3,4096]{1,0:T(4,128)} %center.1, f32[3,256]{1,0:T(4,128)} %points.3, f32[18,256]{1,0:T(8,128)} %modes.1), custom_call_target="tpu_custom_call" | custom-call | tf_op jit(solution)/shard_map/pallas_call | solution.py:509
  2.3 4.0 %collective-permute-start = (f32[48,128]{1,0:T(8,128)}, f32[48,128]{1,0:T(8,128)S(1)}, u32[]{:S(2)}, u32[]{:S(2)}) collective-permute-start(f32[48,128]{1,0:T(8,128)} %shard_map.138), channel_id=1, source_target_pairs={{0,16},{1,17},{2,18},{3,19},{4,20},{5,21},{6,22},{7,23},{8,24},{9,... | collective-permute-start | bytes 73736 | tf_op jit(solution)/shard_map/ppermute | solution.py:37
  6.4 0.0 copy-start.15
  6.4 0.0 copy-start.16
  6.4 1.6 %shard_map.139 = f32[128,128]{1,0:T(8,128)} custom-call(f32[3,8,8,128]{3,2,1,0:T(8,128)} %points.5, s32[8,8,16]{2,1,0:T(8,128)} %numbers.1, s32[8,8]{1,0:T(8,128)} %counts.1), custom_call_target="tpu_custom_call" | custom-call | bytes 2000000 | tf_op jit(solution)/shard_map/pallas_call | solution.py:451
  8.0 0.4 collective-permute-done
  8.4 0.8 %pad_maximum_fusion.1 = f32[224,128]{1,0:T(8,128)S(1)} fusion(f32[128,128]{1,0:T(8,128)} %shard_map.139, f32[48,128]{1,0:T(8,128)S(1)} %collective-permute-done, f32[48,128]{1,0:T(8,128)} %shard_map.138), kind=kLoop, calls=%fused_computation.1 | loop fusion | flops 57344 | bytes 229376 | tf_op jit(solution)/shard_map/concatenate | solution.py:525
  9.2 2.0 %collective-permute-start.1 = (f32[224,128]{1,0:T(8,128)S(1)}, f32[224,128]{1,0:T(8,128)S(1)}, u32[]{:S(2)}, u32[]{:S(2)}) collective-permute-start(f32[224,128]{1,0:T(8,128)S(1)} %pad_maximum_fusion.1), channel_id=1, source_target_pairs={{0,8},{1,9},{2,10},{3,11},{4,12},{5,13},{6,14},{7,15},{8,0},{9,1},... | collective-permute-start | bytes 344072 | tf_op jit(solution)/shard_map/ppermute | solution.py:37
  11.2 0.8 %and_select_fusion = s32[8,8]{1,0:T(8,128)S(1)} fusion(s32[8,8]{1,0:T(8,128)} %counts.1, pred[8]{0:T(512)(128)(4,1)S(1)} %get-tuple-element.63, pred[8]{0:T(512)(128)(4,1)S(1)} %get-tuple-element.62), kind=kLoop, calls=%fused_computation.6 | loop fusion | flops 128 | bytes 528 | tf_op jit(solution)/shard_map/jit(_where)/select_n | solution.py:489
  12.0 0.7 reshape.52.counts
  12.7 5.0 %shard_map.140 = (s32[1056]{0:T(1024)}, s32[1056]{0:T(1024)}, s32[2]{0:T(128)}, bf16[2048,128]{1,0:T(8,128)(2,1)}) custom-call(s32[64,16]{1,0:T(8,128)} %bitcast.17, s32[64,1]{1,0:T(8,128)} %reshape.52.counts, f32[192,128]{1,0:T(8,128)} %bitcast.13), custom_call_target="tpu_custom_call" | custom-call | bytes 8000000 | tf_op jit(solution)/shard_map/pallas_call | solution.py:201
  17.6 0.0 copy-start
  17.6 0.0 copy-start.5
  17.7 0.0 copy-start.8
  17.7 0.0 collective-permute-done.1
  17.7 0.6 fusion
  18.3 0.7 %pad_maximum_fusion.2 = f32[192,128]{1,0:T(8,128)S(1)} fusion(f32[96,128]{1,0:T(8,128)S(1)} %get-tuple-element.61, f32[48,128]{1,0:T(8,128)S(1)} %collective-permute-done, f32[48,128]{1,0:T(8,128)} %shard_map.138), kind=kLoop, calls=%fused_computation.2 | loop fusion | flops 49152 | bytes 196608 | tf_op jit(solution)/shard_map/concatenate | solution.py:531
  19.0 1.5 %collective-permute-start.2 = (f32[192,128]{1,0:T(8,128)S(1)}, f32[192,128]{1,0:T(8,128)S(1)}, u32[]{:S(2)}, u32[]{:S(2)}) collective-permute-start(f32[192,128]{1,0:T(8,128)S(1)} %pad_maximum_fusion.2), channel_id=1, source_target_pairs={{0,4},{1,5},{2,6},{3,7},{4,0},{5,1},{6,2},{7,3},{8,12},{9,13},{10,... | collective-permute-start | bytes 294920 | tf_op jit(solution)/shard_map/ppermute | solution.py:37
  20.6 0.6 slice.29.numbers
  21.2 0.7 slice.30.counts
  21.9 3.0 %shard_map.141 = (s32[544]{0:T(1024)}, s32[544]{0:T(1024)}, s32[2]{0:T(128)}, bf16[1024,128]{1,0:T(8,128)(2,1)}) custom-call(f32[32,128]{1,0:T(8,128)} %slice.29.numbers, f32[32,1]{1,0:T(8,128)} %slice.30.counts, f32[96,128]{1,0:T(8,128)} %get-tuple-element.60.points), custom_call_target="tpu_custom_call" | custom-call | bytes 8000000 | tf_op jit(solution)/shard_map/pallas_call | solution.py:201
  24.9 0.0 copy-start.2
  24.9 0.0 copy-start.7
  24.9 0.0 copy-start.1
  24.9 0.0 copy-start.4
  24.9 0.0 copy-start.6
  24.9 0.0 copy-start.10
  25.0 0.0 copy-start.11
  25.0 0.0 collective-permute-done.2
  25.0 0.1 collective-permute-start.3
  25.1 1.4 %collective-permute-done.3 = f32[384,128]{1,0:T(8,128)S(1)} collective-permute-done((f32[384,128]{1,0:T(8,128)S(1)}, f32[384,128]{1,0:T(8,128)S(1)}, u32[]{:S(2)}, u32[]{:S(2)}) %collective-permute-start.3) | collective-permute-done | bytes 196640 | tf_op jit(solution)/shard_map/ppermute | solution.py:37
  26.5 1.6 %collective-permute-start.4 = (f32[768,128]{1,0:T(8,128)S(1)}, f32[768,128]{1,0:T(8,128)S(1)}, u32[]{:S(2)}, u32[]{:S(2)}) collective-permute-start(f32[768,128]{1,0:T(8,128)S(1)} %constant_dynamic-update-slice_fusion.refs_6_), channel_id=1, source_target_pairs={{0,2},{1,3},{2,0},{3,1},{4,6},{5,7},{6,4},{7,5},{8,10},{9,11},{10,... | collective-permute-start | bytes 1179656 | tf_op jit(solution)/shard_map/ppermute | solution.py:37
  28.1 0.0 copy-done.15
  28.1 0.0 copy-done.16
  28.1 0.0 copy-done
  28.2 0.0 copy-done.5
  28.2 0.0 copy-done.8
  28.2 0.0 copy-done.2
  28.2 0.0 copy-done.7
  28.2 0.0 copy-start.9
  28.2 0.7 copy-done.9
  28.9 4.7 %shard_map.142 = (f32[2328,128]{1,0:T(8,128)S(1)}, f32[1,128]{1,0:T(1,128)S(1)}) custom-call(s32[1056]{0:T(1024)S(1)} %copy-done.5, s32[2]{0:T(128)S(1)} %copy-done.8, s32[544]{0:T(1024)S(1)} %copy-done.7, s32[2]{0:T(128)S(1)} %copy-done.9, bf16[2048,128]{1,0:T(8,128)(2,1)S(1)} %copy-done, bf16[1024,128]{1,0:T(8,128)(2,1)S(1)} %copy-done.2, ...), custom_call_target="tpu_custom_call" | custom-call | bytes 30000000 | tf_op jit(solution)/shard_map/pallas_call | solution.py:568
  33.6 4.2 %collective-permute-done.4.refs_6_ = f32[768,128]{1,0:T(8,128)S(1)} collective-permute-done((f32[768,128]{1,0:T(8,128)S(1)}, f32[768,128]{1,0:T(8,128)S(1)}, u32[]{:S(2)}, u32[]{:S(2)}) %collective-permute-start.4) | collective-permute-done | bytes 393248 | tf_op jit(solution)/shard_map/ppermute | solution.py:37
  37.8 0.0 copy-done.1
  37.8 0.0 copy-done.4
  37.8 0.0 copy-done.6
  37.8 0.0 copy-done.10
  37.8 0.0 copy-done.11
  37.8 5.8 %shard_map.143 = (f32[192,128]{1,0:T(8,128)S(1)}, f32[96,128]{1,0:T(8,128)S(1)}, f32[1,128]{1,0:T(1,128)S(1)}, f32[2,24,128]{2,1,0:T(8,128)S(1)}, f32[2,24,128]{2,1,0:T(8,128)S(1)}) custom-call(s32[1056]{0:T(1024)S(1)} %copy-done.4, s32[2]{0:T(128)S(1)} %copy-done.8, s32[544]{0:T(1024)S(1)} %copy-done.6, s32[2]{0:T(128)S(1)} %copy-done.10, ...), custom_call_target="tpu_custom_call" | custom-call | tf_op jit(solution)/shard_map/pallas_call | solution.py:580
  43.5 0.0 copy-start.3
  43.6 0.6 copy-done.3
  44.2 1.3 %collective-permute-start.6 = (f32[2,24,128]{2,1,0:T(8,128)S(1)}, f32[2,24,128]{2,1,0:T(8,128)S(1)}, u32[]{:S(2)}, u32[]{:S(2)}) collective-permute-start(f32[2,24,128]{2,1,0:T(8,128)S(1)} %get-tuple-element.54), channel_id=1, source_target_pairs={{1,0},{2,1},{3,2},{5,4},{6,5},{7,6},{9,8},{10,9},{11,10},{13,12},{... | collective-permute-start | bytes 73736 | tf_op jit(solution)/shard_map/ppermute | solution.py:41
  45.5 0.7 collective-permute-start.5
  46.1 1.1 %collective-permute-done.6 = f32[2,24,128]{2,1,0:T(8,128)S(1)} collective-permute-done((f32[2,24,128]{2,1,0:T(8,128)S(1)}, f32[2,24,128]{2,1,0:T(8,128)S(1)}, u32[]{:S(2)}, u32[]{:S(2)}) %collective-permute-start.6) | collective-permute-done | bytes 24608 | tf_op jit(solution)/shard_map/ppermute | solution.py:41
  47.3 0.0 copy-start.14
  47.3 1.3 %collective-permute-start.7 = (f32[2,3,9,128]{3,2,1,0:T(8,128)S(1)}, f32[2,3,9,128]{3,2,1,0:T(8,128)S(1)}, u32[]{:S(2)}, u32[]{:S(2)}) collective-permute-start(f32[2,3,9,128]{3,2,1,0:T(8,128)S(1)} %pad_maximum_fusion.3), channel_id=1, source_target_pairs={{4,0},{8,4},{12,8},{16,12},{20,16},{24,20},{28,24},{5,1},{9,5},{13... | collective-permute-start | bytes 82952 | tf_op jit(solution)/shard_map/ppermute | solution.py:41
  48.6 0.5 slice_bitcast_fusion
  49.1 0.0 collective-permute-done.5
  49.1 0.0 copy-start.12
  49.1 19.3 %collective-permute-done.7.plane_halo = f32[2,3,9,128]{3,2,1,0:T(8,128)S(1)} collective-permute-done((f32[2,3,9,128]{3,2,1,0:T(8,128)S(1)}, f32[2,3,9,128]{3,2,1,0:T(8,128)S(1)}, u32[]{:S(2)}, u32[]{:S(2)}) %collective-permute-start.7) | collective-permute-done | bytes 27680 | tf_op jit(solution)/shard_map/ppermute | solution.py:41
  68.4 0.0 copy-done.14
  68.4 0.0 copy-done.12
  68.4 0.6 copy-done.13
  69.0 1.8 %shard_map.144 = (f32[3,8,8,128]{3,2,1,0:T(8,128)}, f32[8,8,128]{2,1,0:T(8,128)}, f32[8,8,128]{2,1,0:T(8,128)}) custom-call(f32[3,8,8,128]{3,2,1,0:T(8,128)} %points.5, f32[3,8,8,128]{3,2,1,0:T(8,128)} %bitcast.15, f32[3,4,8,128]{3,2,1,0:T(8,128)} %bitcast.18, f32[2,3,8,128]{3,2,1,0:T(8,128)} %bitcast.20, f32[2,3,9,128]{3,2,1,0:T(8,128)} %copy-done.13), custom_call_target="tpu_custom_call" | custom-call | tf_op jit(solution)/shard_map/pallas_call | solution.py:609
  (8 shorter events, 0.1 us)
Async XLA Ops:
  2.3 6.1 %collective-permute-start = (f32[48,128]{1,0:T(8,128)}, f32[48,128]{1,0:T(8,128)S(1)}, u32[]{:S(2)}, u32[]{:S(2)}) collective-permute-start(f32[48,128]{1,0:T(8,128)} %shard_map.138), channel_id=1, source_target_pairs={{0,16},{1,17},{2,18},{3,19},{4,20},{5,21},{6,22},{7,23},{8,24},{9,... | collective-permute-start | bytes 73736 | tf_op jit(solution)/shard_map/ppermute | solution.py:37
  6.4 21.8 %copy-start.15 = (f32[6]{0:T(128)S(1)}, f32[6]{0:T(128)}, u32[]{:S(2)}) copy-start(f32[6]{0:T(128)} %param.15) | copy-start | bytes 76
  6.4 21.8 %copy-start.16 = (f32[6]{0:T(128)S(1)}, f32[6]{0:T(128)}, u32[]{:S(2)}) copy-start(f32[6]{0:T(128)} %param.14) | copy-start | bytes 76
  9.2 8.4 %collective-permute-start.1 = (f32[224,128]{1,0:T(8,128)S(1)}, f32[224,128]{1,0:T(8,128)S(1)}, u32[]{:S(2)}, u32[]{:S(2)}) collective-permute-start(f32[224,128]{1,0:T(8,128)S(1)} %pad_maximum_fusion.1), channel_id=1, source_target_pairs={{0,8},{1,9},{2,10},{3,11},{4,12},{5,13},{6,14},{7,15},{8,0},{9,1},... | collective-permute-start | bytes 344072 | tf_op jit(solution)/shard_map/ppermute | solution.py:37
  17.6 10.5 %copy-start = (bf16[2048,128]{1,0:T(8,128)(2,1)S(1)}, bf16[2048,128]{1,0:T(8,128)(2,1)}, u32[]{:S(2)}) copy-start(bf16[2048,128]{1,0:T(8,128)(2,1)} %get-tuple-element.45.refs_4_) | copy-start | bytes 1572868
  17.6 10.5 %copy-start.5 = (s32[1056]{0:T(1024)S(1)}, s32[1056]{0:T(1024)}, u32[]{:S(2)}) copy-start(s32[1056]{0:T(1024)} %get-tuple-element.48.refs_0_) | copy-start | bytes 12676
  17.7 10.5 %copy-start.8 = (s32[2]{0:T(128)S(1)}, s32[2]{0:T(128)}, u32[]{:S(2)}) copy-start(s32[2]{0:T(128)} %get-tuple-element.37.refs_1_) | copy-start | bytes 28
  19.0 5.9 %collective-permute-start.2 = (f32[192,128]{1,0:T(8,128)S(1)}, f32[192,128]{1,0:T(8,128)S(1)}, u32[]{:S(2)}, u32[]{:S(2)}) collective-permute-start(f32[192,128]{1,0:T(8,128)S(1)} %pad_maximum_fusion.2), channel_id=1, source_target_pairs={{0,4},{1,5},{2,6},{3,7},{4,0},{5,1},{6,2},{7,3},{8,12},{9,13},{10,... | collective-permute-start | bytes 294920 | tf_op jit(solution)/shard_map/ppermute | solution.py:37
  24.9 3.3 %copy-start.2 = (bf16[1024,128]{1,0:T(8,128)(2,1)S(1)}, bf16[1024,128]{1,0:T(8,128)(2,1)}, u32[]{:S(2)}) copy-start(bf16[1024,128]{1,0:T(8,128)(2,1)} %get-tuple-element.46.refs_5_) | copy-start | bytes 786436
  24.9 3.3 %copy-start.7 = (s32[544]{0:T(1024)S(1)}, s32[544]{0:T(1024)}, u32[]{:S(2)}) copy-start(s32[544]{0:T(1024)} %get-tuple-element.49.refs_2_) | copy-start | bytes 6532
  24.9 12.8 %copy-start.1 = (f32[3,8,8,128]{3,2,1,0:T(8,128)S(1)}, f32[3,8,8,128]{3,2,1,0:T(8,128)}, u32[]{:S(2)}) copy-start(f32[3,8,8,128]{3,2,1,0:T(8,128)} %points.5) | copy-start | bytes 294916
  24.9 12.8 %copy-start.4 = (s32[1056]{0:T(1024)S(1)}, s32[1056]{0:T(1024)}, u32[]{:S(2)}) copy-start(s32[1056]{0:T(1024)} %get-tuple-element.36.refs_0_) | copy-start | bytes 12676
  24.9 12.8 %copy-start.6 = (s32[544]{0:T(1024)S(1)}, s32[544]{0:T(1024)}, u32[]{:S(2)}) copy-start(s32[544]{0:T(1024)} %get-tuple-element.43.refs_2_) | copy-start | bytes 6532
  24.9 12.8 %copy-start.10 = (s32[2]{0:T(128)S(1)}, s32[2]{0:T(128)}, u32[]{:S(2)}) copy-start(s32[2]{0:T(128)} %get-tuple-element.44.refs_3_) | copy-start | bytes 28
  25.0 12.8 %copy-start.11 = (f32[1,128]{1,0:T(1,128)S(1)}, f32[1,128]{1,0:T(1,128)}, u32[]{:S(2)}) copy-start(f32[1,128]{1,0:T(1,128)} %constant.30.refs_12_) | copy-start | bytes 1540
  25.0 1.5 %collective-permute-start.3 = (f32[384,128]{1,0:T(8,128)S(1)}, f32[384,128]{1,0:T(8,128)S(1)}, u32[]{:S(2)}, u32[]{:S(2)}) collective-permute-start(f32[384,128]{1,0:T(8,128)S(1)} %pad_maximum_fusion), channel_id=1, source_target_pairs={{0,1},{1,0},{2,3},{3,2},{4,5},{5,4},{6,7},{7,6},{8,9},{9,8},{10,11... | collective-permute-start | bytes 589832 | tf_op jit(solution)/shard_map/ppermute | solution.py:37
  26.5 11.2 %collective-permute-start.4 = (f32[768,128]{1,0:T(8,128)S(1)}, f32[768,128]{1,0:T(8,128)S(1)}, u32[]{:S(2)}, u32[]{:S(2)}) collective-permute-start(f32[768,128]{1,0:T(8,128)S(1)} %constant_dynamic-update-slice_fusion.refs_6_), channel_id=1, source_target_pairs={{0,2},{1,3},{2,0},{3,1},{4,6},{5,7},{6,4},{7,5},{8,10},{9,11},{10,... | collective-permute-start | bytes 1179656 | tf_op jit(solution)/shard_map/ppermute | solution.py:37
  28.2 0.7 copy-start.9
  43.5 0.6 copy-start.3
  44.2 3.1 %collective-permute-start.6 = (f32[2,24,128]{2,1,0:T(8,128)S(1)}, f32[2,24,128]{2,1,0:T(8,128)S(1)}, u32[]{:S(2)}, u32[]{:S(2)}) collective-permute-start(f32[2,24,128]{2,1,0:T(8,128)S(1)} %get-tuple-element.54), channel_id=1, source_target_pairs={{1,0},{2,1},{3,2},{5,4},{6,5},{7,6},{9,8},{10,9},{11,10},{13,12},{... | collective-permute-start | bytes 73736 | tf_op jit(solution)/shard_map/ppermute | solution.py:41
  45.5 3.6 %collective-permute-start.5 = (f32[96,128]{1,0:T(8,128)S(1)}, f32[96,128]{1,0:T(8,128)S(1)}, u32[]{:S(2)}, u32[]{:S(2)}) collective-permute-start(f32[96,128]{1,0:T(8,128)S(1)} %get-tuple-element.53), channel_id=1, source_target_pairs={{4,12},{24,16},{5,13},{25,17},{6,14},{26,18},{7,15},{27,19}} | collective-permute-start | bytes 147464 | tf_op jit(solution)/shard_map/ppermute | solution.py:600
  47.3 21.2 %copy-start.14 = (f32[2,24,128]{2,1,0:T(8,128)}, f32[2,24,128]{2,1,0:T(8,128)S(1)}, u32[]{:S(2)}) copy-start(f32[2,24,128]{2,1,0:T(8,128)S(1)} %collective-permute-done.6) | copy-start | bytes 73732
  47.3 21.1 %collective-permute-start.7 = (f32[2,3,9,128]{3,2,1,0:T(8,128)S(1)}, f32[2,3,9,128]{3,2,1,0:T(8,128)S(1)}, u32[]{:S(2)}, u32[]{:S(2)}) collective-permute-start(f32[2,3,9,128]{3,2,1,0:T(8,128)S(1)} %pad_maximum_fusion.3), channel_id=1, source_target_pairs={{4,0},{8,4},{12,8},{16,12},{20,16},{24,20},{28,24},{5,1},{9,5},{13... | collective-permute-start | bytes 82952 | tf_op jit(solution)/shard_map/ppermute | solution.py:41
  49.1 19.3 %copy-start.12 = (f32[96,128]{1,0:T(8,128)}, f32[96,128]{1,0:T(8,128)S(1)}, u32[]{:S(2)}) copy-start(f32[96,128]{1,0:T(8,128)S(1)} %collective-permute-done.5) | copy-start | bytes 147460
  68.4 0.6 copy-start.13

commit v3 on v2

--- a/solution.py
+++ b/solution.py
@@ -19,6 +19,10 @@
 BF16 = jnp.bfloat16
 
 
+def limited(mib):
+    return pltpu.CompilerParams(vmem_limit_bytes=mib << 20)
+
+
 def vmem():
     return pl.BlockSpec(memory_space=pltpu.VMEM)
 
@@ -56,9 +60,8 @@
     return row
 
 
-def pack_kernel(pressure, area, center, points, modes, out):
-    row = load_rows(pressure[...], area[...], center[...])
-    for t in range(out.shape[0] // ROWS):
+def pack_table(row, points, modes, out):
+    for t in range(points.shape[1] // TILE):
         span = slice(t * TILE, (t + 1) * TILE)
         base = t * ROWS
         for c in range(3):
@@ -68,6 +71,41 @@
                 out[at : at + 1, :] = modes[3 * k + c : 3 * k + c + 1, span]
             at = base + 8 * c + 7
             out[at : at + 1, :] = row if (t == 0 and c == 0) else jnp.zeros((1, 128), F32)
+
+
+def count_column(counts, x):
+    rows = counts.shape[1]
+    row = lax.broadcasted_iota(jnp.int32, (rows, rows), 0)
+    lane = lax.broadcasted_iota(jnp.int32, (rows, rows), 1)
+    many = jnp.broadcast_to(counts[x : x + 1, :].astype(F32), (rows, rows))
+    return jnp.sum(jnp.where(row == lane, many, 0.0), axis=1, keepdims=True)
+
+
+def pack_lent(planes, base, nodes, numbers, counts, out):
+    rows, slots = numbers.shape[1:]
+    lent = len(planes) * rows
+    wide = lax.broadcasted_iota(jnp.int32, (rows, out.shape[1]), 1)
+    for i, x in enumerate(planes):
+        at = base + i * rows
+        for c in range(3):
+            out[at + c * lent : at + c * lent + rows, :] = nodes[c, x]
+        at = at + 3 * lent
+        out[at : at + rows, :] = jnp.where(wide == slots, count_column(counts, x), 0.0)
+        out[at : at + rows, 0:slots] = numbers[x].astype(F32)
+
+
+def pack_kernel(spans, pressure, area, center, points, modes, nodes, numbers, counts, out, *lents):
+    row = load_rows(pressure[...], area[...], center[...])
+    pack_table(row, points, modes, out)
+    if spans:
+        pack_lent(spans[0], points.shape[1] // TILE * ROWS, nodes, numbers, counts, out)
+    for span, lent in zip(spans[1:], lents):
+        pack_lent(span, 0, nodes, numbers, counts, lent)
+
+
+def lend_kernel(spans, nodes, numbers, counts, *outs):
+    for span, out in zip(spans, outs):
+        pack_lent(span, 0, nodes, numbers, counts, out)
 
 
 def loads_kernel(pressure, area, center, out):
@@ -128,59 +166,19 @@
     )
 
 
-def lend_kernel(keep, points, numbers, counts, out):
-    _, planes, rows, _ = points.shape
-    slots = numbers.shape[2]
-    lent = (planes - keep) * rows
-    row = lax.broadcasted_iota(jnp.int32, (rows, rows), 0)
-    lane = lax.broadcasted_iota(jnp.int32, (rows, rows), 1)
-    wide = lax.broadcasted_iota(jnp.int32, (rows, out.shape[1]), 1)
-    for x in range(keep, planes):
-        at = (x - keep) * rows
-        for c in range(3):
-            out[c * lent + at : c * lent + at + rows, :] = points[c, x]
-        many = jnp.broadcast_to(counts[x : x + 1, :].astype(F32), (rows, rows))
-        column = jnp.sum(jnp.where(row == lane, many, 0.0), axis=1, keepdims=True)
-        at = at + 3 * lent
-        out[at : at + rows, :] = jnp.where(wide == slots, column, 0.0)
-        out[at : at + rows, 0:slots] = numbers[x].astype(F32)
-
-
-def prepare_kernel(
-    first, slots, bits, placed, counted, numbers, counts, points,
-    items_a, items_b, totals, line_feat, codes, listed, sem,
-):
-    lines = numbers.shape[0]
-    number = numbers[:, 0:slots].astype(jnp.int32)
-    count = counted(counts[...].astype(jnp.int32))
-    row = lax.broadcasted_iota(jnp.int32, (lines, slots), 0)
-    slot = lax.broadcasted_iota(jnp.int32, (lines, slots), 1)
-    code = lax.shift_left(row + first, jnp.full_like(row, bits)) + placed(number)
-    codes[:, 0:slots] = jnp.where(slot < count, code, -1)
-    codes[:, slots : slots + 1] = count
-    copy = pltpu.make_async_copy(codes, listed, sem)
-    copy.start()
-
-    def block(l, carry):
-        rows = [spread(points, c * lines + l) for c in range(3)]
-        at = pl.ds(pl.multiple_of(l * FEATS, FEATS), FEATS)
-        line_feat[at, :] = line_block(rows).astype(BF16)
-        return carry
-
-    lax.fori_loop(0, lines, block, 0, unroll=4)
-    copy.wait()
+def build_lists(lines, slots, bits, first, listed, items_a, items_b, totals):
     step = 4
 
     def one(line, ends):
         def some(g, ends):
             end_a, end_b = ends
-            for e in range(step):
-                code = listed[line, g * step + e]
-                live = 1 + lax.shift_right_arithmetic(code, 31)
-                late = live & lax.shift_right_logical(code, bits - 1)
+            found = [listed[line, g * step + e] for e in range(step)]
+            live = [1 + lax.shift_right_arithmetic(code, 31) for code in found]
+            late = [n & lax.shift_right_logical(code, bits - 1) for n, code in zip(live, found)]
+            for code, n, m in zip(found, live, late):
                 items_a[end_a] = code
                 items_b[end_b] = code
-                end_a, end_b = end_a + (live - late), end_b + late
+                end_a, end_b = end_a + (n - m), end_b + m
             return end_a, end_b
 
         groups = lax.shift_right_logical(listed[line, slots] + (step - 1), 2)
@@ -195,26 +193,90 @@
     totals[1] = end_b
 
 
-def prepared(first, slots, bits, placed, counted, numbers, counts, points):
-    lines, depth = numbers.shape[0], points.shape[1]
+def line_features(lines, points, line_feat):
+    def block(l, carry):
+        rows = [spread(points, c * lines + l) for c in range(3)]
+        at = pl.ds(pl.multiple_of(l * FEATS, FEATS), FEATS)
+        line_feat[at, :] = line_block(rows).astype(BF16)
+        return carry
+
+    lax.fori_loop(0, lines, block, 0, unroll=4)
+
+
+def coded(first, bits, placed, number, count):
+    row = lax.broadcasted_iota(jnp.int32, number.shape, 0)
+    slot = lax.broadcasted_iota(jnp.int32, number.shape, 1)
+    code = lax.shift_left(row + first, jnp.full_like(row, bits)) + placed(number)
+    return jnp.where(slot < count, code, -1)
+
+
+def own_kernel(
+    keep, bits, placed, points, numbers, counts,
+    items_a, items_b, totals, line_feat, codes, listed, sem,
+):
+    planes, rows, slots = numbers.shape
+    slabs = lax.axis_size("slab")
+    lends = is_heavy(lax.axis_index("slab"), slabs)
+    for x in range(planes):
+        count = count_column(counts, x).astype(jnp.int32)
+        if x >= keep:
+            row = lax.broadcasted_iota(jnp.int32, count.shape, 0)
+            count = jnp.where(lends & (row >= 1), 0, count)
+        span = slice(x * rows, (x + 1) * rows)
+        codes[span, 0:slots] = coded(x * rows, bits, placed, numbers[x], count)
+        codes[span, slots : slots + 1] = count
+    copy = pltpu.make_async_copy(codes, listed, sem)
+    copy.start()
+    line_features(planes * rows, points, line_feat)
+    copy.wait()
+    build_lists(planes * rows, slots, bits, 0, listed, items_a, items_b, totals)
+
+
+def lent_kernel(
+    first, rows, slots, lent, bits, placed, units, bases, *refs
+):
+    gots, refs = refs[: len(units)], refs[len(units) :]
+    items_a, items_b, totals, line_feat, codes, listed, got, sem = refs
+    slab, slabs = lax.axis_index("slab"), lax.axis_size("slab")
+    value = gots[-1][pl.ds(bases[-1], 4 * lent), :]
+    for unit, base, ref in list(zip(units, bases, gots))[:-1]:
+        value = jnp.where(is_heavy(slab ^ unit, slabs), ref[pl.ds(base, 4 * lent), :], value)
+    got[...] = value
+    helps = jnp.logical_not(is_heavy(slab, slabs))
+    number = got[3 * lent :, 0:slots].astype(jnp.int32)
+    count = got[3 * lent :, slots : slots + 1].astype(jnp.int32)
+    line = lax.broadcasted_iota(jnp.int32, count.shape, 0)
+    count = jnp.where(helps & (lax.rem(line, rows) >= 1), count, 0)
+    codes[:, 0:slots] = coded(first, bits, placed, number, count)
+    codes[:, slots : slots + 1] = count
+    copy = pltpu.make_async_copy(codes, listed, sem)
+    copy.start()
+    line_features(lent, got, line_feat)
+    copy.wait()
+    build_lists(lent, slots, bits, first, listed, items_a, items_b, totals)
+
+
+def prepared(kernel, lines, slots, depth, scratch, *operands):
     length = lines * slots + 2 * UNROLL
     return pl.pallas_call(
-        functools.partial(prepare_kernel, first, slots, bits, placed, counted),
+        kernel,
         out_shape=(
             jax.ShapeDtypeStruct((length,), jnp.int32),
             jax.ShapeDtypeStruct((length,), jnp.int32),
             jax.ShapeDtypeStruct((2,), jnp.int32),
             jax.ShapeDtypeStruct((lines * FEATS, depth), BF16),
         ),
-        in_specs=[vmem()] * 3,
+        in_specs=[vmem()] * len(operands),
         out_specs=(smem(), smem(), smem(), vmem()),
         scratch_shapes=[
             pltpu.VMEM((lines, TILE), jnp.int32),
             pltpu.SMEM((lines, TILE), jnp.int32),
-            pltpu.SemaphoreType.DMA,
-        ],
+        ]
+        + scratch
+        + [pltpu.SemaphoreType.DMA],
+        compiler_params=limited(4),
         cost_estimate=pl.CostEstimate(flops=0, bytes_accessed=8_000_000, transcendentals=0),
-    )(numbers, counts, points)
+    )(*operands)
 
 
 def add_items(bits, half, lists, table, feats, line_feat, tile_feat, modes, acc, squares):
@@ -345,16 +407,16 @@
 
 
 def volume_kernel(
-    keep, has_lent, points, shift, back, row_halo, plane_halo,
-    out_shift, out_volume, out_change,
+    keep, share, points, shift, row_halo, plane_halo, *refs
 ):
+    *backs, out_shift, out_volume, out_change = refs
     planes, rows, depth = points.shape[1:]
     slab, ctrl = lax.axis_index("slab"), lax.axis_index("ctrl")
     slabs, ctrls = lax.axis_size("slab"), lax.axis_size("ctrl")
     row_id = lax.broadcasted_iota(jnp.int32, (rows, depth), 0)
     lane = lax.broadcasted_iota(jnp.int32, (rows, depth), 1)
     inside = (lane < depth - 1) & (row_id + ctrl * rows < ctrls * rows - 1)
-    if has_lent:
+    if backs:
         from_helper = (row_id >= 1) & is_heavy(slab, slabs)
     last_row = row_id == rows - 1
 
@@ -376,8 +438,9 @@
                     here = points[c, x]
                     if field == 1:
                         moved = shift[c, x]
-                        if has_lent and x >= keep:
-                            moved = jnp.where(from_helper, back[c, x - keep], moved)
+                        if backs and x >= keep:
+                            back = backs[(x - keep) // share]
+                            moved = jnp.where(from_helper, back[c, (x - keep) % share], moved)
                         out_shift[c, x] = moved
                         here = here + moved
                     edge = row_halo[field, c, x : x + 1, :]
@@ -441,25 +504,18 @@
     bits = max(1, (tiles - 1).bit_length())
     pressure = face_pressure.reshape(1, -1)
 
-    lend = slabs % 8 == 0 and slabs & (slabs - 1) == 0 and planes % 2 == 0
-    unit = slabs // 8 * 2
-    keep = planes // 2
-    lent = (planes - keep) * rows if lend else 0
+    unit = slabs // 8
+    share = (planes - 1) // 3
+    keep = planes - 3 * share
+    lend = slabs % 8 == 0 and slabs & (slabs - 1) == 0 and share > 0
+    units = (4 * unit, 2 * unit, unit) if lend else ()
+    spans = [tuple(range(keep + g * share, keep + (g + 1) * share)) for g in range(len(units))]
+    lent = share * rows if lend else 0
     heavy = [s for s in range(slabs) if is_heavy(s, slabs)]
-
-    if lend:
-        sent = pl.pallas_call(
-            functools.partial(lend_kernel, keep),
-            out_shape=jax.ShapeDtypeStruct((4 * lent, TILE), F32),
-            in_specs=[vmem()] * 3,
-            out_specs=vmem(),
-            cost_estimate=pl.CostEstimate(flops=0, bytes_accessed=2_000_000, transcendentals=0),
-        )(node_points, tile_list, tile_count)
 
     direct = columns % TILE == 0 and slabs & (slabs - 1) == 0 and ctrls & (ctrls - 1) == 0
     direct = direct and ctrls > 1 and (columns // TILE) & (columns // TILE - 1) == 0
     own_tiles = columns // TILE
-    got = None
     order = []
     bit = slabs // 2
     while bit:
@@ -481,51 +537,49 @@
             at = at + jnp.where((apart & flag) != 0, own_tiles << turn, 0)
         return at + (number & (own_tiles - 1))
 
-    plane_id = lax.broadcasted_iota(jnp.int32, (planes, rows), 0)
-    row_id = lax.broadcasted_iota(jnp.int32, (planes, rows), 1)
-    counts = tile_count
-    if lend:
-        lends = is_heavy(slab, slabs) & (plane_id >= keep) & (row_id >= 1)
-        counts = jnp.where(lends, 0, counts)
     flat_points = node_points.reshape(3 * own, depth)
     own_lists = prepared(
-        0, slots, bits, placed, lambda count: count,
-        tile_list.reshape(own, slots), counts.reshape(own, 1), flat_points,
+        functools.partial(own_kernel, keep if lend else planes, bits, placed),
+        own, slots, depth, [], flat_points, tile_list, tile_count,
     )
 
-    def borrowed(got):
-        def counted(count):
-            at = lax.axis_index("slab")
-            helper = is_heavy(at ^ unit, slabs) & jnp.logical_not(is_heavy(at, slabs))
-            line = lax.broadcasted_iota(jnp.int32, count.shape, 0)
-            return jnp.where(helper & (line % rows >= 1), count, 0)
-
-        listed = got[3 * lent :]
-        return prepared(
-            own, slots, bits, placed, counted, listed, listed[:, slots : slots + 1], got[: 3 * lent]
+    def borrowed(gots, bases):
+        kernel = functools.partial(
+            lent_kernel, own, rows, slots, lent, bits, placed, units, tuple(bases)
         )
-
+        return prepared(kernel, lent, slots, depth, [pltpu.VMEM((4 * lent, TILE), F32)], *gots)
+
+    gots, bases = [], []
     if direct:
-        early = pl.pallas_call(
-            pack_kernel,
-            out_shape=jax.ShapeDtypeStruct((own_tiles * ROWS, TILE), F32),
-            in_specs=[vmem()] * 5,
-            out_specs=vmem(),
-        )(pressure, face_area, face_center, control_points, control_modes)
-        own_ready, lent_ready = False, False
-        for slab_bit, ctrl_bit in order[:-1]:
+        size = own_tiles * ROWS
+        first, *sents = pl.pallas_call(
+            functools.partial(pack_kernel, spans),
+            out_shape=[
+                jax.ShapeDtypeStruct((rows_of, TILE), F32)
+                for rows_of in [size + 4 * lent] + [4 * lent] * (len(units) - 1)
+            ],
+            in_specs=[vmem()] * 8,
+            out_specs=[vmem()] * max(1, len(units)),
+            compiler_params=limited(56),
+        )(
+            pressure, face_area, face_center, control_points, control_modes,
+            node_points, tile_list, tile_count,
+        )
+        early = first[:size]
+        for turn, (slab_bit, ctrl_bit) in enumerate(order[:-1]):
             size = early.shape[0]
-            if got is not None and not own_ready:
+            if turn == 2:
                 early, own_lists = lax.optimization_barrier((early, own_lists))
-                own_ready = True
-            elif own_ready and not lent_ready:
+            if turn == 3 and lend:
                 early, lent_lists = lax.optimization_barrier((early, lent_lists))
-                lent_ready = True
-            if lend and slab_bit == unit:
-                reply = swapped(jnp.concatenate([early, sent], axis=0), slab_bit, ctrl_bit)
-                got = reply[size:]
+            if lend and slab_bit in units:
+                payload = jnp.concatenate([early, sents[len(gots) - 1]], axis=0) if gots else first
+                reply = swapped(payload, slab_bit, ctrl_bit)
+                gots.append(reply)
+                bases.append(size)
                 reply = reply[:size]
-                lent_lists = borrowed(got)
+                if len(gots) == len(units):
+                    lent_lists = borrowed(gots, bases)
             else:
                 reply = swapped(early, slab_bit, ctrl_bit)
             early = jnp.concatenate([early, reply], axis=0)
@@ -544,9 +598,15 @@
         spare = jnp.zeros((tiles, 3, 1, TILE), F32).at[0, 0, 0, :].set(loads[0])
         table = jnp.concatenate([whole, spare], axis=2).reshape(tiles * ROWS, TILE)
         early, late = table[: tiles // 2 * ROWS], table[tiles // 2 * ROWS :]
-
-    if lend and got is None:
-        lent_lists = borrowed(swapped(sent, unit, 0))
+        if lend:
+            sents = pl.pallas_call(
+                functools.partial(lend_kernel, spans),
+                out_shape=[jax.ShapeDtypeStruct((4 * lent, TILE), F32)] * len(units),
+                in_specs=[vmem()] * 3,
+                out_specs=[vmem()] * len(units),
+            )(node_points, tile_list, tile_count)
+            gots = [swapped(sent, bit, 0) for sent, bit in zip(sents, units)]
+            lent_lists = borrowed(gots, [0] * len(units))
     groups = [own_lists] + ([lent_lists] if lend else [])
     lines = own + lent
 
@@ -574,7 +634,7 @@
         in_specs=list_specs + [vmem()],
         out_specs=(vmem(), vmem()),
         scratch_shapes=scratch + squares,
-        compiler_params=pltpu.CompilerParams(vmem_limit_bytes=32 << 20),
+        compiler_params=limited(16),
         cost_estimate=pl.CostEstimate(flops=0, bytes_accessed=30_000_000, transcendentals=0),
     )(*early_items, *feats, early)
     outs = pl.pallas_call(
@@ -589,33 +649,35 @@
         in_specs=list_specs + [vmem()] * 7,
         out_specs=(vmem(),) * 5,
         scratch_shapes=scratch + [pltpu.VMEM(((lines + 1) * ROWS, depth), F32)] + squares,
-        compiler_params=pltpu.CompilerParams(vmem_limit_bytes=32 << 20),
+        compiler_params=limited(16),
     )(
         *late_items, *feats, late, partial, part_loads, flat_points,
         wide(motion), wide(inverse_mass), wide(jnp.array(GRAVITY, F32)),
     )
     shift, lent_shift, state, row_sent, plane_sent = outs
 
-    if lend:
-        back = lax.ppermute(lent_shift, "slab", [(h ^ unit, h) for h in heavy])
-        back = back.reshape(3, planes - keep, rows, depth)
-    else:
-        back = jnp.zeros((3, 1, rows, depth), F32)
+    backs = [
+        lax.ppermute(lent_shift, "slab", [(h ^ bit, h) for h in heavy]).reshape(
+            3, share, rows, depth
+        )
+        for bit in units
+    ]
     row_halo = shifted_back(row_sent, "ctrl").reshape(2, 3, planes, depth)
     plane_sent = plane_sent.reshape(2, 3, rows, depth)
     plane_halo = shifted_back(
         jnp.concatenate([plane_sent, row_halo[:, :, :1]], axis=2), "slab"
     )
     node_shift, volume, change = pl.pallas_call(
-        functools.partial(volume_kernel, keep, lend),
+        functools.partial(volume_kernel, keep, share),
         out_shape=(
             jax.ShapeDtypeStruct(node_points.shape, F32),
             jax.ShapeDtypeStruct(node_points.shape[1:], F32),
             jax.ShapeDtypeStruct(node_points.shape[1:], F32),
         ),
-        in_specs=[vmem()] * 5,
+        in_specs=[vmem()] * (4 + len(backs)),
         out_specs=(vmem(),) * 3,
-    )(node_points, shift.reshape(3, planes, rows, depth), back, row_halo, plane_halo)
+        compiler_params=limited(8),
+    )(node_points, shift.reshape(3, planes, rows, depth), row_halo, plane_halo, *backs)
     return node_shift, volume, change, state[0, : motion.shape[0]]
 
 

time: 71.6 us -> 61.9 us (0.86)
  waiting for transfers between devices: 26.4 us -> 12.7 us
  Pallas kernels: 23.6 us -> 28.6 us
  starting transfers between devices: 12.5 us -> 16.2 us
  local copies, waits for them, and re-layouts: 5.12 us -> 2.76 us
  other arithmetic: 2.38 us -> 0.05 us
    ppermute x2, waiting for transfers between devices: 20.4 us -> 4.56 us  [shifted_back(): lax.ppermute(value, axis, [(i, i - 1) for i in range(1, lax.axis_size(axi...]
    pallas_call x1, Pallas kernels: 5.75 us -> 10.6 us  [local(): pl.pallas_call(functools.partial(late_kernel, own, lent, parts, bits), ou...]
    ppermute x1 -> x3, starting transfers between devices: 0.66 us -> 4.92 us  [local(): lax.ppermute(lent_shift, 'slab', [(h ^ bit, h) for h in heavy])]
    pallas_call x1, Pallas kernels: 4.71 us -> 8.39 us  [local(): pl.pallas_call(functools.partial(early_kernel, parts, bits), out_shape=(j...]
    pallas_call x5 -> x4, Pallas kernels: 13.1 us -> 9.63 us  [the longest x2 6.99 us: prepared(): pl.pallas_call(kernel, out_shape=(jax.ShapeDtypeStruct((length,), jnp.int...]
    ppermute x5, waiting for transfers between devices: 5.94 us -> 8.16 us  [swapped(): return lax.ppermute(value, ('slab', 'ctrl'), pairs)]
    slice x3 -> x4, local copies, waits for them, and re-layouts: 1.91 us -> 0.79 us  [the longest x1 0.77 us: local(): early = first[:size]]
    concatenate x1 -> x2, other arithmetic: 0.85 us -> 0.02 us  [local(): jnp.concatenate([early, sents[len(gots) - 1]], axis=0)]
  transfers between devices with their start and end apart: 8 -> 10, of which waited for: 5 -> 5; matrix products, arithmetic and copies ran while one was open for 5% -> 2% of each run, Pallas kernels for 20% -> 20%
where the time goes in v3:
time: 61.9 us; the launch traced here: 61.2 us
  Pallas kernels  28.6 us (46%)
  starting transfers between devices  16.2 us (26%)
  waiting for transfers between devices  12.7 us (21%)
  local copies, waits for them, and re-layouts  2.76 us (4%)
  between operations  0.85 us (1%)
    pallas_call x1, Pallas kernels, local(): pl.pallas_call(functools.partial(late_kernel, own, lent, parts, bits), ou...  10.6 us
    ppermute x5, starting transfers between devices, swapped(): return lax.ppermute(value, ('slab', 'ctrl'), pairs)  8.74 us
    pallas_call x1, Pallas kernels, local(): pl.pallas_call(functools.partial(early_kernel, parts, bits), out_shape=(j...  8.39 us
    ppermute x5, waiting for transfers between devices, swapped(): return lax.ppermute(value, ('slab', 'ctrl'), pairs)  8.16 us
    pallas_call x2, Pallas kernels, prepared(): pl.pallas_call(kernel, out_shape=(jax.ShapeDtypeStruct((length,), jnp.int...  6.99 us
    ppermute x3, starting transfers between devices, local(): lax.ppermute(lent_shift, 'slab', [(h ^ bit, h) for h in heavy])  4.92 us
    ppermute x2, waiting for transfers between devices, shifted_back(): lax.ppermute(value, axis, [(i, i - 1) for i in range(1, lax.axis_size(axi...  4.56 us
    ppermute x2, starting transfers between devices, shifted_back(): lax.ppermute(value, axis, [(i, i - 1) for i in range(1, lax.axis_size(axi...  2.58 us
  transfers between devices with their start and end apart: 10, of which 5 were waited for; matrix products, arithmetic and copies ran while one was open for 2% of the time, Pallas kernels for 20%

profile of v3, /device:TPU:0, one launch (start us, length us, event | category | flops | bytes accessed | tf_op | source)
XLA Modules:
  0.0 61.2 jit_solution(1967168584014901009)
XLA Ops:
  0.6 1.8 %shard_map.138 = (f32[112,128]{1,0:T(8,128)}, f32[64,128]{1,0:T(8,128)}, f32[64,128]{1,0:T(8,128)}) custom-call(f32[1,4096]{1,0:T(1,128)} %bitcast.23, f32[3,4096]{1,0:T(4,128)} %area.1, f32[3,4096]{1,0:T(4,128)} %center.1, f32[3,256]{1,0:T(4,128)} %points.2, f32[18,256]{1,0:T(8,128)} %modes.1, f32[3,8,8,128]{3,2,1,0:T(8,128)} %points.3, ...), custom_call_target="tpu_custom_call" | custom-call | tf_op jit(solution)/shard_map/pallas_call | solution.py:555
  2.4 4.0 %collective-permute-start = (f32[112,128]{1,0:T(8,128)}, f32[112,128]{1,0:T(8,128)S(1)}, u32[]{:S(2)}, u32[]{:S(2)}) collective-permute-start(f32[112,128]{1,0:T(8,128)} %get-tuple-element.35), channel_id=1, source_target_pairs={{0,16},{1,17},{2,18},{3,19},{4,20},{5,21},{6,22},{7,23},{8,24},{9,... | collective-permute-start | bytes 172040 | tf_op jit(solution)/shard_map/ppermute | solution.py:41
  6.5 0.0 copy-start.4
  6.5 0.8 %slice.18 = f32[48,128]{1,0:T(8,128)S(1)} slice(f32[112,128]{1,0:T(8,128)} %get-tuple-element.35), slice={[0:48], [0:128]} | slice | bytes 49152 | tf_op jit(solution)/shard_map/slice | solution.py:568
  7.2 0.0 copy-start
  7.2 2.2 %collective-permute-done.refs_0_ = f32[112,128]{1,0:T(8,128)S(1)} collective-permute-done((f32[112,128]{1,0:T(8,128)}, f32[112,128]{1,0:T(8,128)S(1)}, u32[]{:S(2)}, u32[]{:S(2)}) %collective-permute-start) | collective-permute-done | bytes 57376 | tf_op jit(solution)/shard_map/ppermute | solution.py:41
  9.4 0.0 copy-done.4
  9.4 0.0 copy-start.1
  9.4 0.0 copy-start.2
  9.5 1.4 %collective-permute-start.1 = (f32[160,128]{1,0:T(8,128)S(1)}, f32[160,128]{1,0:T(8,128)S(1)}, u32[]{:S(2)}, u32[]{:S(2)}) collective-permute-start(f32[160,128]{1,0:T(8,128)S(1)} %pad_maximum_fusion.3), channel_id=1, source_target_pairs={{0,8},{1,9},{2,10},{3,11},{4,12},{5,13},{6,14},{7,15},{8,0},{9,1},... | collective-permute-start | bytes 245768 | tf_op jit(solution)/shard_map/ppermute | solution.py:41
  10.8 0.0 copy-done
  10.8 0.0 copy-done.1
  10.8 0.0 copy-done.2
  10.8 4.0 %shard_map.139 = (s32[1056]{0:T(1024)S(1)}, s32[1056]{0:T(1024)S(1)}, s32[2]{0:T(128)S(1)}, bf16[2048,128]{1,0:T(8,128)(2,1)S(1)}) custom-call(f32[192,128]{1,0:T(8,128)S(1)} %bitcast.14, s32[8,8,16]{2,1,0:T(8,128)S(1)} %copy-done.1, s32[8,8]{1,0:T(8,128)S(1)} %copy-done.2), custom_call_target="tpu_custom_call" | custom-call | bytes 8000000 | tf_op jit(solution)/shard_map/pallas_call | solution.py:261
  14.8 0.0 collective-permute-done.1.refs_1_
  14.9 0.0 copy-start.5
  14.9 0.7 %copy-done.5 = f32[64,128]{1,0:T(8,128)S(1)} copy-done((f32[64,128]{1,0:T(8,128)S(1)}, f32[64,128]{1,0:T(8,128)}, u32[]{:S(2)}) %copy-start.5) | copy-done | bytes 32792
  15.6 1.6 %collective-permute-start.2 = (f32[256,128]{1,0:T(8,128)S(1)}, f32[256,128]{1,0:T(8,128)S(1)}, u32[]{:S(2)}, u32[]{:S(2)}) collective-permute-start(f32[256,128]{1,0:T(8,128)S(1)} %pad_maximum_fusion.1), channel_id=1, source_target_pairs={{0,4},{1,5},{2,6},{3,7},{4,0},{5,1},{6,2},{7,3},{8,12},{9,13},{10,... | collective-permute-start | bytes 393224 | tf_op jit(solution)/shard_map/ppermute | solution.py:41
  17.2 3.5 %collective-permute-done.2.refs_2_ = f32[256,128]{1,0:T(8,128)S(1)} collective-permute-done((f32[256,128]{1,0:T(8,128)S(1)}, f32[256,128]{1,0:T(8,128)S(1)}, u32[]{:S(2)}, u32[]{:S(2)}) %collective-permute-start.2) | collective-permute-done | bytes 131104 | tf_op jit(solution)/shard_map/ppermute | solution.py:41
  20.7 3.0 %shard_map.140 = (s32[288]{0:T(512)S(1)}, s32[288]{0:T(512)S(1)}, s32[2]{0:T(128)S(1)}, bf16[512,128]{1,0:T(8,128)(2,1)S(1)}) custom-call(f32[112,128]{1,0:T(8,128)S(1)} %collective-permute-done.refs_0_, f32[160,128]{1,0:T(8,128)S(1)} %collective-permute-done.1.refs_1_, f32[256,128]{1,0:T(8,128)S(1)} %collective-permute-done.2.refs_2_), custom_call_target="tpu_custom_call" | custom-call | bytes 8000000 | tf_op jit(solution)/shard_map/pallas_call | solution.py:261
  23.7 0.1 collective-permute-start.3
  23.8 0.0 copy-start.6
  23.8 0.0 copy-start.7
  23.8 1.4 %collective-permute-done.3 = f32[384,128]{1,0:T(8,128)S(1)} collective-permute-done((f32[384,128]{1,0:T(8,128)S(1)}, f32[384,128]{1,0:T(8,128)S(1)}, u32[]{:S(2)}, u32[]{:S(2)}) %collective-permute-start.3) | collective-permute-done | bytes 196640 | tf_op jit(solution)/shard_map/ppermute | solution.py:41
  25.2 1.7 %collective-permute-start.4 = (f32[768,128]{1,0:T(8,128)S(1)}, f32[768,128]{1,0:T(8,128)S(1)}, u32[]{:S(2)}, u32[]{:S(2)}) collective-permute-start(f32[768,128]{1,0:T(8,128)S(1)} %constant_dynamic-update-slice_fusion.refs_6_), channel_id=1, source_target_pairs={{0,2},{1,3},{2,0},{3,1},{4,6},{5,7},{6,4},{7,5},{8,10},{9,11},{10,... | collective-permute-start | bytes 1179656 | tf_op jit(solution)/shard_map/ppermute | solution.py:41
  26.9 0.0 copy-done.6
  26.9 0.0 copy-done.7
  26.9 8.4 %shard_map.141 = (f32[1944,128]{1,0:T(8,128)S(1)}, f32[1,128]{1,0:T(1,128)S(1)}) custom-call(s32[1056]{0:T(1024)S(1)} %get-tuple-element.54.refs_0_, s32[2]{0:T(128)S(1)} %get-tuple-element.42.refs_1_, s32[288]{0:T(512)S(1)} %get-tuple-element.55.refs_2_, s32[2]{0:T(128)S(1)} %get-tuple-element.50.refs_3_, bf16[2048,128]{1,0:T(8,128)(2,1)S(1)} %get-tuple-element.51.refs_4_, ...), custom_call_target="tpu_custom_call" | custom-call | bytes 30000000 | tf_op jit(solution)/shard_map/pallas_call | solution.py:628
  35.3 1.1 %collective-permute-done.4.refs_6_ = f32[768,128]{1,0:T(8,128)S(1)} collective-permute-done((f32[768,128]{1,0:T(8,128)S(1)}, f32[768,128]{1,0:T(8,128)S(1)}, u32[]{:S(2)}, u32[]{:S(2)}) %collective-permute-start.4) | collective-permute-done | bytes 393248 | tf_op jit(solution)/shard_map/ppermute | solution.py:41
  36.5 0.0 copy-start.3
  36.5 0.7 %copy-done.3 = f32[1,128]{1,0:T(1,128)S(1)} copy-done((f32[1,128]{1,0:T(1,128)S(1)}, f32[1,128]{1,0:T(1,128)}, u32[]{:S(2)}) %copy-start.3) | copy-done | bytes 536
  37.1 10.6 %shard_map.142 = (f32[192,128]{1,0:T(8,128)S(1)}, f32[48,128]{1,0:T(8,128)S(1)}, f32[1,128]{1,0:T(1,128)S(1)}, f32[2,24,128]{2,1,0:T(8,128)S(1)}, f32[2,24,128]{2,1,0:T(8,128)S(1)}) custom-call(s32[1056]{0:T(1024)S(1)} %get-tuple-element.41.refs_0_, s32[2]{0:T(128)S(1)} %get-tuple-element.42.refs_1_, s32[288]{0:T(512)S(1)} %get-tuple-element.49.refs_2_, ...), custom_call_target="tpu_custom_call" | custom-call | tf_op jit(solution)/shard_map/pallas_call | solution.py:640
  47.7 1.3 %collective-permute-start.5 = (f32[2,24,128]{2,1,0:T(8,128)S(1)}, f32[2,24,128]{2,1,0:T(8,128)S(1)}, u32[]{:S(2)}, u32[]{:S(2)}) collective-permute-start(f32[2,24,128]{2,1,0:T(8,128)S(1)} %get-tuple-element.59), channel_id=1, source_target_pairs={{1,0},{2,1},{3,2},{5,4},{6,5},{7,6},{9,8},{10,9},{11,10},{13,12},{... | collective-permute-start | bytes 73736 | tf_op jit(solution)/shard_map/ppermute | solution.py:45
  49.0 3.6 %collective-permute-start.7 = (f32[48,128]{1,0:T(8,128)S(1)}, f32[48,128]{1,0:T(8,128)S(1)}, u32[]{:S(2)}, u32[]{:S(2)}) collective-permute-start(f32[48,128]{1,0:T(8,128)S(1)} %get-tuple-element.61), channel_id=1, source_target_pairs={{28,12},{0,16},{29,13},{1,17},{30,14},{2,18},{31,15},{3,19}} | collective-permute-start | bytes 73736 | tf_op jit(solution)/shard_map/ppermute | solution.py:660
  52.6 0.7 %collective-permute-start.8 = (f32[48,128]{1,0:T(8,128)S(1)}, f32[48,128]{1,0:T(8,128)S(1)}, u32[]{:S(2)}, u32[]{:S(2)}) collective-permute-start(f32[48,128]{1,0:T(8,128)S(1)} %get-tuple-element.61), channel_id=1, source_target_pairs={{4,12},{24,16},{5,13},{25,17},{6,14},{26,18},{7,15},{27,19}} | collective-permute-start | bytes 73736 | tf_op jit(solution)/shard_map/ppermute | solution.py:660
  53.2 0.7 %collective-permute-start.9 = (f32[48,128]{1,0:T(8,128)S(1)}, f32[48,128]{1,0:T(8,128)S(1)}, u32[]{:S(2)}, u32[]{:S(2)}) collective-permute-start(f32[48,128]{1,0:T(8,128)S(1)} %get-tuple-element.61), channel_id=1, source_target_pairs={{8,12},{20,16},{9,13},{21,17},{10,14},{22,18},{11,15},{23,19}} | collective-permute-start | bytes 73736 | tf_op jit(solution)/shard_map/ppermute | solution.py:660
  53.9 0.0 collective-permute-done.5
  54.0 1.3 %collective-permute-start.6 = (f32[2,3,9,128]{3,2,1,0:T(8,128)S(1)}, f32[2,3,9,128]{3,2,1,0:T(8,128)S(1)}, u32[]{:S(2)}, u32[]{:S(2)}) collective-permute-start(f32[2,3,9,128]{3,2,1,0:T(8,128)S(1)} %pad_maximum_fusion.4), channel_id=1, source_target_pairs={{4,0},{8,4},{12,8},{16,12},{20,16},{24,20},{28,24},{5,1},{9,5},{13... | collective-permute-start | bytes 82952 | tf_op jit(solution)/shard_map/ppermute | solution.py:45
  55.3 0.5 slice_bitcast_fusion
  55.8 0.0 collective-permute-done.7
  55.8 0.0 collective-permute-done.8
  55.8 0.0 collective-permute-done.9
  55.8 4.6 %collective-permute-done.6.plane_halo = f32[2,3,9,128]{3,2,1,0:T(8,128)S(1)} collective-permute-done((f32[2,3,9,128]{3,2,1,0:T(8,128)S(1)}, f32[2,3,9,128]{3,2,1,0:T(8,128)S(1)}, u32[]{:S(2)}, u32[]{:S(2)}) %collective-permute-start.6) | collective-permute-done | bytes 27680 | tf_op jit(solution)/shard_map/ppermute | solution.py:45
  60.3 0.9 %shard_map.143 = (f32[3,8,8,128]{3,2,1,0:T(8,128)}, f32[8,8,128]{2,1,0:T(8,128)}, f32[8,8,128]{2,1,0:T(8,128)}) custom-call(f32[3,8,8,128]{3,2,1,0:T(8,128)S(1)} %copy-done, f32[3,8,8,128]{3,2,1,0:T(8,128)S(1)} %bitcast.16, f32[2,3,8,128]{3,2,1,0:T(8,128)S(1)} %bitcast.18, f32[2,3,9,128]{3,2,1,0:T(8,128)S(1)} %collective-permute-done.6.plane_halo, ...), custom_call_target="tpu_custom_call" | custom-call | tf_op jit(solution)/shard_map/pallas_call | solution.py:670
  (12 shorter events, 0.1 us)
Async XLA Ops:
  2.4 7.0 %collective-permute-start = (f32[112,128]{1,0:T(8,128)}, f32[112,128]{1,0:T(8,128)S(1)}, u32[]{:S(2)}, u32[]{:S(2)}) collective-permute-start(f32[112,128]{1,0:T(8,128)} %get-tuple-element.35), channel_id=1, source_target_pairs={{0,16},{1,17},{2,18},{3,19},{4,20},{5,21},{6,22},{7,23},{8,24},{9,... | collective-permute-start | bytes 172040 | tf_op jit(solution)/shard_map/ppermute | solution.py:41
  6.5 3.0 %copy-start.4 = (f32[64,128]{1,0:T(8,128)S(1)}, f32[64,128]{1,0:T(8,128)}, u32[]{:S(2)}) copy-start(f32[64,128]{1,0:T(8,128)} %get-tuple-element.36) | copy-start | bytes 98308
  7.2 3.6 %copy-start = (f32[3,8,8,128]{3,2,1,0:T(8,128)S(1)}, f32[3,8,8,128]{3,2,1,0:T(8,128)}, u32[]{:S(2)}) copy-start(f32[3,8,8,128]{3,2,1,0:T(8,128)} %points.3) | copy-start | bytes 294916
  9.4 1.4 %copy-start.1 = (s32[8,8,16]{2,1,0:T(8,128)S(1)}, s32[8,8,16]{2,1,0:T(8,128)}, u32[]{:S(2)}) copy-start(s32[8,8,16]{2,1,0:T(8,128)} %numbers.3) | copy-start | bytes 12292
  9.4 1.4 %copy-start.2 = (s32[8,8]{1,0:T(8,128)S(1)}, s32[8,8]{1,0:T(8,128)}, u32[]{:S(2)}) copy-start(s32[8,8]{1,0:T(8,128)} %counts.3) | copy-start | bytes 772
  9.5 5.4 %collective-permute-start.1 = (f32[160,128]{1,0:T(8,128)S(1)}, f32[160,128]{1,0:T(8,128)S(1)}, u32[]{:S(2)}, u32[]{:S(2)}) collective-permute-start(f32[160,128]{1,0:T(8,128)S(1)} %pad_maximum_fusion.3), channel_id=1, source_target_pairs={{0,8},{1,9},{2,10},{3,11},{4,12},{5,13},{6,14},{7,15},{8,0},{9,1},... | collective-permute-start | bytes 245768 | tf_op jit(solution)/shard_map/ppermute | solution.py:41
  14.9 0.8 %copy-start.5 = (f32[64,128]{1,0:T(8,128)S(1)}, f32[64,128]{1,0:T(8,128)}, u32[]{:S(2)}) copy-start(f32[64,128]{1,0:T(8,128)} %get-tuple-element.44) | copy-start | bytes 98308
  15.6 5.0 %collective-permute-start.2 = (f32[256,128]{1,0:T(8,128)S(1)}, f32[256,128]{1,0:T(8,128)S(1)}, u32[]{:S(2)}, u32[]{:S(2)}) collective-permute-start(f32[256,128]{1,0:T(8,128)S(1)} %pad_maximum_fusion.1), channel_id=1, source_target_pairs={{0,4},{1,5},{2,6},{3,7},{4,0},{5,1},{6,2},{7,3},{8,12},{9,13},{10,... | collective-permute-start | bytes 393224 | tf_op jit(solution)/shard_map/ppermute | solution.py:41
  23.7 1.5 %collective-permute-start.3 = (f32[384,128]{1,0:T(8,128)S(1)}, f32[384,128]{1,0:T(8,128)S(1)}, u32[]{:S(2)}, u32[]{:S(2)}) collective-permute-start(f32[384,128]{1,0:T(8,128)S(1)} %pad_maximum_fusion), channel_id=1, source_target_pairs={{0,1},{1,0},{2,3},{3,2},{4,5},{5,4},{6,7},{7,6},{8,9},{9,8},{10,11... | collective-permute-start | bytes 589832 | tf_op jit(solution)/shard_map/ppermute | solution.py:41
  23.8 3.1 %copy-start.6 = (f32[6]{0:T(128)S(1)}, f32[6]{0:T(128)}, u32[]{:S(2)}) copy-start(f32[6]{0:T(128)} %param.15) | copy-start | bytes 76
  23.8 3.1 %copy-start.7 = (f32[6]{0:T(128)S(1)}, f32[6]{0:T(128)}, u32[]{:S(2)}) copy-start(f32[6]{0:T(128)} %param.14) | copy-start | bytes 76
  25.2 11.2 %collective-permute-start.4 = (f32[768,128]{1,0:T(8,128)S(1)}, f32[768,128]{1,0:T(8,128)S(1)}, u32[]{:S(2)}, u32[]{:S(2)}) collective-permute-start(f32[768,128]{1,0:T(8,128)S(1)} %constant_dynamic-update-slice_fusion.refs_6_), channel_id=1, source_target_pairs={{0,2},{1,3},{2,0},{3,1},{4,6},{5,7},{6,4},{7,5},{8,10},{9,11},{10,... | collective-permute-start | bytes 1179656 | tf_op jit(solution)/shard_map/ppermute | solution.py:41
  36.5 0.7 %copy-start.3 = (f32[1,128]{1,0:T(1,128)S(1)}, f32[1,128]{1,0:T(1,128)}, u32[]{:S(2)}) copy-start(f32[1,128]{1,0:T(1,128)} %constant.13.refs_12_) | copy-start | bytes 1540
  47.7 6.2 %collective-permute-start.5 = (f32[2,24,128]{2,1,0:T(8,128)S(1)}, f32[2,24,128]{2,1,0:T(8,128)S(1)}, u32[]{:S(2)}, u32[]{:S(2)}) collective-permute-start(f32[2,24,128]{2,1,0:T(8,128)S(1)} %get-tuple-element.59), channel_id=1, source_target_pairs={{1,0},{2,1},{3,2},{5,4},{6,5},{7,6},{9,8},{10,9},{11,10},{13,12},{... | collective-permute-start | bytes 73736 | tf_op jit(solution)/shard_map/ppermute | solution.py:45
  49.0 6.8 %collective-permute-start.7 = (f32[48,128]{1,0:T(8,128)S(1)}, f32[48,128]{1,0:T(8,128)S(1)}, u32[]{:S(2)}, u32[]{:S(2)}) collective-permute-start(f32[48,128]{1,0:T(8,128)S(1)} %get-tuple-element.61), channel_id=1, source_target_pairs={{28,12},{0,16},{29,13},{1,17},{30,14},{2,18},{31,15},{3,19}} | collective-permute-start | bytes 73736 | tf_op jit(solution)/shard_map/ppermute | solution.py:660
  52.6 3.2 %collective-permute-start.8 = (f32[48,128]{1,0:T(8,128)S(1)}, f32[48,128]{1,0:T(8,128)S(1)}, u32[]{:S(2)}, u32[]{:S(2)}) collective-permute-start(f32[48,128]{1,0:T(8,128)S(1)} %get-tuple-element.61), channel_id=1, source_target_pairs={{4,12},{24,16},{5,13},{25,17},{6,14},{26,18},{7,15},{27,19}} | collective-permute-start | bytes 73736 | tf_op jit(solution)/shard_map/ppermute | solution.py:660
  53.2 2.5 %collective-permute-start.9 = (f32[48,128]{1,0:T(8,128)S(1)}, f32[48,128]{1,0:T(8,128)S(1)}, u32[]{:S(2)}, u32[]{:S(2)}) collective-permute-start(f32[48,128]{1,0:T(8,128)S(1)} %get-tuple-element.61), channel_id=1, source_target_pairs={{8,12},{20,16},{9,13},{21,17},{10,14},{22,18},{11,15},{23,19}} | collective-permute-start | bytes 73736 | tf_op jit(solution)/shard_map/ppermute | solution.py:660
  54.0 6.4 %collective-permute-start.6 = (f32[2,3,9,128]{3,2,1,0:T(8,128)S(1)}, f32[2,3,9,128]{3,2,1,0:T(8,128)S(1)}, u32[]{:S(2)}, u32[]{:S(2)}) collective-permute-start(f32[2,3,9,128]{3,2,1,0:T(8,128)S(1)} %pad_maximum_fusion.4), channel_id=1, source_target_pairs={{4,0},{8,4},{12,8},{16,12},{20,16},{24,20},{28,24},{5,1},{9,5},{13... | collective-permute-start | bytes 82952 | tf_op jit(solution)/shard_map/ppermute | solution.py:45

commit v4 on v3

--- a/solution.py
+++ b/solution.py
@@ -88,22 +88,38 @@
     for i, x in enumerate(planes):
         at = base + i * rows
         for c in range(3):
-            out[at + c * lent : at + c * lent + rows, :] = nodes[c, x]
+            first = (c * counts.shape[0] + x) * rows
+            out[at + c * lent : at + c * lent + rows, :] = nodes[first : first + rows, :]
         at = at + 3 * lent
         out[at : at + rows, :] = jnp.where(wide == slots, count_column(counts, x), 0.0)
         out[at : at + rows, 0:slots] = numbers[x].astype(F32)
 
 
-def pack_kernel(spans, pressure, area, center, points, modes, nodes, numbers, counts, out, *lents):
+def pack_corner(nodes, numbers, counts, out):
+    slots = numbers.shape[2]
+    lane = lax.broadcasted_iota(jnp.int32, (1, out.shape[1]), 1)
+    out[...] = jnp.zeros(out.shape, F32)
+    for c in range(3):
+        first = c * counts.shape[0] * counts.shape[1]
+        out[c : c + 1, :] = nodes[first : first + 1, :]
+    out[3:4, :] = jnp.where(lane == slots, count_column(counts, 0)[0:1], 0.0)
+    out[3:4, 0:slots] = numbers[0, 0:1, :].astype(F32)
+
+
+def pack_kernel(
+    spans, pressure, area, center, points, modes, nodes, numbers, counts, corner, out, *lents
+):
     row = load_rows(pressure[...], area[...], center[...])
     pack_table(row, points, modes, out)
+    pack_corner(nodes, numbers, counts, corner)
     if spans:
         pack_lent(spans[0], points.shape[1] // TILE * ROWS, nodes, numbers, counts, out)
     for span, lent in zip(spans[1:], lents):
         pack_lent(span, 0, nodes, numbers, counts, lent)
 
 
-def lend_kernel(spans, nodes, numbers, counts, *outs):
+def lend_kernel(spans, nodes, numbers, counts, corner, *outs):
+    pack_corner(nodes, numbers, counts, corner)
     for span, out in zip(spans, outs):
         pack_lent(span, 0, nodes, numbers, counts, out)
 
@@ -166,31 +182,37 @@
     )
 
 
-def build_lists(lines, slots, bits, first, listed, items_a, items_b, totals):
-    step = 4
+def build_lists(lines, slots, bits, first, listed, items):
+    few = min(4, slots)
+    middle = lines * slots + 2 * UNROLL
+
+    def take(line, low, high, ends):
+        end_a, end_b = ends
+        found = [listed[line, e] for e in range(low, high)]
+        live = [1 + lax.shift_right_arithmetic(code, 31) for code in found]
+        late = [n & lax.shift_right_logical(code, bits - 1) for n, code in zip(live, found)]
+        for code, n, m in zip(found, live, late):
+            items[end_a] = code
+            items[end_b] = code
+            end_a, end_b = end_a + (n - m), end_b + m
+        return end_a, end_b
 
     def one(line, ends):
-        def some(g, ends):
-            end_a, end_b = ends
-            found = [listed[line, g * step + e] for e in range(step)]
-            live = [1 + lax.shift_right_arithmetic(code, 31) for code in found]
-            late = [n & lax.shift_right_logical(code, bits - 1) for n, code in zip(live, found)]
-            for code, n, m in zip(found, live, late):
-                items_a[end_a] = code
-                items_b[end_b] = code
-                end_a, end_b = end_a + (n - m), end_b + m
-            return end_a, end_b
-
-        groups = lax.shift_right_logical(listed[line, slots] + (step - 1), 2)
-        return lax.fori_loop(0, groups, some, ends)
-
-    end_a, end_b = lax.fori_loop(0, lines, one, (jnp.int32(0), jnp.int32(0)))
+        ends = take(line, 0, few, ends)
+        return lax.cond(
+            listed[line, slots] > few,
+            lambda ends: take(line, few, slots, ends),
+            lambda ends: ends,
+            ends,
+        )
+
+    end_a, end_b = lax.fori_loop(0, lines, one, (jnp.int32(0), jnp.int32(middle)))
     dummy = (first + lines) << bits
     for e in range(2 * UNROLL):
-        items_a[end_a + e] = dummy
-        items_b[end_b + e] = dummy
-    totals[0] = end_a
-    totals[1] = end_b
+        items[end_a + e] = dummy
+        items[end_b + e] = dummy
+    items[2 * middle] = end_a
+    items[2 * middle + 1] = end_b - middle
 
 
 def line_features(lines, points, line_feat):
@@ -211,10 +233,11 @@
 
 
 def own_kernel(
-    keep, bits, placed, points, numbers, counts,
-    items_a, items_b, totals, line_feat, codes, listed, sem,
+    keep, bits, placed, span, points, numbers, counts,
+    items, line_feat, sent, codes, listed, sem,
 ):
     planes, rows, slots = numbers.shape
+    pack_lent(span, 0, points, numbers, counts, sent)
     slabs = lax.axis_size("slab")
     lends = is_heavy(lax.axis_index("slab"), slabs)
     for x in range(planes):
@@ -229,45 +252,46 @@
     copy.start()
     line_features(planes * rows, points, line_feat)
     copy.wait()
-    build_lists(planes * rows, slots, bits, 0, listed, items_a, items_b, totals)
+    build_lists(planes * rows, slots, bits, 0, listed, items)
 
 
 def lent_kernel(
     first, rows, slots, lent, bits, placed, units, bases, *refs
 ):
     gots, refs = refs[: len(units)], refs[len(units) :]
-    items_a, items_b, totals, line_feat, codes, listed, got, sem = refs
+    corner, items, line_feat, codes, listed, got, sem = refs
     slab, slabs = lax.axis_index("slab"), lax.axis_size("slab")
     value = gots[-1][pl.ds(bases[-1], 4 * lent), :]
     for unit, base, ref in list(zip(units, bases, gots))[:-1]:
         value = jnp.where(is_heavy(slab ^ unit, slabs), ref[pl.ds(base, 4 * lent), :], value)
     got[...] = value
+    for c in range(4):
+        got[c * lent : c * lent + 1, :] = corner[c : c + 1, :]
     helps = jnp.logical_not(is_heavy(slab, slabs))
     number = got[3 * lent :, 0:slots].astype(jnp.int32)
     count = got[3 * lent :, slots : slots + 1].astype(jnp.int32)
     line = lax.broadcasted_iota(jnp.int32, count.shape, 0)
-    count = jnp.where(helps & (lax.rem(line, rows) >= 1), count, 0)
+    count = jnp.where((helps & (lax.rem(line, rows) >= 1)) | (line == 0), count, 0)
     codes[:, 0:slots] = coded(first, bits, placed, number, count)
     codes[:, slots : slots + 1] = count
     copy = pltpu.make_async_copy(codes, listed, sem)
     copy.start()
     line_features(lent, got, line_feat)
     copy.wait()
-    build_lists(lent, slots, bits, first, listed, items_a, items_b, totals)
-
-
-def prepared(kernel, lines, slots, depth, scratch, *operands):
+    build_lists(lent, slots, bits, first, listed, items)
+
+
+def prepared(kernel, lines, slots, depth, more, scratch, *operands):
     length = lines * slots + 2 * UNROLL
     return pl.pallas_call(
         kernel,
         out_shape=(
-            jax.ShapeDtypeStruct((length,), jnp.int32),
-            jax.ShapeDtypeStruct((length,), jnp.int32),
-            jax.ShapeDtypeStruct((2,), jnp.int32),
+            jax.ShapeDtypeStruct((2 * length + 2,), jnp.int32),
             jax.ShapeDtypeStruct((lines * FEATS, depth), BF16),
+            *more,
         ),
         in_specs=[vmem()] * len(operands),
-        out_specs=(smem(), smem(), smem(), vmem()),
+        out_specs=(smem(), vmem()) + (vmem(),) * len(more),
         scratch_shapes=[
             pltpu.VMEM((lines, TILE), jnp.int32),
             pltpu.SMEM((lines, TILE), jnp.int32),
@@ -286,14 +310,16 @@
         line_feat[at : at + feat.shape[0], :] = feat[...]
         at += feat.shape[0]
     line_feat[at:, :] = jnp.zeros((line_feat.shape[0] - at, line_feat.shape[1]), BF16)
-    first = lists[0][1][half]
-    count = sum(total[half] for _, total in lists)
+    middles = [items.shape[0] // 2 - 1 for items in lists]
+    starts = [middle * half for middle in middles]
+    first = lists[0][2 * middles[0] + half]
+    count = sum(items[2 * middle + half] for items, middle in zip(lists, middles))
 
     def build(t, carry):
         base = pl.multiple_of(t * ROWS, 8)
         rows = [spread(table, base + 8 * c) for c in range(3)]
         block = tile_block(rows)
-        tile_feat[pl.ds(pl.multiple_of(t * TILE, TILE), TILE), :] = block.T.astype(BF16)
+        tile_feat[pl.ds(pl.multiple_of(t * TILE, TILE), TILE), :] = block.astype(BF16).T
         value = 4.0 * table[pl.ds(base, ROWS), :]
         high = value.astype(BF16)
         low = (value - high.astype(F32)).astype(BF16)
@@ -305,9 +331,9 @@
     mask = tiles - 1
 
     def unpack(at):
-        code = lists[0][0][jnp.minimum(at, first)]
-        if len(lists) > 1:
-            code = jnp.where(at < first, code, lists[1][0][jnp.maximum(at - first, 0)])
+        code = lists[0][starts[0] + jnp.minimum(at, first)]
+        other = lists[1][starts[1] + jnp.maximum(at - first, 0)]
+        code = jnp.where(at < first, code, other)
         return lax.shift_right_logical(code, bits), code & mask
 
     def distances(u, at):
@@ -354,22 +380,24 @@
 
 
 def early_kernel(parts, bits, *refs):
-    lists = [(refs[i], refs[i + 1]) for i in range(0, 2 * parts, 2)]
-    feats = refs[2 * parts : 3 * parts]
-    table, acc, loads, line_feat, tile_feat, modes, *squares = refs[3 * parts :]
+    lists, feats = refs[:parts], refs[parts : 2 * parts]
+    table, acc, loads, line_feat, tile_feat, modes, *squares = refs[2 * parts :]
     acc[...] = jnp.zeros(acc.shape, F32)
     loads[...] = load_sum(table)
     add_items(bits, 0, lists, table, feats, line_feat, tile_feat, modes, acc, squares)
 
 
 def late_kernel(own, lent, parts, bits, *refs):
-    lists = [(refs[i], refs[i + 1]) for i in range(0, 2 * parts, 2)]
-    feats = refs[2 * parts : 3 * parts]
-    table, early, loads, points, motion, inverse, gravity, *rest = refs[3 * parts :]
+    lists, feats = refs[:parts], refs[parts : 2 * parts]
+    table, early, loads, points, corner, motion, inverse, *rest = refs[2 * parts :]
     out_own, out_extra, out_state, out_row, out_plane, *rest = rest
     line_feat, tile_feat, modes, acc, *squares = rest
     total = loads[...] + load_sum(table)
-    acceleration = inverse[...] * total + gravity[...]
+    lane = lax.broadcasted_iota(jnp.int32, (1, 128), 1)
+    gravity = jnp.zeros((1, 128), F32)
+    for k, pull in enumerate(GRAVITY):
+        gravity = jnp.where(lane == k, pull, gravity)
+    acceleration = inverse[...] * total + gravity
     out_state[...] = motion[...] + TIME_STEP * acceleration
     step = TIME_STEP * motion[...] + 0.5 * TIME_STEP * TIME_STEP * acceleration
     row = lax.broadcasted_iota(jnp.int32, (8, 128), 0)
@@ -391,10 +419,9 @@
         lax.fori_loop(0, count, one, 0, unroll=4)
 
     finish(own, 0, out_own)
-    if lent:
-        finish(lent, own, out_extra)
+    finish(lent, own, out_extra)
     rows = out_row.shape[1] // 3
-    wide = out_plane.shape[1] // 3
+    wide = own // rows
     for c in range(3):
         old = points[c * own : c * own + wide, :]
         out_plane[0, c * wide : (c + 1) * wide, :] = old
@@ -404,12 +431,17 @@
         out_row[1, c * rows : (c + 1) * rows, :] = (
             old + out_own[pl.ds(c * own, rows, stride=wide), :]
         )
+    out_plane[0, 3 * wide :, :] = corner[...]
+    out_plane[1, 3 * wide :, :] = corner[...]
+    for c in range(3):
+        at = slice(3 * wide + c, 3 * wide + c + 1)
+        out_plane[1, at, :] = corner[c : c + 1, :] + out_extra[c * lent : c * lent + 1, :]
 
 
 def volume_kernel(
-    keep, share, points, shift, row_halo, plane_halo, *refs
+    keep, share, points, shift, *refs
 ):
-    *backs, out_shift, out_volume, out_change = refs
+    *backs, plane_halo, row_halo, out_shift, out_volume, out_change = refs
     planes, rows, depth = points.shape[1:]
     slab, ctrl = lax.axis_index("slab"), lax.axis_index("ctrl")
     slabs, ctrls = lax.axis_size("slab"), lax.axis_size("ctrl")
@@ -432,8 +464,8 @@
             parts = []
             for c in range(3):
                 if x == planes:
-                    here = plane_halo[field, c, 0:rows, :]
-                    edge = plane_halo[field, c, rows : rows + 1, :]
+                    here = plane_halo[field, c * rows : (c + 1) * rows, :]
+                    edge = plane_halo[field, 3 * rows + c : 3 * rows + c + 1, :]
                 else:
                     here = points[c, x]
                     if field == 1:
@@ -508,6 +540,7 @@
     share = (planes - 1) // 3
     keep = planes - 3 * share
     lend = slabs % 8 == 0 and slabs & (slabs - 1) == 0 and share > 0
+    assert lend, (slabs, planes)
     units = (4 * unit, 2 * unit, unit) if lend else ()
     spans = [tuple(range(keep + g * share, keep + (g + 1) * share)) for g in range(len(units))]
     lent = share * rows if lend else 0
@@ -538,39 +571,45 @@
         return at + (number & (own_tiles - 1))
 
     flat_points = node_points.reshape(3 * own, depth)
-    own_lists = prepared(
-        functools.partial(own_kernel, keep if lend else planes, bits, placed),
-        own, slots, depth, [], flat_points, tile_list, tile_count,
+    *own_lists, last_sent = prepared(
+        functools.partial(own_kernel, keep, bits, placed, spans[-1]),
+        own, slots, depth, [jax.ShapeDtypeStruct((4 * lent, TILE), F32)], [],
+        flat_points, tile_list, tile_count,
     )
 
     def borrowed(gots, bases):
         kernel = functools.partial(
             lent_kernel, own, rows, slots, lent, bits, placed, units, tuple(bases)
         )
-        return prepared(kernel, lent, slots, depth, [pltpu.VMEM((4 * lent, TILE), F32)], *gots)
+        scratch = [pltpu.VMEM((4 * lent, TILE), F32)]
+        return prepared(kernel, lent, slots, depth, [], scratch, *gots, corner)
 
     gots, bases = [], []
     if direct:
         size = own_tiles * ROWS
-        first, *sents = pl.pallas_call(
-            functools.partial(pack_kernel, spans),
+        corner, first, *sents = pl.pallas_call(
+            functools.partial(pack_kernel, spans[:-1]),
             out_shape=[
                 jax.ShapeDtypeStruct((rows_of, TILE), F32)
-                for rows_of in [size + 4 * lent] + [4 * lent] * (len(units) - 1)
+                for rows_of in [8, size + 4 * lent] + [4 * lent] * (len(units) - 2)
             ],
             in_specs=[vmem()] * 8,
-            out_specs=[vmem()] * max(1, len(units)),
+            out_specs=[vmem()] * len(units),
             compiler_params=limited(56),
         )(
             pressure, face_area, face_center, control_points, control_modes,
-            node_points, tile_list, tile_count,
+            flat_points, tile_list, tile_count,
         )
+        sents.append(last_sent)
         early = first[:size]
+        corner = shifted_back(corner, "ctrl")
         for turn, (slab_bit, ctrl_bit) in enumerate(order[:-1]):
             size = early.shape[0]
             if turn == 2:
-                early, own_lists = lax.optimization_barrier((early, own_lists))
-            if turn == 3 and lend:
+                early, own_lists, sents[-1] = lax.optimization_barrier(
+                    (early, own_lists, sents[-1])
+                )
+            if turn == 3:
                 early, lent_lists = lax.optimization_barrier((early, lent_lists))
             if lend and slab_bit in units:
                 payload = jnp.concatenate([early, sents[len(gots) - 1]], axis=0) if gots else first
@@ -598,16 +637,17 @@
         spare = jnp.zeros((tiles, 3, 1, TILE), F32).at[0, 0, 0, :].set(loads[0])
         table = jnp.concatenate([whole, spare], axis=2).reshape(tiles * ROWS, TILE)
         early, late = table[: tiles // 2 * ROWS], table[tiles // 2 * ROWS :]
-        if lend:
-            sents = pl.pallas_call(
-                functools.partial(lend_kernel, spans),
-                out_shape=[jax.ShapeDtypeStruct((4 * lent, TILE), F32)] * len(units),
-                in_specs=[vmem()] * 3,
-                out_specs=[vmem()] * len(units),
-            )(node_points, tile_list, tile_count)
-            gots = [swapped(sent, bit, 0) for sent, bit in zip(sents, units)]
-            lent_lists = borrowed(gots, [0] * len(units))
-    groups = [own_lists] + ([lent_lists] if lend else [])
+        corner, *sents = pl.pallas_call(
+            functools.partial(lend_kernel, spans),
+            out_shape=[jax.ShapeDtypeStruct((8, TILE), F32)]
+            + [jax.ShapeDtypeStruct((4 * lent, TILE), F32)] * len(units),
+            in_specs=[vmem()] * 3,
+            out_specs=[vmem()] * (1 + len(units)),
+        )(flat_points, tile_list, tile_count)
+        corner = shifted_back(corner, "ctrl")
+        gots = [swapped(sent, bit, 0) for sent, bit in zip(sents, units)]
+        lent_lists = borrowed(gots, [0] * len(units))
+    groups = [own_lists, lent_lists]
     lines = own + lent
 
     def wide(value):
@@ -615,10 +655,9 @@
 
     half = tiles // 2
     parts = len(groups)
-    early_items = [ref for group in groups for ref in (group[0], group[2])]
-    late_items = [ref for group in groups for ref in (group[1], group[2])]
-    feats = [group[3] for group in groups]
-    list_specs = [smem()] * (2 * parts) + [vmem()] * parts
+    lists = [group[0] for group in groups]
+    feats = [group[1] for group in groups]
+    list_specs = [smem()] * parts + [vmem()] * parts
     scratch = [
         pltpu.VMEM(((lines + 1) * FEATS, depth), BF16),
         pltpu.VMEM((half * TILE, FEATS), BF16),
@@ -636,7 +675,7 @@
         scratch_shapes=scratch + squares,
         compiler_params=limited(16),
         cost_estimate=pl.CostEstimate(flops=0, bytes_accessed=30_000_000, transcendentals=0),
-    )(*early_items, *feats, early)
+    )(*lists, *feats, early)
     outs = pl.pallas_call(
         functools.partial(late_kernel, own, lent, parts, bits),
         out_shape=(
@@ -644,15 +683,15 @@
             jax.ShapeDtypeStruct((3 * max(lent, 8), depth), F32),
             jax.ShapeDtypeStruct((1, TILE), F32),
             jax.ShapeDtypeStruct((2, 3 * planes, depth), F32),
-            jax.ShapeDtypeStruct((2, 3 * rows, depth), F32),
+            jax.ShapeDtypeStruct((2, 3 * rows + 8, depth), F32),
         ),
         in_specs=list_specs + [vmem()] * 7,
         out_specs=(vmem(),) * 5,
         scratch_shapes=scratch + [pltpu.VMEM(((lines + 1) * ROWS, depth), F32)] + squares,
         compiler_params=limited(16),
     )(
-        *late_items, *feats, late, partial, part_loads, flat_points,
-        wide(motion), wide(inverse_mass), wide(jnp.array(GRAVITY, F32)),
+        *lists, *feats, late, partial, part_loads, flat_points, corner,
+        wide(motion), wide(inverse_mass),
     )
     shift, lent_shift, state, row_sent, plane_sent = outs
 
@@ -662,11 +701,8 @@
         )
         for bit in units
     ]
+    plane_halo = shifted_back(plane_sent, "slab")
     row_halo = shifted_back(row_sent, "ctrl").reshape(2, 3, planes, depth)
-    plane_sent = plane_sent.reshape(2, 3, rows, depth)
-    plane_halo = shifted_back(
-        jnp.concatenate([plane_sent, row_halo[:, :, :1]], axis=2), "slab"
-    )
     node_shift, volume, change = pl.pallas_call(
         functools.partial(volume_kernel, keep, share),
         out_shape=(
@@ -677,7 +713,7 @@
         in_specs=[vmem()] * (4 + len(backs)),
         out_specs=(vmem(),) * 3,
         compiler_params=limited(8),
-    )(node_points, shift.reshape(3, planes, rows, depth), row_halo, plane_halo, *backs)
+    )(node_points, shift.reshape(3, planes, rows, depth), *backs, plane_halo, row_halo)
     return node_shift, volume, change, state[0, : motion.shape[0]]
 
 

time: 61.9 us -> 60.1 us (0.971)
  the two profiles are of different devices: /device:TPU:0 before, /device:TPU:25 now
where the time goes in v4:
time: 60.1 us; the launch traced here: 59.7 us
  Pallas kernels  28.8 us (48%)
  starting transfers between devices  16.8 us (28%)
  waiting for transfers between devices  11.2 us (19%)
  local copies, waits for them, and re-layouts  2 us (3%)
  between operations  0.86 us (1%)
    ppermute x3, starting transfers between devices, shifted_back(): lax.ppermute(value, axis, [(i, i - 1) for i in range(1, lax.axis_size(axi...  10.6 us
    pallas_call x1, Pallas kernels, local(): pl.pallas_call(functools.partial(late_kernel, own, lent, parts, bits), ou...  10.4 us
    pallas_call x1, Pallas kernels, local(): pl.pallas_call(functools.partial(early_kernel, parts, bits), out_shape=(j...  9.37 us
    pallas_call x2, Pallas kernels, prepared(): pl.pallas_call(kernel, out_shape=(jax.ShapeDtypeStruct((2 * length + 2,),...  6.44 us
    ppermute x5, waiting for transfers between devices, swapped(): return lax.ppermute(value, ('slab', 'ctrl'), pairs)  6.3 us
    ppermute x3, waiting for transfers between devices, shifted_back(): lax.ppermute(value, axis, [(i, i - 1) for i in range(1, lax.axis_size(axi...  4.85 us
    ppermute x3, starting transfers between devices, local(): lax.ppermute(lent_shift, 'slab', [(h ^ bit, h) for h in heavy])  4.6 us
    pallas_call x1, Pallas kernels, local(): pl.pallas_call(functools.partial(pack_kernel, spans[:-1]), out_shape=[jax...  1.78 us
  transfers between devices with their start and end apart: 11, of which 5 were waited for; matrix products, arithmetic and copies ran while one was open for 2% of the time, Pallas kernels for 22%

profile of v4, /device:TPU:25, one launch (start us, length us, event | category | flops | bytes accessed | tf_op | source)
XLA Modules:
  0.0 59.7 jit_solution(5145222280869613445)
XLA Ops:
  0.6 1.8 %shard_map.129 = (f32[8,128]{1,0:T(8,128)}, f32[112,128]{1,0:T(8,128)}, f32[64,128]{1,0:T(8,128)}) custom-call(f32[1,4096]{1,0:T(1,128)} %bitcast.21, f32[3,4096]{1,0:T(4,128)} %area.1, f32[3,4096]{1,0:T(4,128)} %center.1, f32[3,256]{1,0:T(4,128)} %points.2, f32[18,256]{1,0:T(8,128)} %modes.1, f32[192,128]{1,0:T(8,128)} %bitcast.13, s32[8,8,16]{2,1,0:T(8,128)} %numbers.3, ...), custom_call_target="tpu_custom_call" | custom-call | tf_op jit(solution)/shard_map/pallas_call | solution.py:590
  2.4 0.1 collective-permute-start
  2.5 0.0 copy-start.3
  2.5 0.8 %slice.15 = f32[48,128]{1,0:T(8,128)S(1)} slice(f32[112,128]{1,0:T(8,128)} %get-tuple-element.29), slice={[0:48], [0:128]} | slice | bytes 49152 | tf_op jit(solution)/shard_map/slice | solution.py:604
  3.2 0.0 copy-start
  3.2 3.8 %collective-permute-done.refs_0_ = f32[112,128]{1,0:T(8,128)S(1)} collective-permute-done((f32[112,128]{1,0:T(8,128)}, f32[112,128]{1,0:T(8,128)S(1)}, u32[]{:S(2)}, u32[]{:S(2)}) %collective-permute-start) | collective-permute-done | bytes 57376 | tf_op jit(solution)/shard_map/ppermute | solution.py:41
  7.1 0.0 copy-done.3
  7.1 0.0 copy-start.1
  7.1 0.0 copy-start.2
  7.1 0.1 collective-permute-start.1
  7.2 0.0 copy-done
  7.2 0.6 %copy-done.1 = s32[8,8,16]{2,1,0:T(8,128)S(1)} copy-done((s32[8,8,16]{2,1,0:T(8,128)S(1)}, s32[8,8,16]{2,1,0:T(8,128)}, u32[]{:S(2)}) %copy-start.1) | copy-done | bytes 4120
  7.8 0.0 copy-done.2
  7.8 3.8 %shard_map.130 = (s32[2114]{0:T(1024)S(1)}, bf16[2048,128]{1,0:T(8,128)(2,1)S(1)}, f32[64,128]{1,0:T(8,128)S(1)}) custom-call(f32[192,128]{1,0:T(8,128)S(1)} %bitcast.14, s32[8,8,16]{2,1,0:T(8,128)S(1)} %copy-done.1, s32[8,8]{1,0:T(8,128)S(1)} %copy-done.2), custom_call_target="tpu_custom_call" | custom-call | bytes 8000000 | tf_op jit(solution)/shard_map/pallas_call | solution.py:286
  11.6 0.0 collective-permute-done.1.refs_1_
  11.7 0.0 copy-start.6
  11.7 1.3 %collective-permute-start.2 = (f32[256,128]{1,0:T(8,128)S(1)}, f32[256,128]{1,0:T(8,128)S(1)}, u32[]{:S(2)}, u32[]{:S(2)}) collective-permute-start(f32[256,128]{1,0:T(8,128)S(1)} %pad_maximum_fusion.1), channel_id=1, source_target_pairs={{0,4},{1,5},{2,6},{3,7},{4,0},{5,1},{6,2},{7,3},{8,12},{9,13},{10,... | collective-permute-start | bytes 393224 | tf_op jit(solution)/shard_map/ppermute | solution.py:41
  13.0 0.0 copy-done.6
  13.0 4.1 %collective-permute-start.3 = (f32[8,128]{1,0:T(8,128)S(1)}, f32[8,128]{1,0:T(8,128)S(1)}, u32[]{:S(2)}, u32[]{:S(2)}) collective-permute-start(f32[8,128]{1,0:T(8,128)S(1)} %copy-done.6), channel_id=1, source_target_pairs={{1,0},{2,1},{3,2},{5,4},{6,5},{7,6},{9,8},{10,9},{11,10},{13,12},{... | collective-permute-start | bytes 12296 | tf_op jit(solution)/shard_map/ppermute | solution.py:45
  17.1 0.0 collective-permute-done.2.refs_2_
  17.1 2.4 %collective-permute-done.3.refs_3_.refs_8_ = f32[8,128]{1,0:T(8,128)S(1)} collective-permute-done((f32[8,128]{1,0:T(8,128)S(1)}, f32[8,128]{1,0:T(8,128)S(1)}, u32[]{:S(2)}, u32[]{:S(2)}) %collective-permute-start.3) | collective-permute-done | bytes 4128 | tf_op jit(solution)/shard_map/ppermute | solution.py:45
  19.5 2.7 %shard_map.131 = (s32[578]{0:T(1024)S(1)}, bf16[512,128]{1,0:T(8,128)(2,1)S(1)}) custom-call(f32[112,128]{1,0:T(8,128)S(1)} %collective-permute-done.refs_0_, f32[160,128]{1,0:T(8,128)S(1)} %collective-permute-done.1.refs_1_, f32[256,128]{1,0:T(8,128)S(1)} %collective-permute-done.2.refs_2_, f32[8,128]{1,0:T(8,128)S(1)} %collective-permute-done.3.refs_3_.refs_8_), custom_call_target="tpu_custom_call" | custom-call | bytes 8000000 | tf_op jit(solution)/shard_map/pallas_call | solution.py:286
  22.1 0.1 collective-permute-start.4
  22.2 0.0 copy-start.4
  22.2 0.0 copy-start.5
  22.3 1.4 %collective-permute-done.4 = f32[384,128]{1,0:T(8,128)S(1)} collective-permute-done((f32[384,128]{1,0:T(8,128)S(1)}, f32[384,128]{1,0:T(8,128)S(1)}, u32[]{:S(2)}, u32[]{:S(2)}) %collective-permute-start.4) | collective-permute-done | bytes 196640 | tf_op jit(solution)/shard_map/ppermute | solution.py:41
  23.7 0.2 collective-permute-start.5
  23.8 0.0 copy-done.4
  23.8 0.0 copy-done.5
  23.8 9.4 %shard_map.132 = (f32[1944,128]{1,0:T(8,128)S(1)}, f32[1,128]{1,0:T(1,128)S(1)}) custom-call(s32[2114]{0:T(1024)S(1)} %get-tuple-element.34.refs_0_, s32[578]{0:T(1024)S(1)} %get-tuple-element.40.refs_1_, bf16[2048,128]{1,0:T(8,128)(2,1)S(1)} %get-tuple-element.41.refs_2_, bf16[512,128]{1,0:T(8,128)(2,1)S(1)} %get-tuple-element.42.refs_3_, ...), custom_call_target="tpu_custom_call" | custom-call | bytes 30000000 | tf_op jit(solution)/shard_map/pallas_call | solution.py:667
  33.2 1.1 %collective-permute-done.5.refs_4_ = f32[768,128]{1,0:T(8,128)S(1)} collective-permute-done((f32[768,128]{1,0:T(8,128)S(1)}, f32[768,128]{1,0:T(8,128)S(1)}, u32[]{:S(2)}, u32[]{:S(2)}) %collective-permute-start.5) | collective-permute-done | bytes 393248 | tf_op jit(solution)/shard_map/ppermute | solution.py:41
  34.3 10.4 %shard_map.133 = (f32[192,128]{1,0:T(8,128)S(1)}, f32[48,128]{1,0:T(8,128)S(1)}, f32[1,128]{1,0:T(1,128)S(1)}, f32[2,24,128]{2,1,0:T(8,128)S(1)}, f32[2,32,128]{2,1,0:T(8,128)S(1)}) custom-call(s32[2114]{0:T(1024)S(1)} %get-tuple-element.34.refs_0_, s32[578]{0:T(1024)S(1)} %get-tuple-element.40.refs_1_, bf16[2048,128]{1,0:T(8,128)(2,1)S(1)} %get-tuple-element.41.refs_2_, ...), custom_call_target="tpu_custom_call" | custom-call | tf_op jit(solution)/shard_map/pallas_call | solution.py:679
  44.7 0.7 %collective-permute-start.6 = (f32[48,128]{1,0:T(8,128)S(1)}, f32[48,128]{1,0:T(8,128)S(1)}, u32[]{:S(2)}, u32[]{:S(2)}) collective-permute-start(f32[48,128]{1,0:T(8,128)S(1)} %get-tuple-element.47), channel_id=1, source_target_pairs={{28,12},{0,16},{29,13},{1,17},{30,14},{2,18},{31,15},{3,19}} | collective-permute-start | bytes 73736 | tf_op jit(solution)/shard_map/ppermute | solution.py:699
  45.3 3.3 %collective-permute-start.7 = (f32[48,128]{1,0:T(8,128)S(1)}, f32[48,128]{1,0:T(8,128)S(1)}, u32[]{:S(2)}, u32[]{:S(2)}) collective-permute-start(f32[48,128]{1,0:T(8,128)S(1)} %get-tuple-element.47), channel_id=1, source_target_pairs={{4,12},{24,16},{5,13},{25,17},{6,14},{26,18},{7,15},{27,19}} | collective-permute-start | bytes 73736 | tf_op jit(solution)/shard_map/ppermute | solution.py:699
  48.6 0.7 %collective-permute-start.8 = (f32[48,128]{1,0:T(8,128)S(1)}, f32[48,128]{1,0:T(8,128)S(1)}, u32[]{:S(2)}, u32[]{:S(2)}) collective-permute-start(f32[48,128]{1,0:T(8,128)S(1)} %get-tuple-element.47), channel_id=1, source_target_pairs={{8,12},{20,16},{9,13},{21,17},{10,14},{22,18},{11,15},{23,19}} | collective-permute-start | bytes 73736 | tf_op jit(solution)/shard_map/ppermute | solution.py:699
  49.3 3.7 %collective-permute-start.9 = (f32[2,32,128]{2,1,0:T(8,128)S(1)}, f32[2,32,128]{2,1,0:T(8,128)S(1)}, u32[]{:S(2)}, u32[]{:S(2)}) collective-permute-start(f32[2,32,128]{2,1,0:T(8,128)S(1)} %get-tuple-element.48), channel_id=1, source_target_pairs={{4,0},{8,4},{12,8},{16,12},{20,16},{24,20},{28,24},{5,1},{9,5},{13... | collective-permute-start | bytes 98312 | tf_op jit(solution)/shard_map/ppermute | solution.py:45
  53.0 2.8 %collective-permute-start.10 = (f32[2,24,128]{2,1,0:T(8,128)S(1)}, f32[2,24,128]{2,1,0:T(8,128)S(1)}, u32[]{:S(2)}, u32[]{:S(2)}) collective-permute-start(f32[2,24,128]{2,1,0:T(8,128)S(1)} %get-tuple-element.49), channel_id=1, source_target_pairs={{1,0},{2,1},{3,2},{5,4},{6,5},{7,6},{9,8},{10,9},{11,10},{13,12},{... | collective-permute-start | bytes 73736 | tf_op jit(solution)/shard_map/ppermute | solution.py:45
  55.8 0.5 slice_bitcast_fusion
  56.3 0.0 collective-permute-done.6
  56.3 0.0 collective-permute-done.7
  56.3 0.0 collective-permute-done.8
  56.3 2.5 %collective-permute-done.10 = f32[2,24,128]{2,1,0:T(8,128)S(1)} collective-permute-done((f32[2,24,128]{2,1,0:T(8,128)S(1)}, f32[2,24,128]{2,1,0:T(8,128)S(1)}, u32[]{:S(2)}, u32[]{:S(2)}) %collective-permute-start.10) | collective-permute-done | bytes 24608 | tf_op jit(solution)/shard_map/ppermute | solution.py:45
  58.8 0.0 collective-permute-done.9.refs_3_
  58.8 0.9 %shard_map.134 = (f32[3,8,8,128]{3,2,1,0:T(8,128)}, f32[8,8,128]{2,1,0:T(8,128)}, f32[8,8,128]{2,1,0:T(8,128)}) custom-call(f32[3,8,8,128]{3,2,1,0:T(8,128)S(1)} %copy-done, f32[3,8,8,128]{3,2,1,0:T(8,128)S(1)} %bitcast.16, f32[3,2,8,128]{3,2,1,0:T(8,128)S(1)} %bitcast.17, f32[3,2,8,128]{3,2,1,0:T(8,128)S(1)} %bitcast.18, f32[3,2,8,128]{3,2,1,0:T(8,128)S(1)} %bitcast.19, ...), custom_call_target="tpu_custom_call" | custom-call | tf_op jit(solution)/shard_map/pallas_call | solution.py:706
  (10 shorter events, 0.1 us)
Async XLA Ops:
  2.4 4.6 %collective-permute-start = (f32[112,128]{1,0:T(8,128)}, f32[112,128]{1,0:T(8,128)S(1)}, u32[]{:S(2)}, u32[]{:S(2)}) collective-permute-start(f32[112,128]{1,0:T(8,128)} %get-tuple-element.29), channel_id=1, source_target_pairs={{0,16},{1,17},{2,18},{3,19},{4,20},{5,21},{6,22},{7,23},{8,24},{9,... | collective-permute-start | bytes 172040 | tf_op jit(solution)/shard_map/ppermute | solution.py:41
  2.5 4.6 %copy-start.3 = (f32[64,128]{1,0:T(8,128)S(1)}, f32[64,128]{1,0:T(8,128)}, u32[]{:S(2)}) copy-start(f32[64,128]{1,0:T(8,128)} %get-tuple-element.30) | copy-start | bytes 98308
  3.2 3.9 %copy-start = (f32[3,8,8,128]{3,2,1,0:T(8,128)S(1)}, f32[3,8,8,128]{3,2,1,0:T(8,128)}, u32[]{:S(2)}) copy-start(f32[3,8,8,128]{3,2,1,0:T(8,128)} %points.3) | copy-start | bytes 294916
  7.1 0.8 %copy-start.1 = (s32[8,8,16]{2,1,0:T(8,128)S(1)}, s32[8,8,16]{2,1,0:T(8,128)}, u32[]{:S(2)}) copy-start(s32[8,8,16]{2,1,0:T(8,128)} %numbers.3) | copy-start | bytes 12292
  7.1 0.8 %copy-start.2 = (s32[8,8]{1,0:T(8,128)S(1)}, s32[8,8]{1,0:T(8,128)}, u32[]{:S(2)}) copy-start(s32[8,8]{1,0:T(8,128)} %counts.3) | copy-start | bytes 772
  7.1 4.5 %collective-permute-start.1 = (f32[160,128]{1,0:T(8,128)S(1)}, f32[160,128]{1,0:T(8,128)S(1)}, u32[]{:S(2)}, u32[]{:S(2)}) collective-permute-start(f32[160,128]{1,0:T(8,128)S(1)} %pad_maximum_fusion.3), channel_id=1, source_target_pairs={{0,8},{1,9},{2,10},{3,11},{4,12},{5,13},{6,14},{7,15},{8,0},{9,1},... | collective-permute-start | bytes 245768 | tf_op jit(solution)/shard_map/ppermute | solution.py:41
  11.7 1.3 %copy-start.6 = (f32[8,128]{1,0:T(8,128)S(1)}, f32[8,128]{1,0:T(8,128)}, u32[]{:S(2)}) copy-start(f32[8,128]{1,0:T(8,128)} %get-tuple-element.37) | copy-start | bytes 12292
  11.7 5.4 %collective-permute-start.2 = (f32[256,128]{1,0:T(8,128)S(1)}, f32[256,128]{1,0:T(8,128)S(1)}, u32[]{:S(2)}, u32[]{:S(2)}) collective-permute-start(f32[256,128]{1,0:T(8,128)S(1)} %pad_maximum_fusion.1), channel_id=1, source_target_pairs={{0,4},{1,5},{2,6},{3,7},{4,0},{5,1},{6,2},{7,3},{8,12},{9,13},{10,... | collective-permute-start | bytes 393224 | tf_op jit(solution)/shard_map/ppermute | solution.py:41
  13.0 6.5 %collective-permute-start.3 = (f32[8,128]{1,0:T(8,128)S(1)}, f32[8,128]{1,0:T(8,128)S(1)}, u32[]{:S(2)}, u32[]{:S(2)}) collective-permute-start(f32[8,128]{1,0:T(8,128)S(1)} %copy-done.6), channel_id=1, source_target_pairs={{1,0},{2,1},{3,2},{5,4},{6,5},{7,6},{9,8},{10,9},{11,10},{13,12},{... | collective-permute-start | bytes 12296 | tf_op jit(solution)/shard_map/ppermute | solution.py:45
  22.1 1.5 %collective-permute-start.4 = (f32[384,128]{1,0:T(8,128)S(1)}, f32[384,128]{1,0:T(8,128)S(1)}, u32[]{:S(2)}, u32[]{:S(2)}) collective-permute-start(f32[384,128]{1,0:T(8,128)S(1)} %pad_maximum_fusion), channel_id=1, source_target_pairs={{0,1},{1,0},{2,3},{3,2},{4,5},{5,4},{6,7},{7,6},{8,9},{9,8},{10,11... | collective-permute-start | bytes 589832 | tf_op jit(solution)/shard_map/ppermute | solution.py:41
  22.2 1.6 %copy-start.4 = (f32[6]{0:T(128)S(1)}, f32[6]{0:T(128)}, u32[]{:S(2)}) copy-start(f32[6]{0:T(128)} %param.14) | copy-start | bytes 76
  22.2 1.6 %copy-start.5 = (f32[6]{0:T(128)S(1)}, f32[6]{0:T(128)}, u32[]{:S(2)}) copy-start(f32[6]{0:T(128)} %param.13) | copy-start | bytes 76
  23.7 10.6 %collective-permute-start.5 = (f32[768,128]{1,0:T(8,128)S(1)}, f32[768,128]{1,0:T(8,128)S(1)}, u32[]{:S(2)}, u32[]{:S(2)}) collective-permute-start(f32[768,128]{1,0:T(8,128)S(1)} %constant_dynamic-update-slice_fusion.refs_4_), channel_id=1, source_target_pairs={{0,2},{1,3},{2,0},{3,1},{4,6},{5,7},{6,4},{7,5},{8,10},{9,11},{10,... | collective-permute-start | bytes 1179656 | tf_op jit(solution)/shard_map/ppermute | solution.py:41
  44.7 11.6 %collective-permute-start.6 = (f32[48,128]{1,0:T(8,128)S(1)}, f32[48,128]{1,0:T(8,128)S(1)}, u32[]{:S(2)}, u32[]{:S(2)}) collective-permute-start(f32[48,128]{1,0:T(8,128)S(1)} %get-tuple-element.47), channel_id=1, source_target_pairs={{28,12},{0,16},{29,13},{1,17},{30,14},{2,18},{31,15},{3,19}} | collective-permute-start | bytes 73736 | tf_op jit(solution)/shard_map/ppermute | solution.py:699
  45.3 11.0 %collective-permute-start.7 = (f32[48,128]{1,0:T(8,128)S(1)}, f32[48,128]{1,0:T(8,128)S(1)}, u32[]{:S(2)}, u32[]{:S(2)}) collective-permute-start(f32[48,128]{1,0:T(8,128)S(1)} %get-tuple-element.47), channel_id=1, source_target_pairs={{4,12},{24,16},{5,13},{25,17},{6,14},{26,18},{7,15},{27,19}} | collective-permute-start | bytes 73736 | tf_op jit(solution)/shard_map/ppermute | solution.py:699
  48.6 7.7 %collective-permute-start.8 = (f32[48,128]{1,0:T(8,128)S(1)}, f32[48,128]{1,0:T(8,128)S(1)}, u32[]{:S(2)}, u32[]{:S(2)}) collective-permute-start(f32[48,128]{1,0:T(8,128)S(1)} %get-tuple-element.47), channel_id=1, source_target_pairs={{8,12},{20,16},{9,13},{21,17},{10,14},{22,18},{11,15},{23,19}} | collective-permute-start | bytes 73736 | tf_op jit(solution)/shard_map/ppermute | solution.py:699
  49.3 9.5 %collective-permute-start.9 = (f32[2,32,128]{2,1,0:T(8,128)S(1)}, f32[2,32,128]{2,1,0:T(8,128)S(1)}, u32[]{:S(2)}, u32[]{:S(2)}) collective-permute-start(f32[2,32,128]{2,1,0:T(8,128)S(1)} %get-tuple-element.48), channel_id=1, source_target_pairs={{4,0},{8,4},{12,8},{16,12},{20,16},{24,20},{28,24},{5,1},{9,5},{13... | collective-permute-start | bytes 98312 | tf_op jit(solution)/shard_map/ppermute | solution.py:45
  53.0 5.8 %collective-permute-start.10 = (f32[2,24,128]{2,1,0:T(8,128)S(1)}, f32[2,24,128]{2,1,0:T(8,128)S(1)}, u32[]{:S(2)}, u32[]{:S(2)}) collective-permute-start(f32[2,24,128]{2,1,0:T(8,128)S(1)} %get-tuple-element.49), channel_id=1, source_target_pairs={{1,0},{2,1},{3,2},{5,4},{6,5},{7,6},{9,8},{10,9},{11,10},{13,12},{... | collective-permute-start | bytes 73736 | tf_op jit(solution)/shard_map/ppermute | solution.py:45

commit v5 on v4

--- a/solution.py
+++ b/solution.py
@@ -610,18 +610,18 @@
                     (early, own_lists, sents[-1])
                 )
             if turn == 3:
-                early, lent_lists = lax.optimization_barrier((early, lent_lists))
+                early, corner = lax.optimization_barrier((early, corner))
             if lend and slab_bit in units:
                 payload = jnp.concatenate([early, sents[len(gots) - 1]], axis=0) if gots else first
                 reply = swapped(payload, slab_bit, ctrl_bit)
                 gots.append(reply)
                 bases.append(size)
                 reply = reply[:size]
-                if len(gots) == len(units):
-                    lent_lists = borrowed(gots, bases)
             else:
                 reply = swapped(early, slab_bit, ctrl_bit)
             early = jnp.concatenate([early, reply], axis=0)
+        lent_lists = borrowed(gots, bases)
+        early, lent_lists = lax.optimization_barrier((early, lent_lists))
         late = swapped(early, *order[-1])
     else:
         loads = pl.pallas_call(

time: 60.1 us -> 58.9 us (0.980)
  the two profiles are of different devices: /device:TPU:25 before, /device:TPU:0 now
where the time goes in v5:
time: 58.9 us; the launch traced here: 58.8 us
  Pallas kernels  28.2 us (48%)
  starting transfers between devices  20.1 us (34%)
  waiting for transfers between devices  8.01 us (14%)
  local copies, waits for them, and re-layouts  1.61 us (3%)
  between operations  0.83 us (1%)
    pallas_call x1, Pallas kernels, local(): pl.pallas_call(functools.partial(late_kernel, own, lent, parts, bits), ou...  9.72 us
    pallas_call x1, Pallas kernels, local(): pl.pallas_call(functools.partial(early_kernel, parts, bits), out_shape=(j...  9.41 us
    ppermute x5, starting transfers between devices, swapped(): return lax.ppermute(value, ('slab', 'ctrl'), pairs)  8.81 us
    ppermute x3, starting transfers between devices, local(): lax.ppermute(lent_shift, 'slab', [(h ^ bit, h) for h in heavy])  7.4 us
    pallas_call x2, Pallas kernels, prepared(): pl.pallas_call(kernel, out_shape=(jax.ShapeDtypeStruct((2 * length + 2,),...  6.44 us
    ppermute x5, waiting for transfers between devices, swapped(): return lax.ppermute(value, ('slab', 'ctrl'), pairs)  5.31 us
    ppermute x3, starting transfers between devices, shifted_back(): lax.ppermute(value, axis, [(i, i - 1) for i in range(1, lax.axis_size(axi...  3.86 us
    ppermute x3, waiting for transfers between devices, shifted_back(): lax.ppermute(value, axis, [(i, i - 1) for i in range(1, lax.axis_size(axi...  2.68 us
  transfers between devices with their start and end apart: 11, of which 5 were waited for; matrix products, arithmetic and copies ran while one was open for 2% of the time, Pallas kernels for 27%

profile of v5, /device:TPU:0, one launch (start us, length us, event | category | flops | bytes accessed | tf_op | source)
XLA Modules:
  0.0 58.8 jit_solution(3466434065895388655)
XLA Ops:
  0.6 1.8 %shard_map.129 = (f32[8,128]{1,0:T(8,128)}, f32[112,128]{1,0:T(8,128)}, f32[64,128]{1,0:T(8,128)}) custom-call(f32[1,4096]{1,0:T(1,128)} %bitcast.21, f32[3,4096]{1,0:T(4,128)} %area.1, f32[3,4096]{1,0:T(4,128)} %center.1, f32[3,256]{1,0:T(4,128)} %points.2, f32[18,256]{1,0:T(8,128)} %modes.1, f32[192,128]{1,0:T(8,128)} %bitcast.13, s32[8,8,16]{2,1,0:T(8,128)} %numbers.3, ...), custom_call_target="tpu_custom_call" | custom-call | tf_op jit(solution)/shard_map/pallas_call | solution.py:590
  2.4 4.0 %collective-permute-start = (f32[112,128]{1,0:T(8,128)}, f32[112,128]{1,0:T(8,128)S(1)}, u32[]{:S(2)}, u32[]{:S(2)}) collective-permute-start(f32[112,128]{1,0:T(8,128)} %get-tuple-element.31), channel_id=1, source_target_pairs={{0,16},{1,17},{2,18},{3,19},{4,20},{5,21},{6,22},{7,23},{8,24},{9,... | collective-permute-start | bytes 172040 | tf_op jit(solution)/shard_map/ppermute | solution.py:41
  6.5 0.0 copy-start.3
  6.5 0.8 %slice.15 = f32[48,128]{1,0:T(8,128)S(1)} slice(f32[112,128]{1,0:T(8,128)} %get-tuple-element.31), slice={[0:48], [0:128]} | slice | bytes 49152 | tf_op jit(solution)/shard_map/slice | solution.py:604
  7.2 0.0 copy-start
  7.2 2.2 %collective-permute-done.refs_0_ = f32[112,128]{1,0:T(8,128)S(1)} collective-permute-done((f32[112,128]{1,0:T(8,128)}, f32[112,128]{1,0:T(8,128)S(1)}, u32[]{:S(2)}, u32[]{:S(2)}) %collective-permute-start) | collective-permute-done | bytes 57376 | tf_op jit(solution)/shard_map/ppermute | solution.py:41
  9.4 0.0 copy-done.3
  9.4 0.0 copy-start.1
  9.4 0.0 copy-start.2
  9.5 1.4 %collective-permute-start.1 = (f32[160,128]{1,0:T(8,128)S(1)}, f32[160,128]{1,0:T(8,128)S(1)}, u32[]{:S(2)}, u32[]{:S(2)}) collective-permute-start(f32[160,128]{1,0:T(8,128)S(1)} %pad_maximum_fusion.4), channel_id=1, source_target_pairs={{0,8},{1,9},{2,10},{3,11},{4,12},{5,13},{6,14},{7,15},{8,0},{9,1},... | collective-permute-start | bytes 245768 | tf_op jit(solution)/shard_map/ppermute | solution.py:41
  10.8 0.0 copy-done
  10.8 0.0 copy-done.1
  10.8 0.0 copy-done.2
  10.8 3.8 %shard_map.130 = (s32[2114]{0:T(1024)S(1)}, bf16[2048,128]{1,0:T(8,128)(2,1)S(1)}, f32[64,128]{1,0:T(8,128)S(1)}) custom-call(f32[192,128]{1,0:T(8,128)S(1)} %bitcast.14, s32[8,8,16]{2,1,0:T(8,128)S(1)} %copy-done.1, s32[8,8]{1,0:T(8,128)S(1)} %copy-done.2), custom_call_target="tpu_custom_call" | custom-call | bytes 8000000 | tf_op jit(solution)/shard_map/pallas_call | solution.py:286
  14.6 0.0 collective-permute-done.1.refs_1_
  14.7 0.0 copy-start.6
  14.7 1.6 %collective-permute-start.2 = (f32[256,128]{1,0:T(8,128)S(1)}, f32[256,128]{1,0:T(8,128)S(1)}, u32[]{:S(2)}, u32[]{:S(2)}) collective-permute-start(f32[256,128]{1,0:T(8,128)S(1)} %pad_maximum_fusion.2), channel_id=1, source_target_pairs={{0,4},{1,5},{2,6},{3,7},{4,0},{5,1},{6,2},{7,3},{8,12},{9,13},{10,... | collective-permute-start | bytes 393224 | tf_op jit(solution)/shard_map/ppermute | solution.py:41
  16.4 0.0 copy-done.6
  16.4 1.3 %collective-permute-start.3 = (f32[8,128]{1,0:T(8,128)S(1)}, f32[8,128]{1,0:T(8,128)S(1)}, u32[]{:S(2)}, u32[]{:S(2)}) collective-permute-start(f32[8,128]{1,0:T(8,128)S(1)} %copy-done.6), channel_id=1, source_target_pairs={{1,0},{2,1},{3,2},{5,4},{6,5},{7,6},{9,8},{10,9},{11,10},{13,12},{... | collective-permute-start | bytes 12296 | tf_op jit(solution)/shard_map/ppermute | solution.py:45
  17.6 2.1 %collective-permute-done.2.refs_2_ = f32[256,128]{1,0:T(8,128)S(1)} collective-permute-done((f32[256,128]{1,0:T(8,128)S(1)}, f32[256,128]{1,0:T(8,128)S(1)}, u32[]{:S(2)}, u32[]{:S(2)}) %collective-permute-start.2) | collective-permute-done | bytes 131104 | tf_op jit(solution)/shard_map/ppermute | solution.py:41
  19.8 0.0 collective-permute-done.3.refs_3_.refs_8_
  19.8 1.4 %collective-permute-start.4 = (f32[384,128]{1,0:T(8,128)S(1)}, f32[384,128]{1,0:T(8,128)S(1)}, u32[]{:S(2)}, u32[]{:S(2)}) collective-permute-start(f32[384,128]{1,0:T(8,128)S(1)} %pad_maximum_fusion.1), channel_id=1, source_target_pairs={{0,1},{1,0},{2,3},{3,2},{4,5},{5,4},{6,7},{7,6},{8,9},{9,8},{10,11... | collective-permute-start | bytes 589832 | tf_op jit(solution)/shard_map/ppermute | solution.py:41
  21.2 2.7 %shard_map.131 = (s32[578]{0:T(1024)S(1)}, bf16[512,128]{1,0:T(8,128)(2,1)S(1)}) custom-call(f32[112,128]{1,0:T(8,128)S(1)} %collective-permute-done.refs_0_, f32[160,128]{1,0:T(8,128)S(1)} %collective-permute-done.1.refs_1_, f32[256,128]{1,0:T(8,128)S(1)} %collective-permute-done.2.refs_2_, f32[8,128]{1,0:T(8,128)S(1)} %collective-permute-done.3.refs_3_.refs_8_), custom_call_target="tpu_custom_call" | custom-call | bytes 8000000 | tf_op jit(solution)/shard_map/pallas_call | solution.py:286
  23.8 0.0 collective-permute-done.4
  23.9 0.0 copy-start.4
  23.9 0.0 copy-start.5
  23.9 0.4 collective-permute-start.5
  24.3 0.3 copy-done.4
  24.5 0.0 copy-done.5
  24.6 9.4 %shard_map.132 = (f32[1944,128]{1,0:T(8,128)S(1)}, f32[1,128]{1,0:T(1,128)S(1)}) custom-call(s32[2114]{0:T(1024)S(1)} %get-tuple-element.36.refs_0_, s32[578]{0:T(1024)S(1)} %get-tuple-element.44.refs_1_, bf16[2048,128]{1,0:T(8,128)(2,1)S(1)} %get-tuple-element.45.refs_2_, bf16[512,128]{1,0:T(8,128)(2,1)S(1)} %get-tuple-element.46.refs_3_, ...), custom_call_target="tpu_custom_call" | custom-call | bytes 30000000 | tf_op jit(solution)/shard_map/pallas_call | solution.py:667
  34.0 1.0 %collective-permute-done.5.refs_4_ = f32[768,128]{1,0:T(8,128)S(1)} collective-permute-done((f32[768,128]{1,0:T(8,128)S(1)}, f32[768,128]{1,0:T(8,128)S(1)}, u32[]{:S(2)}, u32[]{:S(2)}) %collective-permute-start.5) | collective-permute-done | bytes 393248 | tf_op jit(solution)/shard_map/ppermute | solution.py:41
  35.0 9.7 %shard_map.133 = (f32[192,128]{1,0:T(8,128)S(1)}, f32[48,128]{1,0:T(8,128)S(1)}, f32[1,128]{1,0:T(1,128)S(1)}, f32[2,24,128]{2,1,0:T(8,128)S(1)}, f32[2,32,128]{2,1,0:T(8,128)S(1)}) custom-call(s32[2114]{0:T(1024)S(1)} %get-tuple-element.36.refs_0_, s32[578]{0:T(1024)S(1)} %get-tuple-element.44.refs_1_, bf16[2048,128]{1,0:T(8,128)(2,1)S(1)} %get-tuple-element.45.refs_2_, ...), custom_call_target="tpu_custom_call" | custom-call | tf_op jit(solution)/shard_map/pallas_call | solution.py:679
  44.7 6.1 %collective-permute-start.6 = (f32[48,128]{1,0:T(8,128)S(1)}, f32[48,128]{1,0:T(8,128)S(1)}, u32[]{:S(2)}, u32[]{:S(2)}) collective-permute-start(f32[48,128]{1,0:T(8,128)S(1)} %get-tuple-element.51), channel_id=1, source_target_pairs={{28,12},{0,16},{29,13},{1,17},{30,14},{2,18},{31,15},{3,19}} | collective-permute-start | bytes 73736 | tf_op jit(solution)/shard_map/ppermute | solution.py:699
  50.8 0.7 %collective-permute-start.7 = (f32[48,128]{1,0:T(8,128)S(1)}, f32[48,128]{1,0:T(8,128)S(1)}, u32[]{:S(2)}, u32[]{:S(2)}) collective-permute-start(f32[48,128]{1,0:T(8,128)S(1)} %get-tuple-element.51), channel_id=1, source_target_pairs={{4,12},{24,16},{5,13},{25,17},{6,14},{26,18},{7,15},{27,19}} | collective-permute-start | bytes 73736 | tf_op jit(solution)/shard_map/ppermute | solution.py:699
  51.5 0.7 %collective-permute-start.8 = (f32[48,128]{1,0:T(8,128)S(1)}, f32[48,128]{1,0:T(8,128)S(1)}, u32[]{:S(2)}, u32[]{:S(2)}) collective-permute-start(f32[48,128]{1,0:T(8,128)S(1)} %get-tuple-element.51), channel_id=1, source_target_pairs={{8,12},{20,16},{9,13},{21,17},{10,14},{22,18},{11,15},{23,19}} | collective-permute-start | bytes 73736 | tf_op jit(solution)/shard_map/ppermute | solution.py:699
  52.1 1.3 %collective-permute-start.9 = (f32[2,32,128]{2,1,0:T(8,128)S(1)}, f32[2,32,128]{2,1,0:T(8,128)S(1)}, u32[]{:S(2)}, u32[]{:S(2)}) collective-permute-start(f32[2,32,128]{2,1,0:T(8,128)S(1)} %get-tuple-element.52), channel_id=1, source_target_pairs={{4,0},{8,4},{12,8},{16,12},{20,16},{24,20},{28,24},{5,1},{9,5},{13... | collective-permute-start | bytes 98312 | tf_op jit(solution)/shard_map/ppermute | solution.py:45
  53.4 1.3 %collective-permute-start.10 = (f32[2,24,128]{2,1,0:T(8,128)S(1)}, f32[2,24,128]{2,1,0:T(8,128)S(1)}, u32[]{:S(2)}, u32[]{:S(2)}) collective-permute-start(f32[2,24,128]{2,1,0:T(8,128)S(1)} %get-tuple-element.53), channel_id=1, source_target_pairs={{1,0},{2,1},{3,2},{5,4},{6,5},{7,6},{9,8},{10,9},{11,10},{13,12},{... | collective-permute-start | bytes 73736 | tf_op jit(solution)/shard_map/ppermute | solution.py:45
  54.7 0.5 slice_bitcast_fusion
  55.3 0.0 collective-permute-done.6
  55.3 0.0 collective-permute-done.7
  55.3 0.0 collective-permute-done.8
  55.3 1.3 %collective-permute-done.10 = f32[2,24,128]{2,1,0:T(8,128)S(1)} collective-permute-done((f32[2,24,128]{2,1,0:T(8,128)S(1)}, f32[2,24,128]{2,1,0:T(8,128)S(1)}, u32[]{:S(2)}, u32[]{:S(2)}) %collective-permute-start.10) | collective-permute-done | bytes 24608 | tf_op jit(solution)/shard_map/ppermute | solution.py:45
  56.5 1.4 %collective-permute-done.9.refs_3_ = f32[2,32,128]{2,1,0:T(8,128)S(1)} collective-permute-done((f32[2,32,128]{2,1,0:T(8,128)S(1)}, f32[2,32,128]{2,1,0:T(8,128)S(1)}, u32[]{:S(2)}, u32[]{:S(2)}) %collective-permute-start.9) | collective-permute-done | bytes 32800 | tf_op jit(solution)/shard_map/ppermute | solution.py:45
  58.0 0.9 %shard_map.134 = (f32[3,8,8,128]{3,2,1,0:T(8,128)}, f32[8,8,128]{2,1,0:T(8,128)}, f32[8,8,128]{2,1,0:T(8,128)}) custom-call(f32[3,8,8,128]{3,2,1,0:T(8,128)S(1)} %copy-done, f32[3,8,8,128]{3,2,1,0:T(8,128)S(1)} %bitcast.16, f32[3,2,8,128]{3,2,1,0:T(8,128)S(1)} %bitcast.17, f32[3,2,8,128]{3,2,1,0:T(8,128)S(1)} %bitcast.18, f32[3,2,8,128]{3,2,1,0:T(8,128)S(1)} %bitcast.19, ...), custom_call_target="tpu_custom_call" | custom-call | tf_op jit(solution)/shard_map/pallas_call | solution.py:706
  (9 shorter events, 0.1 us)
Async XLA Ops:
  2.4 7.0 %collective-permute-start = (f32[112,128]{1,0:T(8,128)}, f32[112,128]{1,0:T(8,128)S(1)}, u32[]{:S(2)}, u32[]{:S(2)}) collective-permute-start(f32[112,128]{1,0:T(8,128)} %get-tuple-element.31), channel_id=1, source_target_pairs={{0,16},{1,17},{2,18},{3,19},{4,20},{5,21},{6,22},{7,23},{8,24},{9,... | collective-permute-start | bytes 172040 | tf_op jit(solution)/shard_map/ppermute | solution.py:41
  6.5 3.0 %copy-start.3 = (f32[64,128]{1,0:T(8,128)S(1)}, f32[64,128]{1,0:T(8,128)}, u32[]{:S(2)}) copy-start(f32[64,128]{1,0:T(8,128)} %get-tuple-element.32) | copy-start | bytes 98308
  7.2 3.6 %copy-start = (f32[3,8,8,128]{3,2,1,0:T(8,128)S(1)}, f32[3,8,8,128]{3,2,1,0:T(8,128)}, u32[]{:S(2)}) copy-start(f32[3,8,8,128]{3,2,1,0:T(8,128)} %points.3) | copy-start | bytes 294916
  9.4 1.4 %copy-start.1 = (s32[8,8,16]{2,1,0:T(8,128)S(1)}, s32[8,8,16]{2,1,0:T(8,128)}, u32[]{:S(2)}) copy-start(s32[8,8,16]{2,1,0:T(8,128)} %numbers.3) | copy-start | bytes 12292
  9.4 1.4 %copy-start.2 = (s32[8,8]{1,0:T(8,128)S(1)}, s32[8,8]{1,0:T(8,128)}, u32[]{:S(2)}) copy-start(s32[8,8]{1,0:T(8,128)} %counts.3) | copy-start | bytes 772
  9.5 5.2 %collective-permute-start.1 = (f32[160,128]{1,0:T(8,128)S(1)}, f32[160,128]{1,0:T(8,128)S(1)}, u32[]{:S(2)}, u32[]{:S(2)}) collective-permute-start(f32[160,128]{1,0:T(8,128)S(1)} %pad_maximum_fusion.4), channel_id=1, source_target_pairs={{0,8},{1,9},{2,10},{3,11},{4,12},{5,13},{6,14},{7,15},{8,0},{9,1},... | collective-permute-start | bytes 245768 | tf_op jit(solution)/shard_map/ppermute | solution.py:41
  14.7 1.7 %copy-start.6 = (f32[8,128]{1,0:T(8,128)S(1)}, f32[8,128]{1,0:T(8,128)}, u32[]{:S(2)}) copy-start(f32[8,128]{1,0:T(8,128)} %get-tuple-element.39) | copy-start | bytes 12292
  14.7 5.0 %collective-permute-start.2 = (f32[256,128]{1,0:T(8,128)S(1)}, f32[256,128]{1,0:T(8,128)S(1)}, u32[]{:S(2)}, u32[]{:S(2)}) collective-permute-start(f32[256,128]{1,0:T(8,128)S(1)} %pad_maximum_fusion.2), channel_id=1, source_target_pairs={{0,4},{1,5},{2,6},{3,7},{4,0},{5,1},{6,2},{7,3},{8,12},{9,13},{10,... | collective-permute-start | bytes 393224 | tf_op jit(solution)/shard_map/ppermute | solution.py:41
  16.4 3.4 %collective-permute-start.3 = (f32[8,128]{1,0:T(8,128)S(1)}, f32[8,128]{1,0:T(8,128)S(1)}, u32[]{:S(2)}, u32[]{:S(2)}) collective-permute-start(f32[8,128]{1,0:T(8,128)S(1)} %copy-done.6), channel_id=1, source_target_pairs={{1,0},{2,1},{3,2},{5,4},{6,5},{7,6},{9,8},{10,9},{11,10},{13,12},{... | collective-permute-start | bytes 12296 | tf_op jit(solution)/shard_map/ppermute | solution.py:45
  19.8 4.1 %collective-permute-start.4 = (f32[384,128]{1,0:T(8,128)S(1)}, f32[384,128]{1,0:T(8,128)S(1)}, u32[]{:S(2)}, u32[]{:S(2)}) collective-permute-start(f32[384,128]{1,0:T(8,128)S(1)} %pad_maximum_fusion.1), channel_id=1, source_target_pairs={{0,1},{1,0},{2,3},{3,2},{4,5},{5,4},{6,7},{7,6},{8,9},{9,8},{10,11... | collective-permute-start | bytes 589832 | tf_op jit(solution)/shard_map/ppermute | solution.py:41
  23.9 0.7 %copy-start.4 = (f32[6]{0:T(128)S(1)}, f32[6]{0:T(128)}, u32[]{:S(2)}) copy-start(f32[6]{0:T(128)} %param.14) | copy-start | bytes 76
  23.9 0.7 %copy-start.5 = (f32[6]{0:T(128)S(1)}, f32[6]{0:T(128)}, u32[]{:S(2)}) copy-start(f32[6]{0:T(128)} %param.13) | copy-start | bytes 76
  23.9 11.1 %collective-permute-start.5 = (f32[768,128]{1,0:T(8,128)S(1)}, f32[768,128]{1,0:T(8,128)S(1)}, u32[]{:S(2)}, u32[]{:S(2)}) collective-permute-start(f32[768,128]{1,0:T(8,128)S(1)} %pad_maximum_fusion.refs_4_), channel_id=1, source_target_pairs={{0,2},{1,3},{2,0},{3,1},{4,6},{5,7},{6,4},{7,5},{8,10},{9,11},{10,... | collective-permute-start | bytes 1179656 | tf_op jit(solution)/shard_map/ppermute | solution.py:41
  44.7 10.5 %collective-permute-start.6 = (f32[48,128]{1,0:T(8,128)S(1)}, f32[48,128]{1,0:T(8,128)S(1)}, u32[]{:S(2)}, u32[]{:S(2)}) collective-permute-start(f32[48,128]{1,0:T(8,128)S(1)} %get-tuple-element.51), channel_id=1, source_target_pairs={{28,12},{0,16},{29,13},{1,17},{30,14},{2,18},{31,15},{3,19}} | collective-permute-start | bytes 73736 | tf_op jit(solution)/shard_map/ppermute | solution.py:699
  50.8 4.5 %collective-permute-start.7 = (f32[48,128]{1,0:T(8,128)S(1)}, f32[48,128]{1,0:T(8,128)S(1)}, u32[]{:S(2)}, u32[]{:S(2)}) collective-permute-start(f32[48,128]{1,0:T(8,128)S(1)} %get-tuple-element.51), channel_id=1, source_target_pairs={{4,12},{24,16},{5,13},{25,17},{6,14},{26,18},{7,15},{27,19}} | collective-permute-start | bytes 73736 | tf_op jit(solution)/shard_map/ppermute | solution.py:699
  51.5 3.8 %collective-permute-start.8 = (f32[48,128]{1,0:T(8,128)S(1)}, f32[48,128]{1,0:T(8,128)S(1)}, u32[]{:S(2)}, u32[]{:S(2)}) collective-permute-start(f32[48,128]{1,0:T(8,128)S(1)} %get-tuple-element.51), channel_id=1, source_target_pairs={{8,12},{20,16},{9,13},{21,17},{10,14},{22,18},{11,15},{23,19}} | collective-permute-start | bytes 73736 | tf_op jit(solution)/shard_map/ppermute | solution.py:699
  52.1 5.8 %collective-permute-start.9 = (f32[2,32,128]{2,1,0:T(8,128)S(1)}, f32[2,32,128]{2,1,0:T(8,128)S(1)}, u32[]{:S(2)}, u32[]{:S(2)}) collective-permute-start(f32[2,32,128]{2,1,0:T(8,128)S(1)} %get-tuple-element.52), channel_id=1, source_target_pairs={{4,0},{8,4},{12,8},{16,12},{20,16},{24,20},{28,24},{5,1},{9,5},{13... | collective-permute-start | bytes 98312 | tf_op jit(solution)/shard_map/ppermute | solution.py:45
  53.4 3.1 %collective-permute-start.10 = (f32[2,24,128]{2,1,0:T(8,128)S(1)}, f32[2,24,128]{2,1,0:T(8,128)S(1)}, u32[]{:S(2)}, u32[]{:S(2)}) collective-permute-start(f32[2,24,128]{2,1,0:T(8,128)S(1)} %get-tuple-element.53), channel_id=1, source_target_pairs={{1,0},{2,1},{3,2},{5,4},{6,5},{7,6},{9,8},{10,9},{11,10},{13,12},{... | collective-permute-start | bytes 73736 | tf_op jit(solution)/shard_map/ppermute | solution.py:45

commit v6 on v5

--- a/solution.py
+++ b/solution.py
@@ -81,29 +81,39 @@
     return jnp.sum(jnp.where(row == lane, many, 0.0), axis=1, keepdims=True)
 
 
-def pack_lent(planes, base, nodes, numbers, counts, out):
+def marked(numbers, counts, x):
+    slot = lax.broadcasted_iota(jnp.int32, numbers.shape[1:], 1).astype(F32)
+    return jnp.where(slot < count_column(counts, x), numbers[x].astype(F32) + 1.0, 0.0)
+
+
+def pack_lent(planes, turn, base, nodes, numbers, counts, out):
     rows, slots = numbers.shape[1:]
     lent = len(planes) * rows
-    wide = lax.broadcasted_iota(jnp.int32, (rows, out.shape[1]), 1)
     for i, x in enumerate(planes):
         at = base + i * rows
         for c in range(3):
             first = (c * counts.shape[0] + x) * rows
             out[at + c * lent : at + c * lent + rows, :] = nodes[first : first + rows, :]
-        at = at + 3 * lent
-        out[at : at + rows, :] = jnp.where(wide == slots, count_column(counts, x), 0.0)
-        out[at : at + rows, 0:slots] = numbers[x].astype(F32)
+    at, y = base + rows, 1 + turn
+    for c in range(3):
+        first = (c * counts.shape[0] + 1) * rows + y
+        out[at + c * lent : at + c * lent + 1, :] = nodes[first : first + 1, :]
+    for i, x in enumerate(planes):
+        listed = marked(numbers, counts, x)
+        if i == 1:
+            listed = jnp.concatenate([marked(numbers, counts, 1)[y : y + 1], listed[1:]], axis=0)
+        at = base + i * lent
+        for row in range(rows):
+            out[at : at + 1, row * slots : (row + 1) * slots] = listed[row : row + 1]
 
 
 def pack_corner(nodes, numbers, counts, out):
     slots = numbers.shape[2]
-    lane = lax.broadcasted_iota(jnp.int32, (1, out.shape[1]), 1)
     out[...] = jnp.zeros(out.shape, F32)
     for c in range(3):
         first = c * counts.shape[0] * counts.shape[1]
         out[c : c + 1, :] = nodes[first : first + 1, :]
-    out[3:4, :] = jnp.where(lane == slots, count_column(counts, 0)[0:1], 0.0)
-    out[3:4, 0:slots] = numbers[0, 0:1, :].astype(F32)
+    out[3:4, 0:slots] = marked(numbers, counts, 0)[0:1]
 
 
 def pack_kernel(
@@ -112,16 +122,15 @@
     row = load_rows(pressure[...], area[...], center[...])
     pack_table(row, points, modes, out)
     pack_corner(nodes, numbers, counts, corner)
-    if spans:
-        pack_lent(spans[0], points.shape[1] // TILE * ROWS, nodes, numbers, counts, out)
-    for span, lent in zip(spans[1:], lents):
-        pack_lent(span, 0, nodes, numbers, counts, lent)
+    pack_lent(spans[0], 0, points.shape[1] // TILE * ROWS, nodes, numbers, counts, out)
+    for turn, (span, lent) in enumerate(zip(spans[1:], lents)):
+        pack_lent(span, turn + 1, 0, nodes, numbers, counts, lent)
 
 
 def lend_kernel(spans, nodes, numbers, counts, corner, *outs):
     pack_corner(nodes, numbers, counts, corner)
-    for span, out in zip(spans, outs):
-        pack_lent(span, 0, nodes, numbers, counts, out)
+    for turn, (span, out) in enumerate(zip(spans, outs)):
+        pack_lent(span, turn, 0, nodes, numbers, counts, out)
 
 
 def loads_kernel(pressure, area, center, out):
@@ -186,33 +195,27 @@
     few = min(4, slots)
     middle = lines * slots + 2 * UNROLL
 
-    def take(line, low, high, ends):
-        end_a, end_b = ends
-        found = [listed[line, e] for e in range(low, high)]
-        live = [1 + lax.shift_right_arithmetic(code, 31) for code in found]
-        late = [n & lax.shift_right_logical(code, bits - 1) for n, code in zip(live, found)]
-        for code, n, m in zip(found, live, late):
-            items[end_a] = code
-            items[end_b] = code
-            end_a, end_b = end_a + (n - m), end_b + m
-        return end_a, end_b
-
-    def one(line, ends):
-        ends = take(line, 0, few, ends)
-        return lax.cond(
-            listed[line, slots] > few,
-            lambda ends: take(line, few, slots, ends),
-            lambda ends: ends,
-            ends,
-        )
-
-    end_a, end_b = lax.fori_loop(0, lines, one, (jnp.int32(0), jnp.int32(middle)))
-    dummy = (first + lines) << bits
+    def take(line, low, high):
+        for e in range(low, high):
+            value = listed[line, e]
+            items[lax.shift_right_logical(value, 16)] = value
+
+    def one(line, carry):
+        take(line, 0, few)
+
+        def rest(step, carry):
+            take(line, few, slots)
+            return carry
+
+        return lax.fori_loop(0, jnp.where(listed[line, slots] > few, 1, 0), rest, carry)
+
+    lax.fori_loop(0, lines, one, 0)
+    end_a, end_b = listed[0, slots + 1], listed[0, slots + 2]
     for e in range(2 * UNROLL):
-        items[end_a + e] = dummy
-        items[end_b + e] = dummy
+        items[end_a + e] = (first + lines) << bits
+        items[middle + end_b + e] = (first + lines) << bits
     items[2 * middle] = end_a
-    items[2 * middle + 1] = end_b - middle
+    items[2 * middle + 1] = end_b
 
 
 def line_features(lines, points, line_feat):
@@ -225,29 +228,55 @@
     lax.fori_loop(0, lines, block, 0, unroll=4)
 
 
-def coded(first, bits, placed, number, count):
-    row = lax.broadcasted_iota(jnp.int32, number.shape, 0)
-    slot = lax.broadcasted_iota(jnp.int32, number.shape, 1)
-    code = lax.shift_left(row + first, jnp.full_like(row, bits)) + placed(number)
-    return jnp.where(slot < count, code, -1)
+def code_items(first, bits, placed, numbers, counts, codes):
+    lines, slots = numbers.shape
+    row = lax.broadcasted_iota(jnp.int32, (lines, slots), 0)
+    slot = lax.broadcasted_iota(jnp.int32, (lines, slots), 1)
+    code = lax.shift_left(row + first, jnp.full_like(row, bits)) + placed(numbers)
+    late = lax.shift_right_logical(code, jnp.full_like(row, bits - 1)) & 1
+    middle = lines * slots + 2 * UNROLL
+    high = lax.broadcasted_iota(jnp.int32, (slots, slots), 0)
+    wide = lax.broadcasted_iota(jnp.int32, (slots, slots), 1)
+    before = jnp.where(high < wide, 1.0, 0.0).astype(BF16)
+    high = lax.broadcasted_iota(jnp.int32, (lines, lines), 0)
+    wide = lax.broadcasted_iota(jnp.int32, (lines, lines), 1)
+    above = jnp.where(wide < high, 1.0, 0.0).astype(BF16)
+    place = jnp.full((lines, slots), 2 * middle + 2, jnp.int32)
+    ends = []
+    for part in range(2):
+        chosen = (slot < counts) & (late == part)
+        flag = jnp.where(chosen, 1.0, 0.0)
+        total = jnp.broadcast_to(jnp.sum(flag, axis=1, keepdims=True), (lines, slots))
+        at = jnp.dot(flag.astype(BF16), before, preferred_element_type=F32)
+        at = at + jnp.dot(above, total.astype(BF16), preferred_element_type=F32)
+        place = jnp.where(chosen, at.astype(jnp.int32) + part * middle, place)
+        ends.append(jnp.sum(total[:, 0:1], axis=0, keepdims=True).astype(jnp.int32))
+    codes[:, 0:slots] = lax.shift_left(place, jnp.full_like(place, 16)) | code
+    codes[:, slots : slots + 1] = counts
+    codes[0:1, slots + 1 : slots + 2] = ends[0]
+    codes[0:1, slots + 2 : slots + 3] = ends[1]
 
 
 def own_kernel(
-    keep, bits, placed, span, points, numbers, counts,
+    keep, turns, bits, placed, span, points, numbers, counts,
     items, line_feat, sent, codes, listed, sem,
 ):
     planes, rows, slots = numbers.shape
-    pack_lent(span, 0, points, numbers, counts, sent)
+    pack_lent(span, turns - 1, 0, points, numbers, counts, sent)
     slabs = lax.axis_size("slab")
     lends = is_heavy(lax.axis_index("slab"), slabs)
+    columns = []
     for x in range(planes):
         count = count_column(counts, x).astype(jnp.int32)
         if x >= keep:
             row = lax.broadcasted_iota(jnp.int32, count.shape, 0)
             count = jnp.where(lends & (row >= 1), 0, count)
-        span = slice(x * rows, (x + 1) * rows)
-        codes[span, 0:slots] = coded(x * rows, bits, placed, numbers[x], count)
-        codes[span, slots : slots + 1] = count
+        if x == 1:
+            row = lax.broadcasted_iota(jnp.int32, count.shape, 0)
+            count = jnp.where(lends & (row >= 1) & (row <= turns), 0, count)
+        columns.append(count)
+    number = jnp.concatenate([numbers[x] for x in range(planes)], axis=0)
+    code_items(0, bits, placed, number, jnp.concatenate(columns, axis=0), codes)
     copy = pltpu.make_async_copy(codes, listed, sem)
     copy.start()
     line_features(planes * rows, points, line_feat)
@@ -261,19 +290,25 @@
     gots, refs = refs[: len(units)], refs[len(units) :]
     corner, items, line_feat, codes, listed, got, sem = refs
     slab, slabs = lax.axis_index("slab"), lax.axis_size("slab")
-    value = gots[-1][pl.ds(bases[-1], 4 * lent), :]
+    value = gots[-1][pl.ds(bases[-1], 3 * lent), :]
     for unit, base, ref in list(zip(units, bases, gots))[:-1]:
-        value = jnp.where(is_heavy(slab ^ unit, slabs), ref[pl.ds(base, 4 * lent), :], value)
+        value = jnp.where(is_heavy(slab ^ unit, slabs), ref[pl.ds(base, 3 * lent), :], value)
+    number = [
+        value[i * lent : i * lent + 1, y * slots : (y + 1) * slots]
+        for i in range(lent // rows)
+        for y in range(rows)
+    ]
+    number = jnp.concatenate([corner[3:4, 0:slots]] + number[1:], axis=0)
     got[...] = value
-    for c in range(4):
+    for c in range(3):
         got[c * lent : c * lent + 1, :] = corner[c : c + 1, :]
     helps = jnp.logical_not(is_heavy(slab, slabs))
-    number = got[3 * lent :, 0:slots].astype(jnp.int32)
-    count = got[3 * lent :, slots : slots + 1].astype(jnp.int32)
-    line = lax.broadcasted_iota(jnp.int32, count.shape, 0)
-    count = jnp.where((helps & (lax.rem(line, rows) >= 1)) | (line == 0), count, 0)
-    codes[:, 0:slots] = coded(first, bits, placed, number, count)
-    codes[:, slots : slots + 1] = count
+    line = lax.broadcasted_iota(jnp.int32, number.shape, 0)
+    taken = (helps & ((lax.rem(line, rows) >= 1) | (line == rows))) | (line == 0)
+    number = jnp.where(taken, number, 0.0)
+    count = jnp.sum(jnp.where(number > 0.0, 1.0, 0.0), axis=1, keepdims=True).astype(jnp.int32)
+    number = jnp.maximum(number - 1.0, 0.0).astype(jnp.int32)
+    code_items(first, bits, placed, number, count, codes)
     copy = pltpu.make_async_copy(codes, listed, sem)
     copy.start()
     line_features(lent, got, line_feat)
@@ -286,7 +321,7 @@
     return pl.pallas_call(
         kernel,
         out_shape=(
-            jax.ShapeDtypeStruct((2 * length + 2,), jnp.int32),
+            jax.ShapeDtypeStruct((2 * length + 3,), jnp.int32),
             jax.ShapeDtypeStruct((lines * FEATS, depth), BF16),
             *more,
         ),
@@ -310,7 +345,7 @@
         line_feat[at : at + feat.shape[0], :] = feat[...]
         at += feat.shape[0]
     line_feat[at:, :] = jnp.zeros((line_feat.shape[0] - at, line_feat.shape[1]), BF16)
-    middles = [items.shape[0] // 2 - 1 for items in lists]
+    middles = [(items.shape[0] - 3) // 2 for items in lists]
     starts = [middle * half for middle in middles]
     first = lists[0][2 * middles[0] + half]
     count = sum(items[2 * middle + half] for items, middle in zip(lists, middles))
@@ -334,7 +369,7 @@
         code = lists[0][starts[0] + jnp.minimum(at, first)]
         other = lists[1][starts[1] + jnp.maximum(at - first, 0)]
         code = jnp.where(at < first, code, other)
-        return lax.shift_right_logical(code, bits), code & mask
+        return lax.shift_right_logical(code & 0xFFFF, bits), code & mask
 
     def distances(u, at):
         line, tile = unpack(at)
@@ -473,6 +508,10 @@
                         if backs and x >= keep:
                             back = backs[(x - keep) // share]
                             moved = jnp.where(from_helper, back[c, (x - keep) % share], moved)
+                        if x == 1:
+                            for turn, back in enumerate(backs):
+                                here_too = from_helper & (row_id == 1 + turn)
+                                moved = jnp.where(here_too, back[c, 1, 0:1, :], moved)
                         out_shift[c, x] = moved
                         here = here + moved
                     edge = row_halo[field, c, x : x + 1, :]
@@ -539,8 +578,8 @@
     unit = slabs // 8
     share = (planes - 1) // 3
     keep = planes - 3 * share
-    lend = slabs % 8 == 0 and slabs & (slabs - 1) == 0 and share > 0
-    assert lend, (slabs, planes)
+    lend = slabs % 8 == 0 and slabs & (slabs - 1) == 0 and share > 1 and keep > 1 and rows > 4
+    assert lend and share <= 3 and rows * slots <= TILE, (slabs, planes, rows, slots)
     units = (4 * unit, 2 * unit, unit) if lend else ()
     spans = [tuple(range(keep + g * share, keep + (g + 1) * share)) for g in range(len(units))]
     lent = share * rows if lend else 0
@@ -572,8 +611,8 @@
 
     flat_points = node_points.reshape(3 * own, depth)
     *own_lists, last_sent = prepared(
-        functools.partial(own_kernel, keep, bits, placed, spans[-1]),
-        own, slots, depth, [jax.ShapeDtypeStruct((4 * lent, TILE), F32)], [],
+        functools.partial(own_kernel, keep, len(units), bits, placed, spans[-1]),
+        own, slots, depth, [jax.ShapeDtypeStruct((3 * lent, TILE), F32)], [],
         flat_points, tile_list, tile_count,
     )
 
@@ -581,7 +620,7 @@
         kernel = functools.partial(
             lent_kernel, own, rows, slots, lent, bits, placed, units, tuple(bases)
         )
-        scratch = [pltpu.VMEM((4 * lent, TILE), F32)]
+        scratch = [pltpu.VMEM((3 * lent, TILE), F32)]
         return prepared(kernel, lent, slots, depth, [], scratch, *gots, corner)
 
     gots, bases = [], []
@@ -591,7 +630,7 @@
             functools.partial(pack_kernel, spans[:-1]),
             out_shape=[
                 jax.ShapeDtypeStruct((rows_of, TILE), F32)
-                for rows_of in [8, size + 4 * lent] + [4 * lent] * (len(units) - 2)
+                for rows_of in [8, size + 3 * lent] + [3 * lent] * (len(units) - 2)
             ],
             in_specs=[vmem()] * 8,
             out_specs=[vmem()] * len(units),
@@ -621,7 +660,6 @@
                 reply = swapped(early, slab_bit, ctrl_bit)
             early = jnp.concatenate([early, reply], axis=0)
         lent_lists = borrowed(gots, bases)
-        early, lent_lists = lax.optimization_barrier((early, lent_lists))
         late = swapped(early, *order[-1])
     else:
         loads = pl.pallas_call(
@@ -640,7 +678,7 @@
         corner, *sents = pl.pallas_call(
             functools.partial(lend_kernel, spans),
             out_shape=[jax.ShapeDtypeStruct((8, TILE), F32)]
-            + [jax.ShapeDtypeStruct((4 * lent, TILE), F32)] * len(units),
+            + [jax.ShapeDtypeStruct((3 * lent, TILE), F32)] * len(units),
             in_specs=[vmem()] * 3,
             out_specs=[vmem()] * (1 + len(units)),
         )(flat_points, tile_list, tile_count)

time: 58.9 us -> 56.2 us (0.954)
  starting transfers between devices: 20.1 us -> 18.1 us
    ppermute x3, starting transfers between devices: 7.4 us -> 5.16 us  [local(): lax.ppermute(lent_shift, 'slab', [(h ^ bit, h) for h in heavy])]
    pallas_call x1, Pallas kernels: 9.72 us -> 10.4 us  [local(): pl.pallas_call(functools.partial(late_kernel, own, lent, parts, bits), ou...]
    pallas_call x2, Pallas kernels: 6.44 us -> 5.78 us  [prepared(): pl.pallas_call(kernel, out_shape=(jax.ShapeDtypeStruct((2 * length + 3,),...]
  transfers between devices with their start and end apart: 11 -> 11, of which waited for: 5 -> 5; matrix products, arithmetic and copies ran while one was open for 2% -> 2% of each run, Pallas kernels for 27% -> 26%
where the time goes in v6:
time: 56.2 us; the launch traced here: 55.9 us
  Pallas kernels  27.7 us (49%)
  starting transfers between devices  18.1 us (32%)
  waiting for transfers between devices  7.85 us (14%)
  local copies, waits for them, and re-layouts  1.37 us (2%)
  between operations  0.84 us (1%)
    pallas_call x1, Pallas kernels, local(): pl.pallas_call(functools.partial(late_kernel, own, lent, parts, bits), ou...  10.4 us
    ppermute x5, starting transfers between devices, swapped(): return lax.ppermute(value, ('slab', 'ctrl'), pairs)  9.06 us
    pallas_call x1, Pallas kernels, local(): pl.pallas_call(functools.partial(early_kernel, parts, bits), out_shape=(j...  8.86 us
    pallas_call x2, Pallas kernels, prepared(): pl.pallas_call(kernel, out_shape=(jax.ShapeDtypeStruct((2 * length + 3,),...  5.78 us
    ppermute x5, waiting for transfers between devices, swapped(): return lax.ppermute(value, ('slab', 'ctrl'), pairs)  5.16 us
    ppermute x3, starting transfers between devices, local(): lax.ppermute(lent_shift, 'slab', [(h ^ bit, h) for h in heavy])  5.16 us
    ppermute x3, starting transfers between devices, shifted_back(): lax.ppermute(value, axis, [(i, i - 1) for i in range(1, lax.axis_size(axi...  3.86 us
    ppermute x3, waiting for transfers between devices, shifted_back(): lax.ppermute(value, axis, [(i, i - 1) for i in range(1, lax.axis_size(axi...  2.68 us
  transfers between devices with their start and end apart: 11, of which 5 were waited for; matrix products, arithmetic and copies ran while one was open for 2% of the time, Pallas kernels for 26%

profile of v6, /device:TPU:0, one launch (start us, length us, event | category | flops | bytes accessed | tf_op | source)
XLA Modules:
  0.0 55.9 jit_solution(3886978061455941841)
XLA Ops:
  0.6 1.8 %shard_map.129 = (f32[8,128]{1,0:T(8,128)}, f32[96,128]{1,0:T(8,128)}, f32[48,128]{1,0:T(8,128)}) custom-call(f32[1,4096]{1,0:T(1,128)} %bitcast.21, f32[3,4096]{1,0:T(4,128)} %area.1, f32[3,4096]{1,0:T(4,128)} %center.1, f32[3,256]{1,0:T(4,128)} %points.2, f32[18,256]{1,0:T(8,128)} %modes.1, f32[192,128]{1,0:T(8,128)} %bitcast.13, s32[8,8,16]{2,1,0:T(8,128)} %numbers.3, ...), custom_call_target="tpu_custom_call" | custom-call | tf_op jit(solution)/shard_map/pallas_call | solution.py:629
  2.4 4.0 %collective-permute-start = (f32[96,128]{1,0:T(8,128)}, f32[96,128]{1,0:T(8,128)S(1)}, u32[]{:S(2)}, u32[]{:S(2)}) collective-permute-start(f32[96,128]{1,0:T(8,128)} %get-tuple-element.28), channel_id=1, source_target_pairs={{0,16},{1,17},{2,18},{3,19},{4,20},{5,21},{6,22},{7,23},{8,24},{9,... | collective-permute-start | bytes 147464 | tf_op jit(solution)/shard_map/ppermute | solution.py:41
  6.5 0.0 copy-start.3
  6.5 0.8 %slice.15 = f32[48,128]{1,0:T(8,128)S(1)} slice(f32[96,128]{1,0:T(8,128)} %get-tuple-element.28), slice={[0:48], [0:128]} | slice | bytes 49152 | tf_op jit(solution)/shard_map/slice | solution.py:643
  7.2 0.0 copy-start
  7.2 2.0 %collective-permute-done.refs_0_ = f32[96,128]{1,0:T(8,128)S(1)} collective-permute-done((f32[96,128]{1,0:T(8,128)}, f32[96,128]{1,0:T(8,128)S(1)}, u32[]{:S(2)}, u32[]{:S(2)}) %collective-permute-start) | collective-permute-done | bytes 49184 | tf_op jit(solution)/shard_map/ppermute | solution.py:41
  9.3 0.0 copy-done.3
  9.3 0.0 copy-start.1
  9.3 0.0 copy-start.2
  9.3 1.4 %collective-permute-start.1 = (f32[144,128]{1,0:T(8,128)S(1)}, f32[144,128]{1,0:T(8,128)S(1)}, u32[]{:S(2)}, u32[]{:S(2)}) collective-permute-start(f32[144,128]{1,0:T(8,128)S(1)} %pad_maximum_fusion.3), channel_id=1, source_target_pairs={{0,8},{1,9},{2,10},{3,11},{4,12},{5,13},{6,14},{7,15},{8,0},{9,1},... | collective-permute-start | bytes 221192 | tf_op jit(solution)/shard_map/ppermute | solution.py:41
  10.8 0.0 copy-done
  10.8 0.0 copy-done.1
  10.8 0.0 copy-done.2
  10.8 3.5 %shard_map.130 = (s32[2115]{0:T(1024)S(1)}, bf16[2048,128]{1,0:T(8,128)(2,1)S(1)}, f32[48,128]{1,0:T(8,128)S(1)}) custom-call(f32[192,128]{1,0:T(8,128)S(1)} %bitcast.14, s32[8,8,16]{2,1,0:T(8,128)S(1)} %copy-done.1, s32[8,8]{1,0:T(8,128)S(1)} %copy-done.2), custom_call_target="tpu_custom_call" | custom-call | bytes 8000000 | tf_op jit(solution)/shard_map/pallas_call | solution.py:321
  14.3 0.0 collective-permute-done.1.refs_1_
  14.3 0.0 copy-start.6
  14.4 1.6 %collective-permute-start.2 = (f32[240,128]{1,0:T(8,128)S(1)}, f32[240,128]{1,0:T(8,128)S(1)}, u32[]{:S(2)}, u32[]{:S(2)}) collective-permute-start(f32[240,128]{1,0:T(8,128)S(1)} %pad_maximum_fusion.1), channel_id=1, source_target_pairs={{0,4},{1,5},{2,6},{3,7},{4,0},{5,1},{6,2},{7,3},{8,12},{9,13},{10,... | collective-permute-start | bytes 368648 | tf_op jit(solution)/shard_map/ppermute | solution.py:41
  15.9 0.0 copy-done.6
  15.9 1.3 %collective-permute-start.3 = (f32[8,128]{1,0:T(8,128)S(1)}, f32[8,128]{1,0:T(8,128)S(1)}, u32[]{:S(2)}, u32[]{:S(2)}) collective-permute-start(f32[8,128]{1,0:T(8,128)S(1)} %copy-done.6), channel_id=1, source_target_pairs={{1,0},{2,1},{3,2},{5,4},{6,5},{7,6},{9,8},{10,9},{11,10},{13,12},{... | collective-permute-start | bytes 12296 | tf_op jit(solution)/shard_map/ppermute | solution.py:45
  17.2 2.1 %collective-permute-done.2.refs_2_ = f32[240,128]{1,0:T(8,128)S(1)} collective-permute-done((f32[240,128]{1,0:T(8,128)S(1)}, f32[240,128]{1,0:T(8,128)S(1)}, u32[]{:S(2)}, u32[]{:S(2)}) %collective-permute-start.2) | collective-permute-done | bytes 122912 | tf_op jit(solution)/shard_map/ppermute | solution.py:41
  19.3 0.0 collective-permute-done.3.refs_3_.refs_8_
  19.3 1.4 %collective-permute-start.4 = (f32[384,128]{1,0:T(8,128)S(1)}, f32[384,128]{1,0:T(8,128)S(1)}, u32[]{:S(2)}, u32[]{:S(2)}) collective-permute-start(f32[384,128]{1,0:T(8,128)S(1)} %pad_maximum_fusion), channel_id=1, source_target_pairs={{0,1},{1,0},{2,3},{3,2},{4,5},{5,4},{6,7},{7,6},{8,9},{9,8},{10,11... | collective-permute-start | bytes 589832 | tf_op jit(solution)/shard_map/ppermute | solution.py:41
  20.7 0.0 copy-start.4
  20.8 0.0 copy-start.5
  20.8 1.0 %collective-permute-done.4 = f32[384,128]{1,0:T(8,128)S(1)} collective-permute-done((f32[384,128]{1,0:T(8,128)S(1)}, f32[384,128]{1,0:T(8,128)S(1)}, u32[]{:S(2)}, u32[]{:S(2)}) %collective-permute-start.4) | collective-permute-done | bytes 196640 | tf_op jit(solution)/shard_map/ppermute | solution.py:41
  21.8 0.6 %collective-permute-start.5 = (f32[768,128]{1,0:T(8,128)S(1)}, f32[768,128]{1,0:T(8,128)S(1)}, u32[]{:S(2)}, u32[]{:S(2)}) collective-permute-start(f32[768,128]{1,0:T(8,128)S(1)} %constant_dynamic-update-slice_fusion.refs_4_), channel_id=1, source_target_pairs={{0,2},{1,3},{2,0},{3,1},{4,6},{5,7},{6,4},{7,5},{8,10},{9,11},{10,... | collective-permute-start | bytes 1179656 | tf_op jit(solution)/shard_map/ppermute | solution.py:41
  22.5 0.0 copy-done.4
  22.5 0.0 copy-done.5
  22.5 2.3 %shard_map.131 = (s32[579]{0:T(1024)S(1)}, bf16[512,128]{1,0:T(8,128)(2,1)S(1)}) custom-call(f32[96,128]{1,0:T(8,128)S(1)} %collective-permute-done.refs_0_, f32[144,128]{1,0:T(8,128)S(1)} %collective-permute-done.1.refs_1_, f32[240,128]{1,0:T(8,128)S(1)} %collective-permute-done.2.refs_2_, f32[8,128]{1,0:T(8,128)S(1)} %collective-permute-done.3.refs_3_.refs_8_), custom_call_target="tpu_custom_call" | custom-call | bytes 8000000 | tf_op jit(solution)/shard_map/pallas_call | solution.py:321
  24.7 8.9 %shard_map.132 = (f32[1944,128]{1,0:T(8,128)S(1)}, f32[1,128]{1,0:T(1,128)S(1)}) custom-call(s32[2115]{0:T(1024)S(1)} %get-tuple-element.33.refs_0_, s32[579]{0:T(1024)S(1)} %get-tuple-element.38.refs_1_, bf16[2048,128]{1,0:T(8,128)(2,1)S(1)} %get-tuple-element.39.refs_2_, bf16[512,128]{1,0:T(8,128)(2,1)S(1)} %get-tuple-element.40.refs_3_, ...), custom_call_target="tpu_custom_call" | custom-call | bytes 30000000 | tf_op jit(solution)/shard_map/pallas_call | solution.py:705
  33.6 0.0 collective-permute-done.5.refs_4_
  33.6 10.4 %shard_map.133 = (f32[192,128]{1,0:T(8,128)S(1)}, f32[48,128]{1,0:T(8,128)S(1)}, f32[1,128]{1,0:T(1,128)S(1)}, f32[2,24,128]{2,1,0:T(8,128)S(1)}, f32[2,32,128]{2,1,0:T(8,128)S(1)}) custom-call(s32[2115]{0:T(1024)S(1)} %get-tuple-element.33.refs_0_, s32[579]{0:T(1024)S(1)} %get-tuple-element.38.refs_1_, bf16[2048,128]{1,0:T(8,128)(2,1)S(1)} %get-tuple-element.39.refs_2_, ...), custom_call_target="tpu_custom_call" | custom-call | tf_op jit(solution)/shard_map/pallas_call | solution.py:717
  44.0 3.8 %collective-permute-start.6 = (f32[48,128]{1,0:T(8,128)S(1)}, f32[48,128]{1,0:T(8,128)S(1)}, u32[]{:S(2)}, u32[]{:S(2)}) collective-permute-start(f32[48,128]{1,0:T(8,128)S(1)} %get-tuple-element.45), channel_id=1, source_target_pairs={{28,12},{0,16},{29,13},{1,17},{30,14},{2,18},{31,15},{3,19}} | collective-permute-start | bytes 73736 | tf_op jit(solution)/shard_map/ppermute | solution.py:737
  47.9 0.7 %collective-permute-start.7 = (f32[48,128]{1,0:T(8,128)S(1)}, f32[48,128]{1,0:T(8,128)S(1)}, u32[]{:S(2)}, u32[]{:S(2)}) collective-permute-start(f32[48,128]{1,0:T(8,128)S(1)} %get-tuple-element.45), channel_id=1, source_target_pairs={{4,12},{24,16},{5,13},{25,17},{6,14},{26,18},{7,15},{27,19}} | collective-permute-start | bytes 73736 | tf_op jit(solution)/shard_map/ppermute | solution.py:737
  48.6 0.7 %collective-permute-start.8 = (f32[48,128]{1,0:T(8,128)S(1)}, f32[48,128]{1,0:T(8,128)S(1)}, u32[]{:S(2)}, u32[]{:S(2)}) collective-permute-start(f32[48,128]{1,0:T(8,128)S(1)} %get-tuple-element.45), channel_id=1, source_target_pairs={{8,12},{20,16},{9,13},{21,17},{10,14},{22,18},{11,15},{23,19}} | collective-permute-start | bytes 73736 | tf_op jit(solution)/shard_map/ppermute | solution.py:737
  49.2 1.3 %collective-permute-start.9 = (f32[2,32,128]{2,1,0:T(8,128)S(1)}, f32[2,32,128]{2,1,0:T(8,128)S(1)}, u32[]{:S(2)}, u32[]{:S(2)}) collective-permute-start(f32[2,32,128]{2,1,0:T(8,128)S(1)} %get-tuple-element.46), channel_id=1, source_target_pairs={{4,0},{8,4},{12,8},{16,12},{20,16},{24,20},{28,24},{5,1},{9,5},{13... | collective-permute-start | bytes 98312 | tf_op jit(solution)/shard_map/ppermute | solution.py:45
  50.5 1.3 %collective-permute-start.10 = (f32[2,24,128]{2,1,0:T(8,128)S(1)}, f32[2,24,128]{2,1,0:T(8,128)S(1)}, u32[]{:S(2)}, u32[]{:S(2)}) collective-permute-start(f32[2,24,128]{2,1,0:T(8,128)S(1)} %get-tuple-element.47), channel_id=1, source_target_pairs={{1,0},{2,1},{3,2},{5,4},{6,5},{7,6},{9,8},{10,9},{11,10},{13,12},{... | collective-permute-start | bytes 73736 | tf_op jit(solution)/shard_map/ppermute | solution.py:45
  51.8 0.5 slice_bitcast_fusion
  52.3 0.0 collective-permute-done.6
  52.3 0.0 collective-permute-done.7
  52.4 0.0 collective-permute-done.8
  52.4 1.3 %collective-permute-done.10 = f32[2,24,128]{2,1,0:T(8,128)S(1)} collective-permute-done((f32[2,24,128]{2,1,0:T(8,128)S(1)}, f32[2,24,128]{2,1,0:T(8,128)S(1)}, u32[]{:S(2)}, u32[]{:S(2)}) %collective-permute-start.10) | collective-permute-done | bytes 24608 | tf_op jit(solution)/shard_map/ppermute | solution.py:45
  53.6 1.4 %collective-permute-done.9.refs_3_ = f32[2,32,128]{2,1,0:T(8,128)S(1)} collective-permute-done((f32[2,32,128]{2,1,0:T(8,128)S(1)}, f32[2,32,128]{2,1,0:T(8,128)S(1)}, u32[]{:S(2)}, u32[]{:S(2)}) %collective-permute-start.9) | collective-permute-done | bytes 32800 | tf_op jit(solution)/shard_map/ppermute | solution.py:45
  55.0 0.9 %shard_map.134 = (f32[3,8,8,128]{3,2,1,0:T(8,128)}, f32[8,8,128]{2,1,0:T(8,128)}, f32[8,8,128]{2,1,0:T(8,128)}) custom-call(f32[3,8,8,128]{3,2,1,0:T(8,128)S(1)} %copy-done, f32[3,8,8,128]{3,2,1,0:T(8,128)S(1)} %bitcast.16, f32[3,2,8,128]{3,2,1,0:T(8,128)S(1)} %bitcast.17, f32[3,2,8,128]{3,2,1,0:T(8,128)S(1)} %bitcast.18, f32[3,2,8,128]{3,2,1,0:T(8,128)S(1)} %bitcast.19, ...), custom_call_target="tpu_custom_call" | custom-call | tf_op jit(solution)/shard_map/pallas_call | solution.py:744
  (10 shorter events, 0.1 us)
Async XLA Ops:
  2.4 6.8 %collective-permute-start = (f32[96,128]{1,0:T(8,128)}, f32[96,128]{1,0:T(8,128)S(1)}, u32[]{:S(2)}, u32[]{:S(2)}) collective-permute-start(f32[96,128]{1,0:T(8,128)} %get-tuple-element.28), channel_id=1, source_target_pairs={{0,16},{1,17},{2,18},{3,19},{4,20},{5,21},{6,22},{7,23},{8,24},{9,... | collective-permute-start | bytes 147464 | tf_op jit(solution)/shard_map/ppermute | solution.py:41
  6.5 2.8 %copy-start.3 = (f32[48,128]{1,0:T(8,128)S(1)}, f32[48,128]{1,0:T(8,128)}, u32[]{:S(2)}) copy-start(f32[48,128]{1,0:T(8,128)} %get-tuple-element.29) | copy-start | bytes 73732
  7.2 3.5 %copy-start = (f32[3,8,8,128]{3,2,1,0:T(8,128)S(1)}, f32[3,8,8,128]{3,2,1,0:T(8,128)}, u32[]{:S(2)}) copy-start(f32[3,8,8,128]{3,2,1,0:T(8,128)} %points.3) | copy-start | bytes 294916
  9.3 1.5 %copy-start.1 = (s32[8,8,16]{2,1,0:T(8,128)S(1)}, s32[8,8,16]{2,1,0:T(8,128)}, u32[]{:S(2)}) copy-start(s32[8,8,16]{2,1,0:T(8,128)} %numbers.3) | copy-start | bytes 12292
  9.3 1.5 %copy-start.2 = (s32[8,8]{1,0:T(8,128)S(1)}, s32[8,8]{1,0:T(8,128)}, u32[]{:S(2)}) copy-start(s32[8,8]{1,0:T(8,128)} %counts.3) | copy-start | bytes 772
  9.3 5.0 %collective-permute-start.1 = (f32[144,128]{1,0:T(8,128)S(1)}, f32[144,128]{1,0:T(8,128)S(1)}, u32[]{:S(2)}, u32[]{:S(2)}) collective-permute-start(f32[144,128]{1,0:T(8,128)S(1)} %pad_maximum_fusion.3), channel_id=1, source_target_pairs={{0,8},{1,9},{2,10},{3,11},{4,12},{5,13},{6,14},{7,15},{8,0},{9,1},... | collective-permute-start | bytes 221192 | tf_op jit(solution)/shard_map/ppermute | solution.py:41
  14.3 1.6 %copy-start.6 = (f32[8,128]{1,0:T(8,128)S(1)}, f32[8,128]{1,0:T(8,128)}, u32[]{:S(2)}) copy-start(f32[8,128]{1,0:T(8,128)} %get-tuple-element.36) | copy-start | bytes 12292
  14.4 4.9 %collective-permute-start.2 = (f32[240,128]{1,0:T(8,128)S(1)}, f32[240,128]{1,0:T(8,128)S(1)}, u32[]{:S(2)}, u32[]{:S(2)}) collective-permute-start(f32[240,128]{1,0:T(8,128)S(1)} %pad_maximum_fusion.1), channel_id=1, source_target_pairs={{0,4},{1,5},{2,6},{3,7},{4,0},{5,1},{6,2},{7,3},{8,12},{9,13},{10,... | collective-permute-start | bytes 368648 | tf_op jit(solution)/shard_map/ppermute | solution.py:41
  15.9 3.4 %collective-permute-start.3 = (f32[8,128]{1,0:T(8,128)S(1)}, f32[8,128]{1,0:T(8,128)S(1)}, u32[]{:S(2)}, u32[]{:S(2)}) collective-permute-start(f32[8,128]{1,0:T(8,128)S(1)} %copy-done.6), channel_id=1, source_target_pairs={{1,0},{2,1},{3,2},{5,4},{6,5},{7,6},{9,8},{10,9},{11,10},{13,12},{... | collective-permute-start | bytes 12296 | tf_op jit(solution)/shard_map/ppermute | solution.py:45
  19.3 2.5 %collective-permute-start.4 = (f32[384,128]{1,0:T(8,128)S(1)}, f32[384,128]{1,0:T(8,128)S(1)}, u32[]{:S(2)}, u32[]{:S(2)}) collective-permute-start(f32[384,128]{1,0:T(8,128)S(1)} %pad_maximum_fusion), channel_id=1, source_target_pairs={{0,1},{1,0},{2,3},{3,2},{4,5},{5,4},{6,7},{7,6},{8,9},{9,8},{10,11... | collective-permute-start | bytes 589832 | tf_op jit(solution)/shard_map/ppermute | solution.py:41
  20.7 1.7 %copy-start.4 = (f32[6]{0:T(128)S(1)}, f32[6]{0:T(128)}, u32[]{:S(2)}) copy-start(f32[6]{0:T(128)} %param.14) | copy-start | bytes 76
  20.8 1.7 %copy-start.5 = (f32[6]{0:T(128)S(1)}, f32[6]{0:T(128)}, u32[]{:S(2)}) copy-start(f32[6]{0:T(128)} %param.13) | copy-start | bytes 76
  21.8 11.8 %collective-permute-start.5 = (f32[768,128]{1,0:T(8,128)S(1)}, f32[768,128]{1,0:T(8,128)S(1)}, u32[]{:S(2)}, u32[]{:S(2)}) collective-permute-start(f32[768,128]{1,0:T(8,128)S(1)} %constant_dynamic-update-slice_fusion.refs_4_), channel_id=1, source_target_pairs={{0,2},{1,3},{2,0},{3,1},{4,6},{5,7},{6,4},{7,5},{8,10},{9,11},{10,... | collective-permute-start | bytes 1179656 | tf_op jit(solution)/shard_map/ppermute | solution.py:41
  44.0 8.3 %collective-permute-start.6 = (f32[48,128]{1,0:T(8,128)S(1)}, f32[48,128]{1,0:T(8,128)S(1)}, u32[]{:S(2)}, u32[]{:S(2)}) collective-permute-start(f32[48,128]{1,0:T(8,128)S(1)} %get-tuple-element.45), channel_id=1, source_target_pairs={{28,12},{0,16},{29,13},{1,17},{30,14},{2,18},{31,15},{3,19}} | collective-permute-start | bytes 73736 | tf_op jit(solution)/shard_map/ppermute | solution.py:737
  47.9 4.5 %collective-permute-start.7 = (f32[48,128]{1,0:T(8,128)S(1)}, f32[48,128]{1,0:T(8,128)S(1)}, u32[]{:S(2)}, u32[]{:S(2)}) collective-permute-start(f32[48,128]{1,0:T(8,128)S(1)} %get-tuple-element.45), channel_id=1, source_target_pairs={{4,12},{24,16},{5,13},{25,17},{6,14},{26,18},{7,15},{27,19}} | collective-permute-start | bytes 73736 | tf_op jit(solution)/shard_map/ppermute | solution.py:737
  48.6 3.8 %collective-permute-start.8 = (f32[48,128]{1,0:T(8,128)S(1)}, f32[48,128]{1,0:T(8,128)S(1)}, u32[]{:S(2)}, u32[]{:S(2)}) collective-permute-start(f32[48,128]{1,0:T(8,128)S(1)} %get-tuple-element.45), channel_id=1, source_target_pairs={{8,12},{20,16},{9,13},{21,17},{10,14},{22,18},{11,15},{23,19}} | collective-permute-start | bytes 73736 | tf_op jit(solution)/shard_map/ppermute | solution.py:737
  49.2 5.8 %collective-permute-start.9 = (f32[2,32,128]{2,1,0:T(8,128)S(1)}, f32[2,32,128]{2,1,0:T(8,128)S(1)}, u32[]{:S(2)}, u32[]{:S(2)}) collective-permute-start(f32[2,32,128]{2,1,0:T(8,128)S(1)} %get-tuple-element.46), channel_id=1, source_target_pairs={{4,0},{8,4},{12,8},{16,12},{20,16},{24,20},{28,24},{5,1},{9,5},{13... | collective-permute-start | bytes 98312 | tf_op jit(solution)/shard_map/ppermute | solution.py:45
  50.5 3.1 %collective-permute-start.10 = (f32[2,24,128]{2,1,0:T(8,128)S(1)}, f32[2,24,128]{2,1,0:T(8,128)S(1)}, u32[]{:S(2)}, u32[]{:S(2)}) collective-permute-start(f32[2,24,128]{2,1,0:T(8,128)S(1)} %get-tuple-element.47), channel_id=1, source_target_pairs={{1,0},{2,1},{3,2},{5,4},{6,5},{7,6},{9,8},{10,9},{11,10},{13,12},{... | collective-permute-start | bytes 73736 | tf_op jit(solution)/shard_map/ppermute | solution.py:45

commit v7 on v6

--- a/solution.py
+++ b/solution.py
@@ -12,7 +12,7 @@
 GRAVITY = (0.0, 0.0, -0.5, 0.0, 0.0, 0.0)
 ROWS = 24
 FEATS = 32
-UNROLL = 16
+UNROLL = 20
 MIX = 48
 TINY = 1e-30
 F32 = jnp.float32
@@ -284,11 +284,7 @@
     build_lists(planes * rows, slots, bits, 0, listed, items)
 
 
-def lent_kernel(
-    first, rows, slots, lent, bits, placed, units, bases, *refs
-):
-    gots, refs = refs[: len(units)], refs[len(units) :]
-    corner, items, line_feat, codes, listed, got, sem = refs
+def read_lent(first, rows, slots, lent, bits, placed, units, bases, gots, corner, got, codes):
     slab, slabs = lax.axis_index("slab"), lax.axis_size("slab")
     value = gots[-1][pl.ds(bases[-1], 3 * lent), :]
     for unit, base, ref in list(zip(units, bases, gots))[:-1]:
@@ -309,11 +305,6 @@
     count = jnp.sum(jnp.where(number > 0.0, 1.0, 0.0), axis=1, keepdims=True).astype(jnp.int32)
     number = jnp.maximum(number - 1.0, 0.0).astype(jnp.int32)
     code_items(first, bits, placed, number, count, codes)
-    copy = pltpu.make_async_copy(codes, listed, sem)
-    copy.start()
-    line_features(lent, got, line_feat)
-    copy.wait()
-    build_lists(lent, slots, bits, first, listed, items)
 
 
 def prepared(kernel, lines, slots, depth, more, scratch, *operands):
@@ -338,17 +329,13 @@
     )(*operands)
 
 
-def add_items(bits, half, lists, table, feats, line_feat, tile_feat, modes, acc, squares):
+def add_items(bits, half, lists, table, feats, line_feat, tile_feat, modes, acc, squares, ready):
     tiles = table.shape[0] // ROWS
     at = 0
     for feat in feats:
         line_feat[at : at + feat.shape[0], :] = feat[...]
         at += feat.shape[0]
     line_feat[at:, :] = jnp.zeros((line_feat.shape[0] - at, line_feat.shape[1]), BF16)
-    middles = [(items.shape[0] - 3) // 2 for items in lists]
-    starts = [middle * half for middle in middles]
-    first = lists[0][2 * middles[0] + half]
-    count = sum(items[2 * middle + half] for items, middle in zip(lists, middles))
 
     def build(t, carry):
         base = pl.multiple_of(t * ROWS, 8)
@@ -364,6 +351,11 @@
 
     lax.fori_loop(0, tiles, build, 0, unroll=4)
     mask = tiles - 1
+    ready()
+    middles = [(items.shape[0] - 3) // 2 for items in lists]
+    starts = [middle * half for middle in middles]
+    first = lists[0][2 * middles[0] + half]
+    count = sum(items[2 * middle + half] for items, middle in zip(lists, middles))
 
     def unpack(at):
         code = lists[0][starts[0] + jnp.minimum(at, first)]
@@ -414,12 +406,26 @@
     return jnp.sum(table[pl.ds(7, tiles, stride=ROWS), :], axis=0, keepdims=True)
 
 
-def early_kernel(parts, bits, *refs):
-    lists, feats = refs[:parts], refs[parts : 2 * parts]
-    table, acc, loads, line_feat, tile_feat, modes, *squares = refs[2 * parts :]
+def early_kernel(own, rows, slots, lent, bits, placed, units, bases, *refs):
+    own_items, own_feat, *refs = refs
+    gots, refs = refs[: len(units)], refs[len(units) :]
+    corner, table, acc, loads, items, lent_feat, *refs = refs
+    line_feat, tile_feat, modes, codes, listed, got, sem, *squares = refs
+    read_lent(own, rows, slots, lent, bits, placed, units, bases, gots, corner, got, codes)
+    copy = pltpu.make_async_copy(codes, listed, sem)
+    copy.start()
+    line_features(lent, got, lent_feat)
     acc[...] = jnp.zeros(acc.shape, F32)
     loads[...] = load_sum(table)
-    add_items(bits, 0, lists, table, feats, line_feat, tile_feat, modes, acc, squares)
+
+    def ready():
+        copy.wait()
+        build_lists(lent, slots, bits, own, listed, items)
+
+    add_items(
+        bits, 0, (own_items, items), table, (own_feat, lent_feat),
+        line_feat, tile_feat, modes, acc, squares, ready,
+    )
 
 
 def late_kernel(own, lent, parts, bits, *refs):
@@ -441,7 +447,9 @@
     weight = jnp.broadcast_to(jnp.sum(chosen, axis=1, keepdims=True), (8, 128))
 
     acc[...] = early[...]
-    add_items(bits, 1, lists, table, feats, line_feat, tile_feat, modes, acc, squares)
+    add_items(
+        bits, 1, lists, table, feats, line_feat, tile_feat, modes, acc, squares, lambda: None
+    )
 
     def finish(count, first, out):
         def one(l, carry):
@@ -615,13 +623,6 @@
         own, slots, depth, [jax.ShapeDtypeStruct((3 * lent, TILE), F32)], [],
         flat_points, tile_list, tile_count,
     )
-
-    def borrowed(gots, bases):
-        kernel = functools.partial(
-            lent_kernel, own, rows, slots, lent, bits, placed, units, tuple(bases)
-        )
-        scratch = [pltpu.VMEM((3 * lent, TILE), F32)]
-        return prepared(kernel, lent, slots, depth, [], scratch, *gots, corner)
 
     gots, bases = [], []
     if direct:
@@ -659,7 +660,6 @@
             else:
                 reply = swapped(early, slab_bit, ctrl_bit)
             early = jnp.concatenate([early, reply], axis=0)
-        lent_lists = borrowed(gots, bases)
         late = swapped(early, *order[-1])
     else:
         loads = pl.pallas_call(
@@ -684,36 +684,48 @@
         )(flat_points, tile_list, tile_count)
         corner = shifted_back(corner, "ctrl")
         gots = [swapped(sent, bit, 0) for sent, bit in zip(sents, units)]
-        lent_lists = borrowed(gots, [0] * len(units))
-    groups = [own_lists, lent_lists]
+        bases = [0] * len(units)
     lines = own + lent
 
     def wide(value):
         return jnp.pad(value, (0, TILE - value.shape[0])).reshape(1, TILE)
 
     half = tiles // 2
-    parts = len(groups)
-    lists = [group[0] for group in groups]
-    feats = [group[1] for group in groups]
-    list_specs = [smem()] * parts + [vmem()] * parts
+    length = lent * slots + 2 * UNROLL
     scratch = [
         pltpu.VMEM(((lines + 1) * FEATS, depth), BF16),
         pltpu.VMEM((half * TILE, FEATS), BF16),
         pltpu.VMEM((half * MIX, TILE), BF16),
     ]
     squares = [pltpu.VMEM((TILE, depth), F32)] * UNROLL
-    partial, part_loads = pl.pallas_call(
-        functools.partial(early_kernel, parts, bits),
+    partial, part_loads, *lent_lists = pl.pallas_call(
+        functools.partial(
+            early_kernel, own, rows, slots, lent, bits, placed, units, tuple(bases)
+        ),
         out_shape=(
             jax.ShapeDtypeStruct(((lines + 1) * ROWS, depth), F32),
             jax.ShapeDtypeStruct((1, TILE), F32),
-        ),
-        in_specs=list_specs + [vmem()],
-        out_specs=(vmem(), vmem()),
-        scratch_shapes=scratch + squares,
+            jax.ShapeDtypeStruct((2 * length + 3,), jnp.int32),
+            jax.ShapeDtypeStruct((lent * FEATS, depth), BF16),
+        ),
+        in_specs=[smem()] + [vmem()] * (3 + len(units)),
+        out_specs=(vmem(), vmem(), smem(), vmem()),
+        scratch_shapes=scratch
+        + [
+            pltpu.VMEM((lent, TILE), jnp.int32),
+            pltpu.SMEM((lent, TILE), jnp.int32),
+            pltpu.VMEM((3 * lent, TILE), F32),
+            pltpu.SemaphoreType.DMA,
+        ]
+        + squares,
         compiler_params=limited(16),
         cost_estimate=pl.CostEstimate(flops=0, bytes_accessed=30_000_000, transcendentals=0),
-    )(*lists, *feats, early)
+    )(*own_lists, *gots, corner, early)
+    groups = [own_lists, lent_lists]
+    parts = len(groups)
+    lists = [group[0] for group in groups]
+    feats = [group[1] for group in groups]
+    list_specs = [smem()] * parts + [vmem()] * parts
     outs = pl.pallas_call(
         functools.partial(late_kernel, own, lent, parts, bits),
         out_shape=(

time: 56.2 us -> 55.7 us (level)
  starting transfers between devices: 18.1 us -> 16.2 us
  Pallas kernels: 27.7 us -> 28.6 us
    pallas_call x1, Pallas kernels: 8.86 us -> 11.3 us  [local(): pl.pallas_call(functools.partial(early_kernel, own, rows, slots, lent, bi...]
    pallas_call x2 -> x1, Pallas kernels: 5.78 us -> 3.52 us  [prepared(): pl.pallas_call(kernel, out_shape=(jax.ShapeDtypeStruct((2 * length + 3,),...]
    ppermute x3, starting transfers between devices: 5.16 us -> 3.31 us  [local(): lax.ppermute(lent_shift, 'slab', [(h ^ bit, h) for h in heavy])]
    pallas_call x1, Pallas kernels: 10.4 us -> 11.1 us  [local(): pl.pallas_call(functools.partial(late_kernel, own, lent, parts, bits), ou...]
  transfers between devices with their start and end apart: 11 -> 11, of which waited for: 5 -> 5; matrix products, arithmetic and copies ran while one was open for 2% -> 2% of each run, Pallas kernels for 26% -> 27%
where the time goes in v7:
time: 55.7 us; the launch traced here: 54.9 us
  Pallas kernels  28.6 us (51%)
  starting transfers between devices  16.2 us (29%)
  waiting for transfers between devices  7.85 us (14%)
  local copies, waits for them, and re-layouts  1.37 us (2%)
  between operations  0.83 us (1%)
    pallas_call x1, Pallas kernels, local(): pl.pallas_call(functools.partial(early_kernel, own, rows, slots, lent, bi...  11.3 us
    pallas_call x1, Pallas kernels, local(): pl.pallas_call(functools.partial(late_kernel, own, lent, parts, bits), ou...  11.1 us
    ppermute x5, starting transfers between devices, swapped(): return lax.ppermute(value, ('slab', 'ctrl'), pairs)  9.06 us
    ppermute x5, waiting for transfers between devices, swapped(): return lax.ppermute(value, ('slab', 'ctrl'), pairs)  5.16 us
    ppermute x3, starting transfers between devices, shifted_back(): lax.ppermute(value, axis, [(i, i - 1) for i in range(1, lax.axis_size(axi...  3.86 us
    pallas_call x1, Pallas kernels, prepared(): pl.pallas_call(kernel, out_shape=(jax.ShapeDtypeStruct((2 * length + 3,),...  3.52 us
    ppermute x3, starting transfers between devices, local(): lax.ppermute(lent_shift, 'slab', [(h ^ bit, h) for h in heavy])  3.31 us
    ppermute x3, waiting for transfers between devices, shifted_back(): lax.ppermute(value, axis, [(i, i - 1) for i in range(1, lax.axis_size(axi...  2.68 us
  transfers between devices with their start and end apart: 11, of which 5 were waited for; matrix products, arithmetic and copies ran while one was open for 2% of the time, Pallas kernels for 27%

profile of v7, /device:TPU:0, one launch (start us, length us, event | category | flops | bytes accessed | tf_op | source)
XLA Modules:
  0.0 54.9 jit_solution(3421255808258354206)
XLA Ops:
  0.6 1.8 %shard_map.129 = (f32[8,128]{1,0:T(8,128)}, f32[96,128]{1,0:T(8,128)}, f32[48,128]{1,0:T(8,128)}) custom-call(f32[1,4096]{1,0:T(1,128)} %bitcast.21, f32[3,4096]{1,0:T(4,128)} %area.1, f32[3,4096]{1,0:T(4,128)} %center.1, f32[3,256]{1,0:T(4,128)} %points.2, f32[18,256]{1,0:T(8,128)} %modes.1, f32[192,128]{1,0:T(8,128)} %bitcast.13, s32[8,8,16]{2,1,0:T(8,128)} %numbers.3, ...), custom_call_target="tpu_custom_call" | custom-call | tf_op jit(solution)/shard_map/pallas_call | solution.py:630
  2.4 4.0 %collective-permute-start = (f32[96,128]{1,0:T(8,128)}, f32[96,128]{1,0:T(8,128)S(1)}, u32[]{:S(2)}, u32[]{:S(2)}) collective-permute-start(f32[96,128]{1,0:T(8,128)} %get-tuple-element.28), channel_id=1, source_target_pairs={{0,16},{1,17},{2,18},{3,19},{4,20},{5,21},{6,22},{7,23},{8,24},{9,... | collective-permute-start | bytes 147464 | tf_op jit(solution)/shard_map/ppermute | solution.py:41
  6.5 0.0 copy-start.3
  6.5 0.8 %slice.15 = f32[48,128]{1,0:T(8,128)S(1)} slice(f32[96,128]{1,0:T(8,128)} %get-tuple-element.28), slice={[0:48], [0:128]} | slice | bytes 49152 | tf_op jit(solution)/shard_map/slice | solution.py:644
  7.2 0.0 copy-start
  7.2 2.0 %collective-permute-done.refs_2_ = f32[96,128]{1,0:T(8,128)S(1)} collective-permute-done((f32[96,128]{1,0:T(8,128)}, f32[96,128]{1,0:T(8,128)S(1)}, u32[]{:S(2)}, u32[]{:S(2)}) %collective-permute-start) | collective-permute-done | bytes 49184 | tf_op jit(solution)/shard_map/ppermute | solution.py:41
  9.3 0.0 copy-done.3
  9.3 0.0 copy-start.1
  9.3 0.0 copy-start.2
  9.3 1.4 %collective-permute-start.1 = (f32[144,128]{1,0:T(8,128)S(1)}, f32[144,128]{1,0:T(8,128)S(1)}, u32[]{:S(2)}, u32[]{:S(2)}) collective-permute-start(f32[144,128]{1,0:T(8,128)S(1)} %pad_maximum_fusion.3), channel_id=1, source_target_pairs={{0,8},{1,9},{2,10},{3,11},{4,12},{5,13},{6,14},{7,15},{8,0},{9,1},... | collective-permute-start | bytes 221192 | tf_op jit(solution)/shard_map/ppermute | solution.py:41
  10.8 0.0 copy-done
  10.8 0.0 copy-done.1
  10.8 0.0 copy-done.2
  10.8 3.5 %shard_map.130 = (s32[2131]{0:T(1024)S(1)}, bf16[2048,128]{1,0:T(8,128)(2,1)S(1)}, f32[48,128]{1,0:T(8,128)S(1)}) custom-call(f32[192,128]{1,0:T(8,128)S(1)} %bitcast.14, s32[8,8,16]{2,1,0:T(8,128)S(1)} %copy-done.1, s32[8,8]{1,0:T(8,128)S(1)} %copy-done.2), custom_call_target="tpu_custom_call" | custom-call | bytes 8000000 | tf_op jit(solution)/shard_map/pallas_call | solution.py:312
  14.3 0.0 collective-permute-done.1.refs_3_
  14.3 0.0 copy-start.6
  14.4 1.6 %collective-permute-start.2 = (f32[240,128]{1,0:T(8,128)S(1)}, f32[240,128]{1,0:T(8,128)S(1)}, u32[]{:S(2)}, u32[]{:S(2)}) collective-permute-start(f32[240,128]{1,0:T(8,128)S(1)} %pad_maximum_fusion.1), channel_id=1, source_target_pairs={{0,4},{1,5},{2,6},{3,7},{4,0},{5,1},{6,2},{7,3},{8,12},{9,13},{10,... | collective-permute-start | bytes 368648 | tf_op jit(solution)/shard_map/ppermute | solution.py:41
  15.9 0.0 copy-done.6
  15.9 1.3 %collective-permute-start.3 = (f32[8,128]{1,0:T(8,128)S(1)}, f32[8,128]{1,0:T(8,128)S(1)}, u32[]{:S(2)}, u32[]{:S(2)}) collective-permute-start(f32[8,128]{1,0:T(8,128)S(1)} %copy-done.6), channel_id=1, source_target_pairs={{1,0},{2,1},{3,2},{5,4},{6,5},{7,6},{9,8},{10,9},{11,10},{13,12},{... | collective-permute-start | bytes 12296 | tf_op jit(solution)/shard_map/ppermute | solution.py:45
  17.2 2.1 %collective-permute-done.2.refs_4_ = f32[240,128]{1,0:T(8,128)S(1)} collective-permute-done((f32[240,128]{1,0:T(8,128)S(1)}, f32[240,128]{1,0:T(8,128)S(1)}, u32[]{:S(2)}, u32[]{:S(2)}) %collective-permute-start.2) | collective-permute-done | bytes 122912 | tf_op jit(solution)/shard_map/ppermute | solution.py:41
  19.3 0.0 collective-permute-done.3.refs_5_.refs_8_
  19.4 1.4 %collective-permute-start.4 = (f32[384,128]{1,0:T(8,128)S(1)}, f32[384,128]{1,0:T(8,128)S(1)}, u32[]{:S(2)}, u32[]{:S(2)}) collective-permute-start(f32[384,128]{1,0:T(8,128)S(1)} %pad_maximum_fusion), channel_id=1, source_target_pairs={{0,1},{1,0},{2,3},{3,2},{4,5},{5,4},{6,7},{7,6},{8,9},{9,8},{10,11... | collective-permute-start | bytes 589832 | tf_op jit(solution)/shard_map/ppermute | solution.py:41
  20.8 0.0 copy-start.4
  20.8 0.0 copy-start.5
  20.8 1.0 %collective-permute-done.4 = f32[384,128]{1,0:T(8,128)S(1)} collective-permute-done((f32[384,128]{1,0:T(8,128)S(1)}, f32[384,128]{1,0:T(8,128)S(1)}, u32[]{:S(2)}, u32[]{:S(2)}) %collective-permute-start.4) | collective-permute-done | bytes 196640 | tf_op jit(solution)/shard_map/ppermute | solution.py:41
  21.8 0.6 %collective-permute-start.5 = (f32[768,128]{1,0:T(8,128)S(1)}, f32[768,128]{1,0:T(8,128)S(1)}, u32[]{:S(2)}, u32[]{:S(2)}) collective-permute-start(f32[768,128]{1,0:T(8,128)S(1)} %constant_dynamic-update-slice_fusion.refs_6_), channel_id=1, source_target_pairs={{0,2},{1,3},{2,0},{3,1},{4,6},{5,7},{6,4},{7,5},{8,10},{9,11},{10,... | collective-permute-start | bytes 1179656 | tf_op jit(solution)/shard_map/ppermute | solution.py:41
  22.5 0.0 copy-done.4
  22.5 0.0 copy-done.5
  22.5 11.3 %shard_map.131 = (f32[1944,128]{1,0:T(8,128)S(1)}, f32[1,128]{1,0:T(1,128)S(1)}, s32[595]{0:T(1024)S(1)}, bf16[512,128]{1,0:T(8,128)(2,1)S(1)}) custom-call(s32[2131]{0:T(1024)S(1)} %get-tuple-element.33.refs_0_, bf16[2048,128]{1,0:T(8,128)(2,1)S(1)} %get-tuple-element.34.refs_1_.refs_2_, f32[96,128]{1,0:T(8,128)S(1)} %collective-permute-done.refs_2_, ...), custom_call_target="tpu_custom_call" | custom-call | bytes 30000000 | tf_op jit(solution)/shard_map/pallas_call | solution.py:701
  33.8 0.0 collective-permute-done.5.refs_4_
  33.8 11.1 %shard_map.132 = (f32[192,128]{1,0:T(8,128)S(1)}, f32[48,128]{1,0:T(8,128)S(1)}, f32[1,128]{1,0:T(1,128)S(1)}, f32[2,24,128]{2,1,0:T(8,128)S(1)}, f32[2,32,128]{2,1,0:T(8,128)S(1)}) custom-call(s32[2131]{0:T(1024)S(1)} %get-tuple-element.33.refs_0_, s32[595]{0:T(1024)S(1)} %get-tuple-element.40.refs_1_, ...), custom_call_target="tpu_custom_call" | custom-call | tf_op jit(solution)/shard_map/pallas_call | solution.py:729
  44.9 2.0 %collective-permute-start.6 = (f32[48,128]{1,0:T(8,128)S(1)}, f32[48,128]{1,0:T(8,128)S(1)}, u32[]{:S(2)}, u32[]{:S(2)}) collective-permute-start(f32[48,128]{1,0:T(8,128)S(1)} %get-tuple-element.45), channel_id=1, source_target_pairs={{28,12},{0,16},{29,13},{1,17},{30,14},{2,18},{31,15},{3,19}} | collective-permute-start | bytes 73736 | tf_op jit(solution)/shard_map/ppermute | solution.py:749
  46.9 0.7 %collective-permute-start.7 = (f32[48,128]{1,0:T(8,128)S(1)}, f32[48,128]{1,0:T(8,128)S(1)}, u32[]{:S(2)}, u32[]{:S(2)}) collective-permute-start(f32[48,128]{1,0:T(8,128)S(1)} %get-tuple-element.45), channel_id=1, source_target_pairs={{4,12},{24,16},{5,13},{25,17},{6,14},{26,18},{7,15},{27,19}} | collective-permute-start | bytes 73736 | tf_op jit(solution)/shard_map/ppermute | solution.py:749
  47.6 0.7 %collective-permute-start.8 = (f32[48,128]{1,0:T(8,128)S(1)}, f32[48,128]{1,0:T(8,128)S(1)}, u32[]{:S(2)}, u32[]{:S(2)}) collective-permute-start(f32[48,128]{1,0:T(8,128)S(1)} %get-tuple-element.45), channel_id=1, source_target_pairs={{8,12},{20,16},{9,13},{21,17},{10,14},{22,18},{11,15},{23,19}} | collective-permute-start | bytes 73736 | tf_op jit(solution)/shard_map/ppermute | solution.py:749
  48.2 1.3 %collective-permute-start.9 = (f32[2,32,128]{2,1,0:T(8,128)S(1)}, f32[2,32,128]{2,1,0:T(8,128)S(1)}, u32[]{:S(2)}, u32[]{:S(2)}) collective-permute-start(f32[2,32,128]{2,1,0:T(8,128)S(1)} %get-tuple-element.46), channel_id=1, source_target_pairs={{4,0},{8,4},{12,8},{16,12},{20,16},{24,20},{28,24},{5,1},{9,5},{13... | collective-permute-start | bytes 98312 | tf_op jit(solution)/shard_map/ppermute | solution.py:45
  49.5 1.3 %collective-permute-start.10 = (f32[2,24,128]{2,1,0:T(8,128)S(1)}, f32[2,24,128]{2,1,0:T(8,128)S(1)}, u32[]{:S(2)}, u32[]{:S(2)}) collective-permute-start(f32[2,24,128]{2,1,0:T(8,128)S(1)} %get-tuple-element.47), channel_id=1, source_target_pairs={{1,0},{2,1},{3,2},{5,4},{6,5},{7,6},{9,8},{10,9},{11,10},{13,12},{... | collective-permute-start | bytes 73736 | tf_op jit(solution)/shard_map/ppermute | solution.py:45
  50.8 0.5 slice_bitcast_fusion
  51.4 0.0 collective-permute-done.6
  51.4 0.0 collective-permute-done.7
  51.4 0.0 collective-permute-done.8
  51.4 1.3 %collective-permute-done.10 = f32[2,24,128]{2,1,0:T(8,128)S(1)} collective-permute-done((f32[2,24,128]{2,1,0:T(8,128)S(1)}, f32[2,24,128]{2,1,0:T(8,128)S(1)}, u32[]{:S(2)}, u32[]{:S(2)}) %collective-permute-start.10) | collective-permute-done | bytes 24608 | tf_op jit(solution)/shard_map/ppermute | solution.py:45
  52.6 1.4 %collective-permute-done.9.refs_3_ = f32[2,32,128]{2,1,0:T(8,128)S(1)} collective-permute-done((f32[2,32,128]{2,1,0:T(8,128)S(1)}, f32[2,32,128]{2,1,0:T(8,128)S(1)}, u32[]{:S(2)}, u32[]{:S(2)}) %collective-permute-start.9) | collective-permute-done | bytes 32800 | tf_op jit(solution)/shard_map/ppermute | solution.py:45
  54.1 0.9 %shard_map.133 = (f32[3,8,8,128]{3,2,1,0:T(8,128)}, f32[8,8,128]{2,1,0:T(8,128)}, f32[8,8,128]{2,1,0:T(8,128)}) custom-call(f32[3,8,8,128]{3,2,1,0:T(8,128)S(1)} %copy-done, f32[3,8,8,128]{3,2,1,0:T(8,128)S(1)} %bitcast.16, f32[3,2,8,128]{3,2,1,0:T(8,128)S(1)} %bitcast.17, f32[3,2,8,128]{3,2,1,0:T(8,128)S(1)} %bitcast.18, f32[3,2,8,128]{3,2,1,0:T(8,128)S(1)} %bitcast.19, ...), custom_call_target="tpu_custom_call" | custom-call | tf_op jit(solution)/shard_map/pallas_call | solution.py:756
  (10 shorter events, 0.1 us)
Async XLA Ops:
  2.4 6.8 %collective-permute-start = (f32[96,128]{1,0:T(8,128)}, f32[96,128]{1,0:T(8,128)S(1)}, u32[]{:S(2)}, u32[]{:S(2)}) collective-permute-start(f32[96,128]{1,0:T(8,128)} %get-tuple-element.28), channel_id=1, source_target_pairs={{0,16},{1,17},{2,18},{3,19},{4,20},{5,21},{6,22},{7,23},{8,24},{9,... | collective-permute-start | bytes 147464 | tf_op jit(solution)/shard_map/ppermute | solution.py:41
  6.5 2.8 %copy-start.3 = (f32[48,128]{1,0:T(8,128)S(1)}, f32[48,128]{1,0:T(8,128)}, u32[]{:S(2)}) copy-start(f32[48,128]{1,0:T(8,128)} %get-tuple-element.29) | copy-start | bytes 73732
  7.2 3.5 %copy-start = (f32[3,8,8,128]{3,2,1,0:T(8,128)S(1)}, f32[3,8,8,128]{3,2,1,0:T(8,128)}, u32[]{:S(2)}) copy-start(f32[3,8,8,128]{3,2,1,0:T(8,128)} %points.3) | copy-start | bytes 294916
  9.3 1.5 %copy-start.1 = (s32[8,8,16]{2,1,0:T(8,128)S(1)}, s32[8,8,16]{2,1,0:T(8,128)}, u32[]{:S(2)}) copy-start(s32[8,8,16]{2,1,0:T(8,128)} %numbers.3) | copy-start | bytes 12292
  9.3 1.5 %copy-start.2 = (s32[8,8]{1,0:T(8,128)S(1)}, s32[8,8]{1,0:T(8,128)}, u32[]{:S(2)}) copy-start(s32[8,8]{1,0:T(8,128)} %counts.3) | copy-start | bytes 772
  9.3 5.0 %collective-permute-start.1 = (f32[144,128]{1,0:T(8,128)S(1)}, f32[144,128]{1,0:T(8,128)S(1)}, u32[]{:S(2)}, u32[]{:S(2)}) collective-permute-start(f32[144,128]{1,0:T(8,128)S(1)} %pad_maximum_fusion.3), channel_id=1, source_target_pairs={{0,8},{1,9},{2,10},{3,11},{4,12},{5,13},{6,14},{7,15},{8,0},{9,1},... | collective-permute-start | bytes 221192 | tf_op jit(solution)/shard_map/ppermute | solution.py:41
  14.3 1.6 %copy-start.6 = (f32[8,128]{1,0:T(8,128)S(1)}, f32[8,128]{1,0:T(8,128)}, u32[]{:S(2)}) copy-start(f32[8,128]{1,0:T(8,128)} %get-tuple-element.37) | copy-start | bytes 12292
  14.4 4.9 %collective-permute-start.2 = (f32[240,128]{1,0:T(8,128)S(1)}, f32[240,128]{1,0:T(8,128)S(1)}, u32[]{:S(2)}, u32[]{:S(2)}) collective-permute-start(f32[240,128]{1,0:T(8,128)S(1)} %pad_maximum_fusion.1), channel_id=1, source_target_pairs={{0,4},{1,5},{2,6},{3,7},{4,0},{5,1},{6,2},{7,3},{8,12},{9,13},{10,... | collective-permute-start | bytes 368648 | tf_op jit(solution)/shard_map/ppermute | solution.py:41
  15.9 3.4 %collective-permute-start.3 = (f32[8,128]{1,0:T(8,128)S(1)}, f32[8,128]{1,0:T(8,128)S(1)}, u32[]{:S(2)}, u32[]{:S(2)}) collective-permute-start(f32[8,128]{1,0:T(8,128)S(1)} %copy-done.6), channel_id=1, source_target_pairs={{1,0},{2,1},{3,2},{5,4},{6,5},{7,6},{9,8},{10,9},{11,10},{13,12},{... | collective-permute-start | bytes 12296 | tf_op jit(solution)/shard_map/ppermute | solution.py:45
  19.4 2.5 %collective-permute-start.4 = (f32[384,128]{1,0:T(8,128)S(1)}, f32[384,128]{1,0:T(8,128)S(1)}, u32[]{:S(2)}, u32[]{:S(2)}) collective-permute-start(f32[384,128]{1,0:T(8,128)S(1)} %pad_maximum_fusion), channel_id=1, source_target_pairs={{0,1},{1,0},{2,3},{3,2},{4,5},{5,4},{6,7},{7,6},{8,9},{9,8},{10,11... | collective-permute-start | bytes 589832 | tf_op jit(solution)/shard_map/ppermute | solution.py:41
  20.8 1.7 %copy-start.4 = (f32[6]{0:T(128)S(1)}, f32[6]{0:T(128)}, u32[]{:S(2)}) copy-start(f32[6]{0:T(128)} %param.14) | copy-start | bytes 76
  20.8 1.7 %copy-start.5 = (f32[6]{0:T(128)S(1)}, f32[6]{0:T(128)}, u32[]{:S(2)}) copy-start(f32[6]{0:T(128)} %param.13) | copy-start | bytes 76
  21.8 12.0 %collective-permute-start.5 = (f32[768,128]{1,0:T(8,128)S(1)}, f32[768,128]{1,0:T(8,128)S(1)}, u32[]{:S(2)}, u32[]{:S(2)}) collective-permute-start(f32[768,128]{1,0:T(8,128)S(1)} %constant_dynamic-update-slice_fusion.refs_6_), channel_id=1, source_target_pairs={{0,2},{1,3},{2,0},{3,1},{4,6},{5,7},{6,4},{7,5},{8,10},{9,11},{10,... | collective-permute-start | bytes 1179656 | tf_op jit(solution)/shard_map/ppermute | solution.py:41
  44.9 6.5 %collective-permute-start.6 = (f32[48,128]{1,0:T(8,128)S(1)}, f32[48,128]{1,0:T(8,128)S(1)}, u32[]{:S(2)}, u32[]{:S(2)}) collective-permute-start(f32[48,128]{1,0:T(8,128)S(1)} %get-tuple-element.45), channel_id=1, source_target_pairs={{28,12},{0,16},{29,13},{1,17},{30,14},{2,18},{31,15},{3,19}} | collective-permute-start | bytes 73736 | tf_op jit(solution)/shard_map/ppermute | solution.py:749
  46.9 4.5 %collective-permute-start.7 = (f32[48,128]{1,0:T(8,128)S(1)}, f32[48,128]{1,0:T(8,128)S(1)}, u32[]{:S(2)}, u32[]{:S(2)}) collective-permute-start(f32[48,128]{1,0:T(8,128)S(1)} %get-tuple-element.45), channel_id=1, source_target_pairs={{4,12},{24,16},{5,13},{25,17},{6,14},{26,18},{7,15},{27,19}} | collective-permute-start | bytes 73736 | tf_op jit(solution)/shard_map/ppermute | solution.py:749
  47.6 3.8 %collective-permute-start.8 = (f32[48,128]{1,0:T(8,128)S(1)}, f32[48,128]{1,0:T(8,128)S(1)}, u32[]{:S(2)}, u32[]{:S(2)}) collective-permute-start(f32[48,128]{1,0:T(8,128)S(1)} %get-tuple-element.45), channel_id=1, source_target_pairs={{8,12},{20,16},{9,13},{21,17},{10,14},{22,18},{11,15},{23,19}} | collective-permute-start | bytes 73736 | tf_op jit(solution)/shard_map/ppermute | solution.py:749
  48.2 5.8 %collective-permute-start.9 = (f32[2,32,128]{2,1,0:T(8,128)S(1)}, f32[2,32,128]{2,1,0:T(8,128)S(1)}, u32[]{:S(2)}, u32[]{:S(2)}) collective-permute-start(f32[2,32,128]{2,1,0:T(8,128)S(1)} %get-tuple-element.46), channel_id=1, source_target_pairs={{4,0},{8,4},{12,8},{16,12},{20,16},{24,20},{28,24},{5,1},{9,5},{13... | collective-permute-start | bytes 98312 | tf_op jit(solution)/shard_map/ppermute | solution.py:45
  49.5 3.1 %collective-permute-start.10 = (f32[2,24,128]{2,1,0:T(8,128)S(1)}, f32[2,24,128]{2,1,0:T(8,128)S(1)}, u32[]{:S(2)}, u32[]{:S(2)}) collective-permute-start(f32[2,24,128]{2,1,0:T(8,128)S(1)} %get-tuple-element.47), channel_id=1, source_target_pairs={{1,0},{2,1},{3,2},{5,4},{6,5},{7,6},{9,8},{10,9},{11,10},{13,12},{... | collective-permute-start | bytes 73736 | tf_op jit(solution)/shard_map/ppermute | solution.py:45

commit v8 on v7

--- a/solution.py
+++ b/solution.py
@@ -441,25 +441,18 @@
     acceleration = inverse[...] * total + gravity
     out_state[...] = motion[...] + TIME_STEP * acceleration
     step = TIME_STEP * motion[...] + 0.5 * TIME_STEP * TIME_STEP * acceleration
-    row = lax.broadcasted_iota(jnp.int32, (8, 128), 0)
-    lane = lax.broadcasted_iota(jnp.int32, (8, 128), 1)
-    chosen = jnp.where((lane == row - 1) & (lane < 6), jnp.broadcast_to(step, (8, 128)), 0.0)
-    weight = jnp.broadcast_to(jnp.sum(chosen, axis=1, keepdims=True), (8, 128))
-
     acc[...] = early[...]
     add_items(
         bits, 1, lists, table, feats, line_feat, tile_feat, modes, acc, squares, lambda: None
     )
 
     def finish(count, first, out):
-        def one(l, carry):
-            base = pl.multiple_of((first + l) * ROWS, 8)
-            for c in range(3):
-                value = jnp.sum(weight * acc[pl.ds(base + 8 * c, 8), :], axis=0, keepdims=True)
-                out[pl.ds(c * count + l, 1), :] = value
-            return carry
-
-        lax.fori_loop(0, count, one, 0, unroll=4)
+        for c in range(3):
+            value = jnp.zeros((count, out.shape[1]), F32)
+            for k in range(6):
+                at = first * ROWS + 8 * c + 1 + k
+                value = value + step[:, k : k + 1] * acc[pl.ds(at, count, stride=ROWS), :]
+            out[c * count : (c + 1) * count, :] = value
 
     finish(own, 0, out_own)
     finish(lent, own, out_extra)

time: 55.7 us -> 55.9 us (level)
  starting transfers between devices: 16.2 us -> 18.7 us
  Pallas kernels: 28.6 us -> 26.7 us
    ppermute x3, starting transfers between devices: 3.31 us -> 5.74 us  [local(): lax.ppermute(lent_shift, 'slab', [(h ^ bit, h) for h in heavy])]
    pallas_call x1, Pallas kernels: 11.1 us -> 9.27 us  [local(): pl.pallas_call(functools.partial(late_kernel, own, lent, parts, bits), ou...]
where the time goes in v8:
time: 55.9 us; the launch traced here: 55.5 us
  Pallas kernels  26.7 us (48%)
  starting transfers between devices  18.7 us (33%)
  waiting for transfers between devices  7.85 us (14%)
  local copies, waits for them, and re-layouts  1.37 us (2%)
  between operations  0.83 us (1%)
    pallas_call x1, Pallas kernels, local(): pl.pallas_call(functools.partial(early_kernel, own, rows, slots, lent, bi...  11.3 us
    pallas_call x1, Pallas kernels, local(): pl.pallas_call(functools.partial(late_kernel, own, lent, parts, bits), ou...  9.27 us
    ppermute x5, starting transfers between devices, swapped(): return lax.ppermute(value, ('slab', 'ctrl'), pairs)  9.06 us
    ppermute x3, starting transfers between devices, local(): lax.ppermute(lent_shift, 'slab', [(h ^ bit, h) for h in heavy])  5.74 us
    ppermute x5, waiting for transfers between devices, swapped(): return lax.ppermute(value, ('slab', 'ctrl'), pairs)  5.16 us
    ppermute x3, starting transfers between devices, shifted_back(): lax.ppermute(value, axis, [(i, i - 1) for i in range(1, lax.axis_size(axi...  3.86 us
    pallas_call x1, Pallas kernels, prepared(): pl.pallas_call(kernel, out_shape=(jax.ShapeDtypeStruct((2 * length + 3,),...  3.52 us
    ppermute x3, waiting for transfers between devices, shifted_back(): lax.ppermute(value, axis, [(i, i - 1) for i in range(1, lax.axis_size(axi...  2.68 us
  transfers between devices with their start and end apart: 11, of which 5 were waited for; matrix products, arithmetic and copies ran while one was open for 2% of the time, Pallas kernels for 27%

profile of v8, /device:TPU:0, one launch (start us, length us, event | category | flops | bytes accessed | tf_op | source)
XLA Modules:
  0.0 55.5 jit_solution(5893592628431947724)
XLA Ops:
  0.6 1.8 %shard_map.129 = (f32[8,128]{1,0:T(8,128)}, f32[96,128]{1,0:T(8,128)}, f32[48,128]{1,0:T(8,128)}) custom-call(f32[1,4096]{1,0:T(1,128)} %bitcast.21, f32[3,4096]{1,0:T(4,128)} %area.1, f32[3,4096]{1,0:T(4,128)} %center.1, f32[3,256]{1,0:T(4,128)} %points.2, f32[18,256]{1,0:T(8,128)} %modes.1, f32[192,128]{1,0:T(8,128)} %bitcast.13, s32[8,8,16]{2,1,0:T(8,128)} %numbers.3, ...), custom_call_target="tpu_custom_call" | custom-call | tf_op jit(solution)/shard_map/pallas_call | solution.py:623
  2.4 4.0 %collective-permute-start = (f32[96,128]{1,0:T(8,128)}, f32[96,128]{1,0:T(8,128)S(1)}, u32[]{:S(2)}, u32[]{:S(2)}) collective-permute-start(f32[96,128]{1,0:T(8,128)} %get-tuple-element.28), channel_id=1, source_target_pairs={{0,16},{1,17},{2,18},{3,19},{4,20},{5,21},{6,22},{7,23},{8,24},{9,... | collective-permute-start | bytes 147464 | tf_op jit(solution)/shard_map/ppermute | solution.py:41
  6.5 0.0 copy-start.3
  6.5 0.8 %slice.15 = f32[48,128]{1,0:T(8,128)S(1)} slice(f32[96,128]{1,0:T(8,128)} %get-tuple-element.28), slice={[0:48], [0:128]} | slice | bytes 49152 | tf_op jit(solution)/shard_map/slice | solution.py:637
  7.2 0.0 copy-start
  7.2 2.0 %collective-permute-done.refs_2_ = f32[96,128]{1,0:T(8,128)S(1)} collective-permute-done((f32[96,128]{1,0:T(8,128)}, f32[96,128]{1,0:T(8,128)S(1)}, u32[]{:S(2)}, u32[]{:S(2)}) %collective-permute-start) | collective-permute-done | bytes 49184 | tf_op jit(solution)/shard_map/ppermute | solution.py:41
  9.3 0.0 copy-done.3
  9.3 0.0 copy-start.1
  9.3 0.0 copy-start.2
  9.3 1.4 %collective-permute-start.1 = (f32[144,128]{1,0:T(8,128)S(1)}, f32[144,128]{1,0:T(8,128)S(1)}, u32[]{:S(2)}, u32[]{:S(2)}) collective-permute-start(f32[144,128]{1,0:T(8,128)S(1)} %pad_maximum_fusion.3), channel_id=1, source_target_pairs={{0,8},{1,9},{2,10},{3,11},{4,12},{5,13},{6,14},{7,15},{8,0},{9,1},... | collective-permute-start | bytes 221192 | tf_op jit(solution)/shard_map/ppermute | solution.py:41
  10.8 0.0 copy-done
  10.8 0.0 copy-done.1
  10.8 0.0 copy-done.2
  10.8 3.5 %shard_map.130 = (s32[2131]{0:T(1024)S(1)}, bf16[2048,128]{1,0:T(8,128)(2,1)S(1)}, f32[48,128]{1,0:T(8,128)S(1)}) custom-call(f32[192,128]{1,0:T(8,128)S(1)} %bitcast.14, s32[8,8,16]{2,1,0:T(8,128)S(1)} %copy-done.1, s32[8,8]{1,0:T(8,128)S(1)} %copy-done.2), custom_call_target="tpu_custom_call" | custom-call | bytes 8000000 | tf_op jit(solution)/shard_map/pallas_call | solution.py:312
  14.3 0.0 collective-permute-done.1.refs_3_
  14.3 0.0 copy-start.6
  14.4 1.6 %collective-permute-start.2 = (f32[240,128]{1,0:T(8,128)S(1)}, f32[240,128]{1,0:T(8,128)S(1)}, u32[]{:S(2)}, u32[]{:S(2)}) collective-permute-start(f32[240,128]{1,0:T(8,128)S(1)} %pad_maximum_fusion.1), channel_id=1, source_target_pairs={{0,4},{1,5},{2,6},{3,7},{4,0},{5,1},{6,2},{7,3},{8,12},{9,13},{10,... | collective-permute-start | bytes 368648 | tf_op jit(solution)/shard_map/ppermute | solution.py:41
  15.9 0.0 copy-done.6
  15.9 1.3 %collective-permute-start.3 = (f32[8,128]{1,0:T(8,128)S(1)}, f32[8,128]{1,0:T(8,128)S(1)}, u32[]{:S(2)}, u32[]{:S(2)}) collective-permute-start(f32[8,128]{1,0:T(8,128)S(1)} %copy-done.6), channel_id=1, source_target_pairs={{1,0},{2,1},{3,2},{5,4},{6,5},{7,6},{9,8},{10,9},{11,10},{13,12},{... | collective-permute-start | bytes 12296 | tf_op jit(solution)/shard_map/ppermute | solution.py:45
  17.2 2.1 %collective-permute-done.2.refs_4_ = f32[240,128]{1,0:T(8,128)S(1)} collective-permute-done((f32[240,128]{1,0:T(8,128)S(1)}, f32[240,128]{1,0:T(8,128)S(1)}, u32[]{:S(2)}, u32[]{:S(2)}) %collective-permute-start.2) | collective-permute-done | bytes 122912 | tf_op jit(solution)/shard_map/ppermute | solution.py:41
  19.3 0.0 collective-permute-done.3.refs_5_.refs_8_
  19.4 1.4 %collective-permute-start.4 = (f32[384,128]{1,0:T(8,128)S(1)}, f32[384,128]{1,0:T(8,128)S(1)}, u32[]{:S(2)}, u32[]{:S(2)}) collective-permute-start(f32[384,128]{1,0:T(8,128)S(1)} %pad_maximum_fusion), channel_id=1, source_target_pairs={{0,1},{1,0},{2,3},{3,2},{4,5},{5,4},{6,7},{7,6},{8,9},{9,8},{10,11... | collective-permute-start | bytes 589832 | tf_op jit(solution)/shard_map/ppermute | solution.py:41
  20.8 0.0 copy-start.4
  20.8 0.0 copy-start.5
  20.8 1.0 %collective-permute-done.4 = f32[384,128]{1,0:T(8,128)S(1)} collective-permute-done((f32[384,128]{1,0:T(8,128)S(1)}, f32[384,128]{1,0:T(8,128)S(1)}, u32[]{:S(2)}, u32[]{:S(2)}) %collective-permute-start.4) | collective-permute-done | bytes 196640 | tf_op jit(solution)/shard_map/ppermute | solution.py:41
  21.8 0.6 %collective-permute-start.5 = (f32[768,128]{1,0:T(8,128)S(1)}, f32[768,128]{1,0:T(8,128)S(1)}, u32[]{:S(2)}, u32[]{:S(2)}) collective-permute-start(f32[768,128]{1,0:T(8,128)S(1)} %constant_dynamic-update-slice_fusion.refs_6_), channel_id=1, source_target_pairs={{0,2},{1,3},{2,0},{3,1},{4,6},{5,7},{6,4},{7,5},{8,10},{9,11},{10,... | collective-permute-start | bytes 1179656 | tf_op jit(solution)/shard_map/ppermute | solution.py:41
  22.5 0.0 copy-done.4
  22.5 0.0 copy-done.5
  22.5 11.3 %shard_map.131 = (f32[1944,128]{1,0:T(8,128)S(1)}, f32[1,128]{1,0:T(1,128)S(1)}, s32[595]{0:T(1024)S(1)}, bf16[512,128]{1,0:T(8,128)(2,1)S(1)}) custom-call(s32[2131]{0:T(1024)S(1)} %get-tuple-element.33.refs_0_, bf16[2048,128]{1,0:T(8,128)(2,1)S(1)} %get-tuple-element.34.refs_1_.refs_2_, f32[96,128]{1,0:T(8,128)S(1)} %collective-permute-done.refs_2_, ...), custom_call_target="tpu_custom_call" | custom-call | bytes 30000000 | tf_op jit(solution)/shard_map/pallas_call | solution.py:694
  33.8 0.0 collective-permute-done.5.refs_4_
  33.8 9.3 %shard_map.132 = (f32[192,128]{1,0:T(8,128)S(1)}, f32[48,128]{1,0:T(8,128)S(1)}, f32[1,128]{1,0:T(1,128)S(1)}, f32[2,24,128]{2,1,0:T(8,128)S(1)}, f32[2,32,128]{2,1,0:T(8,128)S(1)}) custom-call(s32[2131]{0:T(1024)S(1)} %get-tuple-element.33.refs_0_, s32[595]{0:T(1024)S(1)} %get-tuple-element.40.refs_1_, ...), custom_call_target="tpu_custom_call" | custom-call | tf_op jit(solution)/shard_map/pallas_call | solution.py:722
  43.0 4.4 %collective-permute-start.6 = (f32[48,128]{1,0:T(8,128)S(1)}, f32[48,128]{1,0:T(8,128)S(1)}, u32[]{:S(2)}, u32[]{:S(2)}) collective-permute-start(f32[48,128]{1,0:T(8,128)S(1)} %get-tuple-element.45), channel_id=1, source_target_pairs={{28,12},{0,16},{29,13},{1,17},{30,14},{2,18},{31,15},{3,19}} | collective-permute-start | bytes 73736 | tf_op jit(solution)/shard_map/ppermute | solution.py:742
  47.5 0.7 %collective-permute-start.7 = (f32[48,128]{1,0:T(8,128)S(1)}, f32[48,128]{1,0:T(8,128)S(1)}, u32[]{:S(2)}, u32[]{:S(2)}) collective-permute-start(f32[48,128]{1,0:T(8,128)S(1)} %get-tuple-element.45), channel_id=1, source_target_pairs={{4,12},{24,16},{5,13},{25,17},{6,14},{26,18},{7,15},{27,19}} | collective-permute-start | bytes 73736 | tf_op jit(solution)/shard_map/ppermute | solution.py:742
  48.1 0.7 %collective-permute-start.8 = (f32[48,128]{1,0:T(8,128)S(1)}, f32[48,128]{1,0:T(8,128)S(1)}, u32[]{:S(2)}, u32[]{:S(2)}) collective-permute-start(f32[48,128]{1,0:T(8,128)S(1)} %get-tuple-element.45), channel_id=1, source_target_pairs={{8,12},{20,16},{9,13},{21,17},{10,14},{22,18},{11,15},{23,19}} | collective-permute-start | bytes 73736 | tf_op jit(solution)/shard_map/ppermute | solution.py:742
  48.8 1.3 %collective-permute-start.9 = (f32[2,32,128]{2,1,0:T(8,128)S(1)}, f32[2,32,128]{2,1,0:T(8,128)S(1)}, u32[]{:S(2)}, u32[]{:S(2)}) collective-permute-start(f32[2,32,128]{2,1,0:T(8,128)S(1)} %get-tuple-element.46), channel_id=1, source_target_pairs={{4,0},{8,4},{12,8},{16,12},{20,16},{24,20},{28,24},{5,1},{9,5},{13... | collective-permute-start | bytes 98312 | tf_op jit(solution)/shard_map/ppermute | solution.py:45
  50.1 1.3 %collective-permute-start.10 = (f32[2,24,128]{2,1,0:T(8,128)S(1)}, f32[2,24,128]{2,1,0:T(8,128)S(1)}, u32[]{:S(2)}, u32[]{:S(2)}) collective-permute-start(f32[2,24,128]{2,1,0:T(8,128)S(1)} %get-tuple-element.47), channel_id=1, source_target_pairs={{1,0},{2,1},{3,2},{5,4},{6,5},{7,6},{9,8},{10,9},{11,10},{13,12},{... | collective-permute-start | bytes 73736 | tf_op jit(solution)/shard_map/ppermute | solution.py:45
  51.4 0.5 slice_bitcast_fusion
  51.9 0.0 collective-permute-done.6
  51.9 0.0 collective-permute-done.7
  51.9 0.0 collective-permute-done.8
  51.9 1.3 %collective-permute-done.10 = f32[2,24,128]{2,1,0:T(8,128)S(1)} collective-permute-done((f32[2,24,128]{2,1,0:T(8,128)S(1)}, f32[2,24,128]{2,1,0:T(8,128)S(1)}, u32[]{:S(2)}, u32[]{:S(2)}) %collective-permute-start.10) | collective-permute-done | bytes 24608 | tf_op jit(solution)/shard_map/ppermute | solution.py:45
  53.2 1.4 %collective-permute-done.9.refs_3_ = f32[2,32,128]{2,1,0:T(8,128)S(1)} collective-permute-done((f32[2,32,128]{2,1,0:T(8,128)S(1)}, f32[2,32,128]{2,1,0:T(8,128)S(1)}, u32[]{:S(2)}, u32[]{:S(2)}) %collective-permute-start.9) | collective-permute-done | bytes 32800 | tf_op jit(solution)/shard_map/ppermute | solution.py:45
  54.6 0.9 %shard_map.133 = (f32[3,8,8,128]{3,2,1,0:T(8,128)}, f32[8,8,128]{2,1,0:T(8,128)}, f32[8,8,128]{2,1,0:T(8,128)}) custom-call(f32[3,8,8,128]{3,2,1,0:T(8,128)S(1)} %copy-done, f32[3,8,8,128]{3,2,1,0:T(8,128)S(1)} %bitcast.16, f32[3,2,8,128]{3,2,1,0:T(8,128)S(1)} %bitcast.17, f32[3,2,8,128]{3,2,1,0:T(8,128)S(1)} %bitcast.18, f32[3,2,8,128]{3,2,1,0:T(8,128)S(1)} %bitcast.19, ...), custom_call_target="tpu_custom_call" | custom-call | tf_op jit(solution)/shard_map/pallas_call | solution.py:749
  (10 shorter events, 0.1 us)
Async XLA Ops:
  2.4 6.8 %collective-permute-start = (f32[96,128]{1,0:T(8,128)}, f32[96,128]{1,0:T(8,128)S(1)}, u32[]{:S(2)}, u32[]{:S(2)}) collective-permute-start(f32[96,128]{1,0:T(8,128)} %get-tuple-element.28), channel_id=1, source_target_pairs={{0,16},{1,17},{2,18},{3,19},{4,20},{5,21},{6,22},{7,23},{8,24},{9,... | collective-permute-start | bytes 147464 | tf_op jit(solution)/shard_map/ppermute | solution.py:41
  6.5 2.8 %copy-start.3 = (f32[48,128]{1,0:T(8,128)S(1)}, f32[48,128]{1,0:T(8,128)}, u32[]{:S(2)}) copy-start(f32[48,128]{1,0:T(8,128)} %get-tuple-element.29) | copy-start | bytes 73732
  7.2 3.5 %copy-start = (f32[3,8,8,128]{3,2,1,0:T(8,128)S(1)}, f32[3,8,8,128]{3,2,1,0:T(8,128)}, u32[]{:S(2)}) copy-start(f32[3,8,8,128]{3,2,1,0:T(8,128)} %points.3) | copy-start | bytes 294916
  9.3 1.5 %copy-start.1 = (s32[8,8,16]{2,1,0:T(8,128)S(1)}, s32[8,8,16]{2,1,0:T(8,128)}, u32[]{:S(2)}) copy-start(s32[8,8,16]{2,1,0:T(8,128)} %numbers.3) | copy-start | bytes 12292
  9.3 1.5 %copy-start.2 = (s32[8,8]{1,0:T(8,128)S(1)}, s32[8,8]{1,0:T(8,128)}, u32[]{:S(2)}) copy-start(s32[8,8]{1,0:T(8,128)} %counts.3) | copy-start | bytes 772
  9.3 5.0 %collective-permute-start.1 = (f32[144,128]{1,0:T(8,128)S(1)}, f32[144,128]{1,0:T(8,128)S(1)}, u32[]{:S(2)}, u32[]{:S(2)}) collective-permute-start(f32[144,128]{1,0:T(8,128)S(1)} %pad_maximum_fusion.3), channel_id=1, source_target_pairs={{0,8},{1,9},{2,10},{3,11},{4,12},{5,13},{6,14},{7,15},{8,0},{9,1},... | collective-permute-start | bytes 221192 | tf_op jit(solution)/shard_map/ppermute | solution.py:41
  14.3 1.6 %copy-start.6 = (f32[8,128]{1,0:T(8,128)S(1)}, f32[8,128]{1,0:T(8,128)}, u32[]{:S(2)}) copy-start(f32[8,128]{1,0:T(8,128)} %get-tuple-element.37) | copy-start | bytes 12292
  14.4 4.9 %collective-permute-start.2 = (f32[240,128]{1,0:T(8,128)S(1)}, f32[240,128]{1,0:T(8,128)S(1)}, u32[]{:S(2)}, u32[]{:S(2)}) collective-permute-start(f32[240,128]{1,0:T(8,128)S(1)} %pad_maximum_fusion.1), channel_id=1, source_target_pairs={{0,4},{1,5},{2,6},{3,7},{4,0},{5,1},{6,2},{7,3},{8,12},{9,13},{10,... | collective-permute-start | bytes 368648 | tf_op jit(solution)/shard_map/ppermute | solution.py:41
  15.9 3.4 %collective-permute-start.3 = (f32[8,128]{1,0:T(8,128)S(1)}, f32[8,128]{1,0:T(8,128)S(1)}, u32[]{:S(2)}, u32[]{:S(2)}) collective-permute-start(f32[8,128]{1,0:T(8,128)S(1)} %copy-done.6), channel_id=1, source_target_pairs={{1,0},{2,1},{3,2},{5,4},{6,5},{7,6},{9,8},{10,9},{11,10},{13,12},{... | collective-permute-start | bytes 12296 | tf_op jit(solution)/shard_map/ppermute | solution.py:45
  19.4 2.5 %collective-permute-start.4 = (f32[384,128]{1,0:T(8,128)S(1)}, f32[384,128]{1,0:T(8,128)S(1)}, u32[]{:S(2)}, u32[]{:S(2)}) collective-permute-start(f32[384,128]{1,0:T(8,128)S(1)} %pad_maximum_fusion), channel_id=1, source_target_pairs={{0,1},{1,0},{2,3},{3,2},{4,5},{5,4},{6,7},{7,6},{8,9},{9,8},{10,11... | collective-permute-start | bytes 589832 | tf_op jit(solution)/shard_map/ppermute | solution.py:41
  20.8 1.7 %copy-start.4 = (f32[6]{0:T(128)S(1)}, f32[6]{0:T(128)}, u32[]{:S(2)}) copy-start(f32[6]{0:T(128)} %param.14) | copy-start | bytes 76
  20.8 1.7 %copy-start.5 = (f32[6]{0:T(128)S(1)}, f32[6]{0:T(128)}, u32[]{:S(2)}) copy-start(f32[6]{0:T(128)} %param.13) | copy-start | bytes 76
  21.8 11.9 %collective-permute-start.5 = (f32[768,128]{1,0:T(8,128)S(1)}, f32[768,128]{1,0:T(8,128)S(1)}, u32[]{:S(2)}, u32[]{:S(2)}) collective-permute-start(f32[768,128]{1,0:T(8,128)S(1)} %constant_dynamic-update-slice_fusion.refs_6_), channel_id=1, source_target_pairs={{0,2},{1,3},{2,0},{3,1},{4,6},{5,7},{6,4},{7,5},{8,10},{9,11},{10,... | collective-permute-start | bytes 1179656 | tf_op jit(solution)/shard_map/ppermute | solution.py:41
  43.0 8.9 %collective-permute-start.6 = (f32[48,128]{1,0:T(8,128)S(1)}, f32[48,128]{1,0:T(8,128)S(1)}, u32[]{:S(2)}, u32[]{:S(2)}) collective-permute-start(f32[48,128]{1,0:T(8,128)S(1)} %get-tuple-element.45), channel_id=1, source_target_pairs={{28,12},{0,16},{29,13},{1,17},{30,14},{2,18},{31,15},{3,19}} | collective-permute-start | bytes 73736 | tf_op jit(solution)/shard_map/ppermute | solution.py:742
  47.5 4.5 %collective-permute-start.7 = (f32[48,128]{1,0:T(8,128)S(1)}, f32[48,128]{1,0:T(8,128)S(1)}, u32[]{:S(2)}, u32[]{:S(2)}) collective-permute-start(f32[48,128]{1,0:T(8,128)S(1)} %get-tuple-element.45), channel_id=1, source_target_pairs={{4,12},{24,16},{5,13},{25,17},{6,14},{26,18},{7,15},{27,19}} | collective-permute-start | bytes 73736 | tf_op jit(solution)/shard_map/ppermute | solution.py:742
  48.1 3.8 %collective-permute-start.8 = (f32[48,128]{1,0:T(8,128)S(1)}, f32[48,128]{1,0:T(8,128)S(1)}, u32[]{:S(2)}, u32[]{:S(2)}) collective-permute-start(f32[48,128]{1,0:T(8,128)S(1)} %get-tuple-element.45), channel_id=1, source_target_pairs={{8,12},{20,16},{9,13},{21,17},{10,14},{22,18},{11,15},{23,19}} | collective-permute-start | bytes 73736 | tf_op jit(solution)/shard_map/ppermute | solution.py:742
  48.8 5.8 %collective-permute-start.9 = (f32[2,32,128]{2,1,0:T(8,128)S(1)}, f32[2,32,128]{2,1,0:T(8,128)S(1)}, u32[]{:S(2)}, u32[]{:S(2)}) collective-permute-start(f32[2,32,128]{2,1,0:T(8,128)S(1)} %get-tuple-element.46), channel_id=1, source_target_pairs={{4,0},{8,4},{12,8},{16,12},{20,16},{24,20},{28,24},{5,1},{9,5},{13... | collective-permute-start | bytes 98312 | tf_op jit(solution)/shard_map/ppermute | solution.py:45
  50.1 3.1 %collective-permute-start.10 = (f32[2,24,128]{2,1,0:T(8,128)S(1)}, f32[2,24,128]{2,1,0:T(8,128)S(1)}, u32[]{:S(2)}, u32[]{:S(2)}) collective-permute-start(f32[2,24,128]{2,1,0:T(8,128)S(1)} %get-tuple-element.47), channel_id=1, source_target_pairs={{1,0},{2,1},{3,2},{5,4},{6,5},{7,6},{9,8},{10,9},{11,10},{13,12},{... | collective-permute-start | bytes 73736 | tf_op jit(solution)/shard_map/ppermute | solution.py:45

commit v9 on v8

--- a/solution.py
+++ b/solution.py
@@ -349,7 +349,7 @@
         modes[at, :] = jnp.concatenate([high, low], axis=0)
         return carry
 
-    lax.fori_loop(0, tiles, build, 0, unroll=4)
+    lax.fori_loop(0, tiles, build, 0, unroll=8)
     mask = tiles - 1
     ready()
     middles = [(items.shape[0] - 3) // 2 for items in lists]

time: 55.9 us -> 55.6 us (level)
  Pallas kernels: 26.7 us -> 25.4 us
    pallas_call x1, Pallas kernels: 11.3 us -> 10.3 us  [local(): pl.pallas_call(functools.partial(early_kernel, own, rows, slots, lent, bi...]
  transfers between devices with their start and end apart: 11 -> 11, of which waited for: 5 -> 6; matrix products, arithmetic and copies ran while one was open for 2% -> 2% of each run, Pallas kernels for 27% -> 25%
where the time goes in v9:
time: 55.6 us; the launch traced here: 55.2 us
  Pallas kernels  25.4 us (46%)
  starting transfers between devices  19.2 us (35%)
  waiting for transfers between devices  8.4 us (15%)
  local copies, waits for them, and re-layouts  1.37 us (2%)
  between operations  0.82 us (1%)
    pallas_call x1, Pallas kernels, local(): pl.pallas_call(functools.partial(early_kernel, own, rows, slots, lent, bi...  10.3 us
    ppermute x5, starting transfers between devices, swapped(): return lax.ppermute(value, ('slab', 'ctrl'), pairs)  9.06 us
    pallas_call x1, Pallas kernels, local(): pl.pallas_call(functools.partial(late_kernel, own, lent, parts, bits), ou...  8.97 us
    ppermute x3, starting transfers between devices, local(): lax.ppermute(lent_shift, 'slab', [(h ^ bit, h) for h in heavy])  6.28 us
    ppermute x5, waiting for transfers between devices, swapped(): return lax.ppermute(value, ('slab', 'ctrl'), pairs)  5.71 us
    ppermute x3, starting transfers between devices, shifted_back(): lax.ppermute(value, axis, [(i, i - 1) for i in range(1, lax.axis_size(axi...  3.86 us
    pallas_call x1, Pallas kernels, prepared(): pl.pallas_call(kernel, out_shape=(jax.ShapeDtypeStruct((2 * length + 3,),...  3.52 us
    ppermute x3, waiting for transfers between devices, shifted_back(): lax.ppermute(value, axis, [(i, i - 1) for i in range(1, lax.axis_size(axi...  2.68 us
  transfers between devices with their start and end apart: 11, of which 6 were waited for; matrix products, arithmetic and copies ran while one was open for 2% of the time, Pallas kernels for 25%

profile of v9, /device:TPU:0, one launch (start us, length us, event | category | flops | bytes accessed | tf_op | source)
XLA Modules:
  0.0 55.2 jit_solution(3148592585660470676)
XLA Ops:
  0.6 1.8 %shard_map.129 = (f32[8,128]{1,0:T(8,128)}, f32[96,128]{1,0:T(8,128)}, f32[48,128]{1,0:T(8,128)}) custom-call(f32[1,4096]{1,0:T(1,128)} %bitcast.21, f32[3,4096]{1,0:T(4,128)} %area.1, f32[3,4096]{1,0:T(4,128)} %center.1, f32[3,256]{1,0:T(4,128)} %points.2, f32[18,256]{1,0:T(8,128)} %modes.1, f32[192,128]{1,0:T(8,128)} %bitcast.13, s32[8,8,16]{2,1,0:T(8,128)} %numbers.3, ...), custom_call_target="tpu_custom_call" | custom-call | tf_op jit(solution)/shard_map/pallas_call | solution.py:623
  2.4 4.0 %collective-permute-start = (f32[96,128]{1,0:T(8,128)}, f32[96,128]{1,0:T(8,128)S(1)}, u32[]{:S(2)}, u32[]{:S(2)}) collective-permute-start(f32[96,128]{1,0:T(8,128)} %get-tuple-element.28), channel_id=1, source_target_pairs={{0,16},{1,17},{2,18},{3,19},{4,20},{5,21},{6,22},{7,23},{8,24},{9,... | collective-permute-start | bytes 147464 | tf_op jit(solution)/shard_map/ppermute | solution.py:41
  6.5 0.0 copy-start.3
  6.5 0.8 %slice.15 = f32[48,128]{1,0:T(8,128)S(1)} slice(f32[96,128]{1,0:T(8,128)} %get-tuple-element.28), slice={[0:48], [0:128]} | slice | bytes 49152 | tf_op jit(solution)/shard_map/slice | solution.py:637
  7.2 0.0 copy-start
  7.2 2.0 %collective-permute-done.refs_2_ = f32[96,128]{1,0:T(8,128)S(1)} collective-permute-done((f32[96,128]{1,0:T(8,128)}, f32[96,128]{1,0:T(8,128)S(1)}, u32[]{:S(2)}, u32[]{:S(2)}) %collective-permute-start) | collective-permute-done | bytes 49184 | tf_op jit(solution)/shard_map/ppermute | solution.py:41
  9.3 0.0 copy-done.3
  9.3 0.0 copy-start.1
  9.3 0.0 copy-start.2
  9.3 1.4 %collective-permute-start.1 = (f32[144,128]{1,0:T(8,128)S(1)}, f32[144,128]{1,0:T(8,128)S(1)}, u32[]{:S(2)}, u32[]{:S(2)}) collective-permute-start(f32[144,128]{1,0:T(8,128)S(1)} %pad_maximum_fusion.3), channel_id=1, source_target_pairs={{0,8},{1,9},{2,10},{3,11},{4,12},{5,13},{6,14},{7,15},{8,0},{9,1},... | collective-permute-start | bytes 221192 | tf_op jit(solution)/shard_map/ppermute | solution.py:41
  10.8 0.0 copy-done
  10.8 0.0 copy-done.1
  10.8 0.0 copy-done.2
  10.8 3.5 %shard_map.130 = (s32[2131]{0:T(1024)S(1)}, bf16[2048,128]{1,0:T(8,128)(2,1)S(1)}, f32[48,128]{1,0:T(8,128)S(1)}) custom-call(f32[192,128]{1,0:T(8,128)S(1)} %bitcast.14, s32[8,8,16]{2,1,0:T(8,128)S(1)} %copy-done.1, s32[8,8]{1,0:T(8,128)S(1)} %copy-done.2), custom_call_target="tpu_custom_call" | custom-call | bytes 8000000 | tf_op jit(solution)/shard_map/pallas_call | solution.py:312
  14.3 0.0 collective-permute-done.1.refs_3_
  14.3 0.0 copy-start.6
  14.4 1.6 %collective-permute-start.2 = (f32[240,128]{1,0:T(8,128)S(1)}, f32[240,128]{1,0:T(8,128)S(1)}, u32[]{:S(2)}, u32[]{:S(2)}) collective-permute-start(f32[240,128]{1,0:T(8,128)S(1)} %pad_maximum_fusion.1), channel_id=1, source_target_pairs={{0,4},{1,5},{2,6},{3,7},{4,0},{5,1},{6,2},{7,3},{8,12},{9,13},{10,... | collective-permute-start | bytes 368648 | tf_op jit(solution)/shard_map/ppermute | solution.py:41
  15.9 0.0 copy-done.6
  15.9 1.3 %collective-permute-start.3 = (f32[8,128]{1,0:T(8,128)S(1)}, f32[8,128]{1,0:T(8,128)S(1)}, u32[]{:S(2)}, u32[]{:S(2)}) collective-permute-start(f32[8,128]{1,0:T(8,128)S(1)} %copy-done.6), channel_id=1, source_target_pairs={{1,0},{2,1},{3,2},{5,4},{6,5},{7,6},{9,8},{10,9},{11,10},{13,12},{... | collective-permute-start | bytes 12296 | tf_op jit(solution)/shard_map/ppermute | solution.py:45
  17.2 2.1 %collective-permute-done.2.refs_4_ = f32[240,128]{1,0:T(8,128)S(1)} collective-permute-done((f32[240,128]{1,0:T(8,128)S(1)}, f32[240,128]{1,0:T(8,128)S(1)}, u32[]{:S(2)}, u32[]{:S(2)}) %collective-permute-start.2) | collective-permute-done | bytes 122912 | tf_op jit(solution)/shard_map/ppermute | solution.py:41
  19.3 0.0 collective-permute-done.3.refs_5_.refs_8_
  19.4 1.4 %collective-permute-start.4 = (f32[384,128]{1,0:T(8,128)S(1)}, f32[384,128]{1,0:T(8,128)S(1)}, u32[]{:S(2)}, u32[]{:S(2)}) collective-permute-start(f32[384,128]{1,0:T(8,128)S(1)} %pad_maximum_fusion), channel_id=1, source_target_pairs={{0,1},{1,0},{2,3},{3,2},{4,5},{5,4},{6,7},{7,6},{8,9},{9,8},{10,11... | collective-permute-start | bytes 589832 | tf_op jit(solution)/shard_map/ppermute | solution.py:41
  20.8 0.0 copy-start.4
  20.8 0.0 copy-start.5
  20.8 1.0 %collective-permute-done.4 = f32[384,128]{1,0:T(8,128)S(1)} collective-permute-done((f32[384,128]{1,0:T(8,128)S(1)}, f32[384,128]{1,0:T(8,128)S(1)}, u32[]{:S(2)}, u32[]{:S(2)}) %collective-permute-start.4) | collective-permute-done | bytes 196640 | tf_op jit(solution)/shard_map/ppermute | solution.py:41
  21.8 0.6 %collective-permute-start.5 = (f32[768,128]{1,0:T(8,128)S(1)}, f32[768,128]{1,0:T(8,128)S(1)}, u32[]{:S(2)}, u32[]{:S(2)}) collective-permute-start(f32[768,128]{1,0:T(8,128)S(1)} %constant_dynamic-update-slice_fusion.refs_6_), channel_id=1, source_target_pairs={{0,2},{1,3},{2,0},{3,1},{4,6},{5,7},{6,4},{7,5},{8,10},{9,11},{10,... | collective-permute-start | bytes 1179656 | tf_op jit(solution)/shard_map/ppermute | solution.py:41
  22.5 0.0 copy-done.4
  22.5 0.0 copy-done.5
  22.5 10.3 %shard_map.131 = (f32[1944,128]{1,0:T(8,128)S(1)}, f32[1,128]{1,0:T(1,128)S(1)}, s32[595]{0:T(1024)S(1)}, bf16[512,128]{1,0:T(8,128)(2,1)S(1)}) custom-call(s32[2131]{0:T(1024)S(1)} %get-tuple-element.33.refs_0_, bf16[2048,128]{1,0:T(8,128)(2,1)S(1)} %get-tuple-element.34.refs_1_.refs_2_, f32[96,128]{1,0:T(8,128)S(1)} %collective-permute-done.refs_2_, ...), custom_call_target="tpu_custom_call" | custom-call | bytes 30000000 | tf_op jit(solution)/shard_map/pallas_call | solution.py:694
  32.7 0.5 collective-permute-done.5.refs_4_
  33.3 9.0 %shard_map.132 = (f32[192,128]{1,0:T(8,128)S(1)}, f32[48,128]{1,0:T(8,128)S(1)}, f32[1,128]{1,0:T(1,128)S(1)}, f32[2,24,128]{2,1,0:T(8,128)S(1)}, f32[2,32,128]{2,1,0:T(8,128)S(1)}) custom-call(s32[2131]{0:T(1024)S(1)} %get-tuple-element.33.refs_0_, s32[595]{0:T(1024)S(1)} %get-tuple-element.40.refs_1_, ...), custom_call_target="tpu_custom_call" | custom-call | tf_op jit(solution)/shard_map/pallas_call | solution.py:722
  42.3 5.0 %collective-permute-start.6 = (f32[48,128]{1,0:T(8,128)S(1)}, f32[48,128]{1,0:T(8,128)S(1)}, u32[]{:S(2)}, u32[]{:S(2)}) collective-permute-start(f32[48,128]{1,0:T(8,128)S(1)} %get-tuple-element.45), channel_id=1, source_target_pairs={{28,12},{0,16},{29,13},{1,17},{30,14},{2,18},{31,15},{3,19}} | collective-permute-start | bytes 73736 | tf_op jit(solution)/shard_map/ppermute | solution.py:742
  47.2 0.7 %collective-permute-start.7 = (f32[48,128]{1,0:T(8,128)S(1)}, f32[48,128]{1,0:T(8,128)S(1)}, u32[]{:S(2)}, u32[]{:S(2)}) collective-permute-start(f32[48,128]{1,0:T(8,128)S(1)} %get-tuple-element.45), channel_id=1, source_target_pairs={{4,12},{24,16},{5,13},{25,17},{6,14},{26,18},{7,15},{27,19}} | collective-permute-start | bytes 73736 | tf_op jit(solution)/shard_map/ppermute | solution.py:742
  47.9 0.7 %collective-permute-start.8 = (f32[48,128]{1,0:T(8,128)S(1)}, f32[48,128]{1,0:T(8,128)S(1)}, u32[]{:S(2)}, u32[]{:S(2)}) collective-permute-start(f32[48,128]{1,0:T(8,128)S(1)} %get-tuple-element.45), channel_id=1, source_target_pairs={{8,12},{20,16},{9,13},{21,17},{10,14},{22,18},{11,15},{23,19}} | collective-permute-start | bytes 73736 | tf_op jit(solution)/shard_map/ppermute | solution.py:742
  48.6 1.3 %collective-permute-start.9 = (f32[2,32,128]{2,1,0:T(8,128)S(1)}, f32[2,32,128]{2,1,0:T(8,128)S(1)}, u32[]{:S(2)}, u32[]{:S(2)}) collective-permute-start(f32[2,32,128]{2,1,0:T(8,128)S(1)} %get-tuple-element.46), channel_id=1, source_target_pairs={{4,0},{8,4},{12,8},{16,12},{20,16},{24,20},{28,24},{5,1},{9,5},{13... | collective-permute-start | bytes 98312 | tf_op jit(solution)/shard_map/ppermute | solution.py:45
  49.9 1.3 %collective-permute-start.10 = (f32[2,24,128]{2,1,0:T(8,128)S(1)}, f32[2,24,128]{2,1,0:T(8,128)S(1)}, u32[]{:S(2)}, u32[]{:S(2)}) collective-permute-start(f32[2,24,128]{2,1,0:T(8,128)S(1)} %get-tuple-element.47), channel_id=1, source_target_pairs={{1,0},{2,1},{3,2},{5,4},{6,5},{7,6},{9,8},{10,9},{11,10},{13,12},{... | collective-permute-start | bytes 73736 | tf_op jit(solution)/shard_map/ppermute | solution.py:45
  51.2 0.5 slice_bitcast_fusion
  51.7 0.0 collective-permute-done.6
  51.7 0.0 collective-permute-done.7
  51.7 0.0 collective-permute-done.8
  51.7 1.3 %collective-permute-done.10 = f32[2,24,128]{2,1,0:T(8,128)S(1)} collective-permute-done((f32[2,24,128]{2,1,0:T(8,128)S(1)}, f32[2,24,128]{2,1,0:T(8,128)S(1)}, u32[]{:S(2)}, u32[]{:S(2)}) %collective-permute-start.10) | collective-permute-done | bytes 24608 | tf_op jit(solution)/shard_map/ppermute | solution.py:45
  53.0 1.4 %collective-permute-done.9.refs_3_ = f32[2,32,128]{2,1,0:T(8,128)S(1)} collective-permute-done((f32[2,32,128]{2,1,0:T(8,128)S(1)}, f32[2,32,128]{2,1,0:T(8,128)S(1)}, u32[]{:S(2)}, u32[]{:S(2)}) %collective-permute-start.9) | collective-permute-done | bytes 32800 | tf_op jit(solution)/shard_map/ppermute | solution.py:45
  54.4 0.9 %shard_map.133 = (f32[3,8,8,128]{3,2,1,0:T(8,128)}, f32[8,8,128]{2,1,0:T(8,128)}, f32[8,8,128]{2,1,0:T(8,128)}) custom-call(f32[3,8,8,128]{3,2,1,0:T(8,128)S(1)} %copy-done, f32[3,8,8,128]{3,2,1,0:T(8,128)S(1)} %bitcast.16, f32[3,2,8,128]{3,2,1,0:T(8,128)S(1)} %bitcast.17, f32[3,2,8,128]{3,2,1,0:T(8,128)S(1)} %bitcast.18, f32[3,2,8,128]{3,2,1,0:T(8,128)S(1)} %bitcast.19, ...), custom_call_target="tpu_custom_call" | custom-call | tf_op jit(solution)/shard_map/pallas_call | solution.py:749
  (10 shorter events, 0.1 us)
Async XLA Ops:
  2.4 6.8 %collective-permute-start = (f32[96,128]{1,0:T(8,128)}, f32[96,128]{1,0:T(8,128)S(1)}, u32[]{:S(2)}, u32[]{:S(2)}) collective-permute-start(f32[96,128]{1,0:T(8,128)} %get-tuple-element.28), channel_id=1, source_target_pairs={{0,16},{1,17},{2,18},{3,19},{4,20},{5,21},{6,22},{7,23},{8,24},{9,... | collective-permute-start | bytes 147464 | tf_op jit(solution)/shard_map/ppermute | solution.py:41
  6.5 2.8 %copy-start.3 = (f32[48,128]{1,0:T(8,128)S(1)}, f32[48,128]{1,0:T(8,128)}, u32[]{:S(2)}) copy-start(f32[48,128]{1,0:T(8,128)} %get-tuple-element.29) | copy-start | bytes 73732
  7.2 3.5 %copy-start = (f32[3,8,8,128]{3,2,1,0:T(8,128)S(1)}, f32[3,8,8,128]{3,2,1,0:T(8,128)}, u32[]{:S(2)}) copy-start(f32[3,8,8,128]{3,2,1,0:T(8,128)} %points.3) | copy-start | bytes 294916
  9.3 1.5 %copy-start.1 = (s32[8,8,16]{2,1,0:T(8,128)S(1)}, s32[8,8,16]{2,1,0:T(8,128)}, u32[]{:S(2)}) copy-start(s32[8,8,16]{2,1,0:T(8,128)} %numbers.3) | copy-start | bytes 12292
  9.3 1.5 %copy-start.2 = (s32[8,8]{1,0:T(8,128)S(1)}, s32[8,8]{1,0:T(8,128)}, u32[]{:S(2)}) copy-start(s32[8,8]{1,0:T(8,128)} %counts.3) | copy-start | bytes 772
  9.3 5.0 %collective-permute-start.1 = (f32[144,128]{1,0:T(8,128)S(1)}, f32[144,128]{1,0:T(8,128)S(1)}, u32[]{:S(2)}, u32[]{:S(2)}) collective-permute-start(f32[144,128]{1,0:T(8,128)S(1)} %pad_maximum_fusion.3), channel_id=1, source_target_pairs={{0,8},{1,9},{2,10},{3,11},{4,12},{5,13},{6,14},{7,15},{8,0},{9,1},... | collective-permute-start | bytes 221192 | tf_op jit(solution)/shard_map/ppermute | solution.py:41
  14.3 1.6 %copy-start.6 = (f32[8,128]{1,0:T(8,128)S(1)}, f32[8,128]{1,0:T(8,128)}, u32[]{:S(2)}) copy-start(f32[8,128]{1,0:T(8,128)} %get-tuple-element.37) | copy-start | bytes 12292
  14.4 4.9 %collective-permute-start.2 = (f32[240,128]{1,0:T(8,128)S(1)}, f32[240,128]{1,0:T(8,128)S(1)}, u32[]{:S(2)}, u32[]{:S(2)}) collective-permute-start(f32[240,128]{1,0:T(8,128)S(1)} %pad_maximum_fusion.1), channel_id=1, source_target_pairs={{0,4},{1,5},{2,6},{3,7},{4,0},{5,1},{6,2},{7,3},{8,12},{9,13},{10,... | collective-permute-start | bytes 368648 | tf_op jit(solution)/shard_map/ppermute | solution.py:41
  15.9 3.4 %collective-permute-start.3 = (f32[8,128]{1,0:T(8,128)S(1)}, f32[8,128]{1,0:T(8,128)S(1)}, u32[]{:S(2)}, u32[]{:S(2)}) collective-permute-start(f32[8,128]{1,0:T(8,128)S(1)} %copy-done.6), channel_id=1, source_target_pairs={{1,0},{2,1},{3,2},{5,4},{6,5},{7,6},{9,8},{10,9},{11,10},{13,12},{... | collective-permute-start | bytes 12296 | tf_op jit(solution)/shard_map/ppermute | solution.py:45
  19.4 2.5 %collective-permute-start.4 = (f32[384,128]{1,0:T(8,128)S(1)}, f32[384,128]{1,0:T(8,128)S(1)}, u32[]{:S(2)}, u32[]{:S(2)}) collective-permute-start(f32[384,128]{1,0:T(8,128)S(1)} %pad_maximum_fusion), channel_id=1, source_target_pairs={{0,1},{1,0},{2,3},{3,2},{4,5},{5,4},{6,7},{7,6},{8,9},{9,8},{10,11... | collective-permute-start | bytes 589832 | tf_op jit(solution)/shard_map/ppermute | solution.py:41
  20.8 1.7 %copy-start.4 = (f32[6]{0:T(128)S(1)}, f32[6]{0:T(128)}, u32[]{:S(2)}) copy-start(f32[6]{0:T(128)} %param.14) | copy-start | bytes 76
  20.8 1.7 %copy-start.5 = (f32[6]{0:T(128)S(1)}, f32[6]{0:T(128)}, u32[]{:S(2)}) copy-start(f32[6]{0:T(128)} %param.13) | copy-start | bytes 76
  21.8 11.5 %collective-permute-start.5 = (f32[768,128]{1,0:T(8,128)S(1)}, f32[768,128]{1,0:T(8,128)S(1)}, u32[]{:S(2)}, u32[]{:S(2)}) collective-permute-start(f32[768,128]{1,0:T(8,128)S(1)} %constant_dynamic-update-slice_fusion.refs_6_), channel_id=1, source_target_pairs={{0,2},{1,3},{2,0},{3,1},{4,6},{5,7},{6,4},{7,5},{8,10},{9,11},{10,... | collective-permute-start | bytes 1179656 | tf_op jit(solution)/shard_map/ppermute | solution.py:41
  42.3 9.4 %collective-permute-start.6 = (f32[48,128]{1,0:T(8,128)S(1)}, f32[48,128]{1,0:T(8,128)S(1)}, u32[]{:S(2)}, u32[]{:S(2)}) collective-permute-start(f32[48,128]{1,0:T(8,128)S(1)} %get-tuple-element.45), channel_id=1, source_target_pairs={{28,12},{0,16},{29,13},{1,17},{30,14},{2,18},{31,15},{3,19}} | collective-permute-start | bytes 73736 | tf_op jit(solution)/shard_map/ppermute | solution.py:742
  47.2 4.5 %collective-permute-start.7 = (f32[48,128]{1,0:T(8,128)S(1)}, f32[48,128]{1,0:T(8,128)S(1)}, u32[]{:S(2)}, u32[]{:S(2)}) collective-permute-start(f32[48,128]{1,0:T(8,128)S(1)} %get-tuple-element.45), channel_id=1, source_target_pairs={{4,12},{24,16},{5,13},{25,17},{6,14},{26,18},{7,15},{27,19}} | collective-permute-start | bytes 73736 | tf_op jit(solution)/shard_map/ppermute | solution.py:742
  47.9 3.8 %collective-permute-start.8 = (f32[48,128]{1,0:T(8,128)S(1)}, f32[48,128]{1,0:T(8,128)S(1)}, u32[]{:S(2)}, u32[]{:S(2)}) collective-permute-start(f32[48,128]{1,0:T(8,128)S(1)} %get-tuple-element.45), channel_id=1, source_target_pairs={{8,12},{20,16},{9,13},{21,17},{10,14},{22,18},{11,15},{23,19}} | collective-permute-start | bytes 73736 | tf_op jit(solution)/shard_map/ppermute | solution.py:742
  48.6 5.8 %collective-permute-start.9 = (f32[2,32,128]{2,1,0:T(8,128)S(1)}, f32[2,32,128]{2,1,0:T(8,128)S(1)}, u32[]{:S(2)}, u32[]{:S(2)}) collective-permute-start(f32[2,32,128]{2,1,0:T(8,128)S(1)} %get-tuple-element.46), channel_id=1, source_target_pairs={{4,0},{8,4},{12,8},{16,12},{20,16},{24,20},{28,24},{5,1},{9,5},{13... | collective-permute-start | bytes 98312 | tf_op jit(solution)/shard_map/ppermute | solution.py:45
  49.9 3.1 %collective-permute-start.10 = (f32[2,24,128]{2,1,0:T(8,128)S(1)}, f32[2,24,128]{2,1,0:T(8,128)S(1)}, u32[]{:S(2)}, u32[]{:S(2)}) collective-permute-start(f32[2,24,128]{2,1,0:T(8,128)S(1)} %get-tuple-element.47), channel_id=1, source_target_pairs={{1,0},{2,1},{3,2},{5,4},{6,5},{7,6},{9,8},{10,9},{11,10},{13,12},{... | collective-permute-start | bytes 73736 | tf_op jit(solution)/shard_map/ppermute | solution.py:45

commit v10 on v9

--- a/solution.py
+++ b/solution.py
@@ -225,7 +225,7 @@
         line_feat[at, :] = line_block(rows).astype(BF16)
         return carry
 
-    lax.fori_loop(0, lines, block, 0, unroll=4)
+    lax.fori_loop(0, lines, block, 0, unroll=8)
 
 
 def code_items(first, bits, placed, numbers, counts, codes):

time: 55.6 us -> 55.4 us (level); the launches traced: 55.2 us -> 54.5 us
  starting transfers between devices: 19.2 us -> 17.4 us
  Pallas kernels: 25.4 us -> 27 us
    ppermute x3, starting transfers between devices: 6.28 us -> 4.48 us  [local(): lax.ppermute(lent_shift, 'slab', [(h ^ bit, h) for h in heavy])]
    pallas_call x1, Pallas kernels: 8.97 us -> 9.75 us  [local(): pl.pallas_call(functools.partial(late_kernel, own, lent, parts, bits), ou...]
    pallas_call x1, Pallas kernels: 10.3 us -> 11 us  [local(): pl.pallas_call(functools.partial(early_kernel, own, rows, slots, lent, bi...]
  transfers between devices with their start and end apart: 11 -> 11, of which waited for: 6 -> 5; matrix products, arithmetic and copies ran while one was open for 2% -> 2% of each run, Pallas kernels for 25% -> 27%
where the time goes in v10:
time: 55.4 us; the launch traced here: 54.5 us
  Pallas kernels  27 us (49%)
  starting transfers between devices  17.4 us (31%)
  waiting for transfers between devices  7.85 us (14%)
  local copies, waits for them, and re-layouts  1.37 us (2%)
  between operations  0.83 us (1%)
    pallas_call x1, Pallas kernels, local(): pl.pallas_call(functools.partial(early_kernel, own, rows, slots, lent, bi...  11 us
    pallas_call x1, Pallas kernels, local(): pl.pallas_call(functools.partial(late_kernel, own, lent, parts, bits), ou...  9.75 us
    ppermute x5, starting transfers between devices, swapped(): return lax.ppermute(value, ('slab', 'ctrl'), pairs)  9.06 us
    ppermute x5, waiting for transfers between devices, swapped(): return lax.ppermute(value, ('slab', 'ctrl'), pairs)  5.16 us
    ppermute x3, starting transfers between devices, local(): lax.ppermute(lent_shift, 'slab', [(h ^ bit, h) for h in heavy])  4.48 us
    ppermute x3, starting transfers between devices, shifted_back(): lax.ppermute(value, axis, [(i, i - 1) for i in range(1, lax.axis_size(axi...  3.86 us
    pallas_call x1, Pallas kernels, prepared(): pl.pallas_call(kernel, out_shape=(jax.ShapeDtypeStruct((2 * length + 3,),...  3.52 us
    ppermute x3, waiting for transfers between devices, shifted_back(): lax.ppermute(value, axis, [(i, i - 1) for i in range(1, lax.axis_size(axi...  2.68 us
  transfers between devices with their start and end apart: 11, of which 5 were waited for; matrix products, arithmetic and copies ran while one was open for 2% of the time, Pallas kernels for 27%

profile of v10, /device:TPU:0, one launch (start us, length us, event | category | flops | bytes accessed | tf_op | source)
XLA Modules:
  0.0 54.5 jit_solution(2781242727257098140)
XLA Ops:
  0.6 1.8 %shard_map.129 = (f32[8,128]{1,0:T(8,128)}, f32[96,128]{1,0:T(8,128)}, f32[48,128]{1,0:T(8,128)}) custom-call(f32[1,4096]{1,0:T(1,128)} %bitcast.21, f32[3,4096]{1,0:T(4,128)} %area.1, f32[3,4096]{1,0:T(4,128)} %center.1, f32[3,256]{1,0:T(4,128)} %points.2, f32[18,256]{1,0:T(8,128)} %modes.1, f32[192,128]{1,0:T(8,128)} %bitcast.13, s32[8,8,16]{2,1,0:T(8,128)} %numbers.3, ...), custom_call_target="tpu_custom_call" | custom-call | tf_op jit(solution)/shard_map/pallas_call | solution.py:623
  2.4 4.0 %collective-permute-start = (f32[96,128]{1,0:T(8,128)}, f32[96,128]{1,0:T(8,128)S(1)}, u32[]{:S(2)}, u32[]{:S(2)}) collective-permute-start(f32[96,128]{1,0:T(8,128)} %get-tuple-element.28), channel_id=1, source_target_pairs={{0,16},{1,17},{2,18},{3,19},{4,20},{5,21},{6,22},{7,23},{8,24},{9,... | collective-permute-start | bytes 147464 | tf_op jit(solution)/shard_map/ppermute | solution.py:41
  6.5 0.0 copy-start.3
  6.5 0.8 %slice.15 = f32[48,128]{1,0:T(8,128)S(1)} slice(f32[96,128]{1,0:T(8,128)} %get-tuple-element.28), slice={[0:48], [0:128]} | slice | bytes 49152 | tf_op jit(solution)/shard_map/slice | solution.py:637
  7.2 0.0 copy-start
  7.2 2.0 %collective-permute-done.refs_2_ = f32[96,128]{1,0:T(8,128)S(1)} collective-permute-done((f32[96,128]{1,0:T(8,128)}, f32[96,128]{1,0:T(8,128)S(1)}, u32[]{:S(2)}, u32[]{:S(2)}) %collective-permute-start) | collective-permute-done | bytes 49184 | tf_op jit(solution)/shard_map/ppermute | solution.py:41
  9.3 0.0 copy-done.3
  9.3 0.0 copy-start.1
  9.3 0.0 copy-start.2
  9.3 1.4 %collective-permute-start.1 = (f32[144,128]{1,0:T(8,128)S(1)}, f32[144,128]{1,0:T(8,128)S(1)}, u32[]{:S(2)}, u32[]{:S(2)}) collective-permute-start(f32[144,128]{1,0:T(8,128)S(1)} %pad_maximum_fusion.3), channel_id=1, source_target_pairs={{0,8},{1,9},{2,10},{3,11},{4,12},{5,13},{6,14},{7,15},{8,0},{9,1},... | collective-permute-start | bytes 221192 | tf_op jit(solution)/shard_map/ppermute | solution.py:41
  10.8 0.0 copy-done
  10.8 0.0 copy-done.1
  10.8 0.0 copy-done.2
  10.8 3.5 %shard_map.130 = (s32[2131]{0:T(1024)S(1)}, bf16[2048,128]{1,0:T(8,128)(2,1)S(1)}, f32[48,128]{1,0:T(8,128)S(1)}) custom-call(f32[192,128]{1,0:T(8,128)S(1)} %bitcast.14, s32[8,8,16]{2,1,0:T(8,128)S(1)} %copy-done.1, s32[8,8]{1,0:T(8,128)S(1)} %copy-done.2), custom_call_target="tpu_custom_call" | custom-call | bytes 8000000 | tf_op jit(solution)/shard_map/pallas_call | solution.py:312
  14.3 0.0 collective-permute-done.1.refs_3_
  14.3 0.0 copy-start.6
  14.4 1.6 %collective-permute-start.2 = (f32[240,128]{1,0:T(8,128)S(1)}, f32[240,128]{1,0:T(8,128)S(1)}, u32[]{:S(2)}, u32[]{:S(2)}) collective-permute-start(f32[240,128]{1,0:T(8,128)S(1)} %pad_maximum_fusion.1), channel_id=1, source_target_pairs={{0,4},{1,5},{2,6},{3,7},{4,0},{5,1},{6,2},{7,3},{8,12},{9,13},{10,... | collective-permute-start | bytes 368648 | tf_op jit(solution)/shard_map/ppermute | solution.py:41
  15.9 0.0 copy-done.6
  15.9 1.3 %collective-permute-start.3 = (f32[8,128]{1,0:T(8,128)S(1)}, f32[8,128]{1,0:T(8,128)S(1)}, u32[]{:S(2)}, u32[]{:S(2)}) collective-permute-start(f32[8,128]{1,0:T(8,128)S(1)} %copy-done.6), channel_id=1, source_target_pairs={{1,0},{2,1},{3,2},{5,4},{6,5},{7,6},{9,8},{10,9},{11,10},{13,12},{... | collective-permute-start | bytes 12296 | tf_op jit(solution)/shard_map/ppermute | solution.py:45
  17.2 2.1 %collective-permute-done.2.refs_4_ = f32[240,128]{1,0:T(8,128)S(1)} collective-permute-done((f32[240,128]{1,0:T(8,128)S(1)}, f32[240,128]{1,0:T(8,128)S(1)}, u32[]{:S(2)}, u32[]{:S(2)}) %collective-permute-start.2) | collective-permute-done | bytes 122912 | tf_op jit(solution)/shard_map/ppermute | solution.py:41
  19.3 0.0 collective-permute-done.3.refs_5_.refs_8_
  19.4 1.4 %collective-permute-start.4 = (f32[384,128]{1,0:T(8,128)S(1)}, f32[384,128]{1,0:T(8,128)S(1)}, u32[]{:S(2)}, u32[]{:S(2)}) collective-permute-start(f32[384,128]{1,0:T(8,128)S(1)} %pad_maximum_fusion), channel_id=1, source_target_pairs={{0,1},{1,0},{2,3},{3,2},{4,5},{5,4},{6,7},{7,6},{8,9},{9,8},{10,11... | collective-permute-start | bytes 589832 | tf_op jit(solution)/shard_map/ppermute | solution.py:41
  20.8 0.0 copy-start.4
  20.8 0.0 copy-start.5
  20.8 1.0 %collective-permute-done.4 = f32[384,128]{1,0:T(8,128)S(1)} collective-permute-done((f32[384,128]{1,0:T(8,128)S(1)}, f32[384,128]{1,0:T(8,128)S(1)}, u32[]{:S(2)}, u32[]{:S(2)}) %collective-permute-start.4) | collective-permute-done | bytes 196640 | tf_op jit(solution)/shard_map/ppermute | solution.py:41
  21.8 0.6 %collective-permute-start.5 = (f32[768,128]{1,0:T(8,128)S(1)}, f32[768,128]{1,0:T(8,128)S(1)}, u32[]{:S(2)}, u32[]{:S(2)}) collective-permute-start(f32[768,128]{1,0:T(8,128)S(1)} %constant_dynamic-update-slice_fusion.refs_6_), channel_id=1, source_target_pairs={{0,2},{1,3},{2,0},{3,1},{4,6},{5,7},{6,4},{7,5},{8,10},{9,11},{10,... | collective-permute-start | bytes 1179656 | tf_op jit(solution)/shard_map/ppermute | solution.py:41
  22.5 0.0 copy-done.4
  22.5 0.0 copy-done.5
  22.5 11.0 %shard_map.131 = (f32[1944,128]{1,0:T(8,128)S(1)}, f32[1,128]{1,0:T(1,128)S(1)}, s32[595]{0:T(1024)S(1)}, bf16[512,128]{1,0:T(8,128)(2,1)S(1)}) custom-call(s32[2131]{0:T(1024)S(1)} %get-tuple-element.33.refs_0_, bf16[2048,128]{1,0:T(8,128)(2,1)S(1)} %get-tuple-element.34.refs_1_.refs_2_, f32[96,128]{1,0:T(8,128)S(1)} %collective-permute-done.refs_2_, ...), custom_call_target="tpu_custom_call" | custom-call | bytes 30000000 | tf_op jit(solution)/shard_map/pallas_call | solution.py:694
  33.5 0.0 collective-permute-done.5.refs_4_
  33.5 9.8 %shard_map.132 = (f32[192,128]{1,0:T(8,128)S(1)}, f32[48,128]{1,0:T(8,128)S(1)}, f32[1,128]{1,0:T(1,128)S(1)}, f32[2,24,128]{2,1,0:T(8,128)S(1)}, f32[2,32,128]{2,1,0:T(8,128)S(1)}) custom-call(s32[2131]{0:T(1024)S(1)} %get-tuple-element.33.refs_0_, s32[595]{0:T(1024)S(1)} %get-tuple-element.40.refs_1_, ...), custom_call_target="tpu_custom_call" | custom-call | tf_op jit(solution)/shard_map/pallas_call | solution.py:722
  43.3 3.2 %collective-permute-start.6 = (f32[48,128]{1,0:T(8,128)S(1)}, f32[48,128]{1,0:T(8,128)S(1)}, u32[]{:S(2)}, u32[]{:S(2)}) collective-permute-start(f32[48,128]{1,0:T(8,128)S(1)} %get-tuple-element.45), channel_id=1, source_target_pairs={{28,12},{0,16},{29,13},{1,17},{30,14},{2,18},{31,15},{3,19}} | collective-permute-start | bytes 73736 | tf_op jit(solution)/shard_map/ppermute | solution.py:742
  46.4 0.7 %collective-permute-start.7 = (f32[48,128]{1,0:T(8,128)S(1)}, f32[48,128]{1,0:T(8,128)S(1)}, u32[]{:S(2)}, u32[]{:S(2)}) collective-permute-start(f32[48,128]{1,0:T(8,128)S(1)} %get-tuple-element.45), channel_id=1, source_target_pairs={{4,12},{24,16},{5,13},{25,17},{6,14},{26,18},{7,15},{27,19}} | collective-permute-start | bytes 73736 | tf_op jit(solution)/shard_map/ppermute | solution.py:742
  47.1 0.7 %collective-permute-start.8 = (f32[48,128]{1,0:T(8,128)S(1)}, f32[48,128]{1,0:T(8,128)S(1)}, u32[]{:S(2)}, u32[]{:S(2)}) collective-permute-start(f32[48,128]{1,0:T(8,128)S(1)} %get-tuple-element.45), channel_id=1, source_target_pairs={{8,12},{20,16},{9,13},{21,17},{10,14},{22,18},{11,15},{23,19}} | collective-permute-start | bytes 73736 | tf_op jit(solution)/shard_map/ppermute | solution.py:742
  47.8 1.3 %collective-permute-start.9 = (f32[2,32,128]{2,1,0:T(8,128)S(1)}, f32[2,32,128]{2,1,0:T(8,128)S(1)}, u32[]{:S(2)}, u32[]{:S(2)}) collective-permute-start(f32[2,32,128]{2,1,0:T(8,128)S(1)} %get-tuple-element.46), channel_id=1, source_target_pairs={{4,0},{8,4},{12,8},{16,12},{20,16},{24,20},{28,24},{5,1},{9,5},{13... | collective-permute-start | bytes 98312 | tf_op jit(solution)/shard_map/ppermute | solution.py:45
  49.1 1.3 %collective-permute-start.10 = (f32[2,24,128]{2,1,0:T(8,128)S(1)}, f32[2,24,128]{2,1,0:T(8,128)S(1)}, u32[]{:S(2)}, u32[]{:S(2)}) collective-permute-start(f32[2,24,128]{2,1,0:T(8,128)S(1)} %get-tuple-element.47), channel_id=1, source_target_pairs={{1,0},{2,1},{3,2},{5,4},{6,5},{7,6},{9,8},{10,9},{11,10},{13,12},{... | collective-permute-start | bytes 73736 | tf_op jit(solution)/shard_map/ppermute | solution.py:45
  50.4 0.5 slice_bitcast_fusion
  50.9 0.0 collective-permute-done.6
  50.9 0.0 collective-permute-done.7
  50.9 0.0 collective-permute-done.8
  50.9 1.3 %collective-permute-done.10 = f32[2,24,128]{2,1,0:T(8,128)S(1)} collective-permute-done((f32[2,24,128]{2,1,0:T(8,128)S(1)}, f32[2,24,128]{2,1,0:T(8,128)S(1)}, u32[]{:S(2)}, u32[]{:S(2)}) %collective-permute-start.10) | collective-permute-done | bytes 24608 | tf_op jit(solution)/shard_map/ppermute | solution.py:45
  52.2 1.4 %collective-permute-done.9.refs_3_ = f32[2,32,128]{2,1,0:T(8,128)S(1)} collective-permute-done((f32[2,32,128]{2,1,0:T(8,128)S(1)}, f32[2,32,128]{2,1,0:T(8,128)S(1)}, u32[]{:S(2)}, u32[]{:S(2)}) %collective-permute-start.9) | collective-permute-done | bytes 32800 | tf_op jit(solution)/shard_map/ppermute | solution.py:45
  53.6 0.9 %shard_map.133 = (f32[3,8,8,128]{3,2,1,0:T(8,128)}, f32[8,8,128]{2,1,0:T(8,128)}, f32[8,8,128]{2,1,0:T(8,128)}) custom-call(f32[3,8,8,128]{3,2,1,0:T(8,128)S(1)} %copy-done, f32[3,8,8,128]{3,2,1,0:T(8,128)S(1)} %bitcast.16, f32[3,2,8,128]{3,2,1,0:T(8,128)S(1)} %bitcast.17, f32[3,2,8,128]{3,2,1,0:T(8,128)S(1)} %bitcast.18, f32[3,2,8,128]{3,2,1,0:T(8,128)S(1)} %bitcast.19, ...), custom_call_target="tpu_custom_call" | custom-call | tf_op jit(solution)/shard_map/pallas_call | solution.py:749
  (10 shorter events, 0.1 us)
Async XLA Ops:
  2.4 6.8 %collective-permute-start = (f32[96,128]{1,0:T(8,128)}, f32[96,128]{1,0:T(8,128)S(1)}, u32[]{:S(2)}, u32[]{:S(2)}) collective-permute-start(f32[96,128]{1,0:T(8,128)} %get-tuple-element.28), channel_id=1, source_target_pairs={{0,16},{1,17},{2,18},{3,19},{4,20},{5,21},{6,22},{7,23},{8,24},{9,... | collective-permute-start | bytes 147464 | tf_op jit(solution)/shard_map/ppermute | solution.py:41
  6.5 2.8 %copy-start.3 = (f32[48,128]{1,0:T(8,128)S(1)}, f32[48,128]{1,0:T(8,128)}, u32[]{:S(2)}) copy-start(f32[48,128]{1,0:T(8,128)} %get-tuple-element.29) | copy-start | bytes 73732
  7.2 3.5 %copy-start = (f32[3,8,8,128]{3,2,1,0:T(8,128)S(1)}, f32[3,8,8,128]{3,2,1,0:T(8,128)}, u32[]{:S(2)}) copy-start(f32[3,8,8,128]{3,2,1,0:T(8,128)} %points.3) | copy-start | bytes 294916
  9.3 1.5 %copy-start.1 = (s32[8,8,16]{2,1,0:T(8,128)S(1)}, s32[8,8,16]{2,1,0:T(8,128)}, u32[]{:S(2)}) copy-start(s32[8,8,16]{2,1,0:T(8,128)} %numbers.3) | copy-start | bytes 12292
  9.3 1.5 %copy-start.2 = (s32[8,8]{1,0:T(8,128)S(1)}, s32[8,8]{1,0:T(8,128)}, u32[]{:S(2)}) copy-start(s32[8,8]{1,0:T(8,128)} %counts.3) | copy-start | bytes 772
  9.3 5.0 %collective-permute-start.1 = (f32[144,128]{1,0:T(8,128)S(1)}, f32[144,128]{1,0:T(8,128)S(1)}, u32[]{:S(2)}, u32[]{:S(2)}) collective-permute-start(f32[144,128]{1,0:T(8,128)S(1)} %pad_maximum_fusion.3), channel_id=1, source_target_pairs={{0,8},{1,9},{2,10},{3,11},{4,12},{5,13},{6,14},{7,15},{8,0},{9,1},... | collective-permute-start | bytes 221192 | tf_op jit(solution)/shard_map/ppermute | solution.py:41
  14.3 1.6 %copy-start.6 = (f32[8,128]{1,0:T(8,128)S(1)}, f32[8,128]{1,0:T(8,128)}, u32[]{:S(2)}) copy-start(f32[8,128]{1,0:T(8,128)} %get-tuple-element.37) | copy-start | bytes 12292
  14.4 4.9 %collective-permute-start.2 = (f32[240,128]{1,0:T(8,128)S(1)}, f32[240,128]{1,0:T(8,128)S(1)}, u32[]{:S(2)}, u32[]{:S(2)}) collective-permute-start(f32[240,128]{1,0:T(8,128)S(1)} %pad_maximum_fusion.1), channel_id=1, source_target_pairs={{0,4},{1,5},{2,6},{3,7},{4,0},{5,1},{6,2},{7,3},{8,12},{9,13},{10,... | collective-permute-start | bytes 368648 | tf_op jit(solution)/shard_map/ppermute | solution.py:41
  15.9 3.4 %collective-permute-start.3 = (f32[8,128]{1,0:T(8,128)S(1)}, f32[8,128]{1,0:T(8,128)S(1)}, u32[]{:S(2)}, u32[]{:S(2)}) collective-permute-start(f32[8,128]{1,0:T(8,128)S(1)} %copy-done.6), channel_id=1, source_target_pairs={{1,0},{2,1},{3,2},{5,4},{6,5},{7,6},{9,8},{10,9},{11,10},{13,12},{... | collective-permute-start | bytes 12296 | tf_op jit(solution)/shard_map/ppermute | solution.py:45
  19.4 2.5 %collective-permute-start.4 = (f32[384,128]{1,0:T(8,128)S(1)}, f32[384,128]{1,0:T(8,128)S(1)}, u32[]{:S(2)}, u32[]{:S(2)}) collective-permute-start(f32[384,128]{1,0:T(8,128)S(1)} %pad_maximum_fusion), channel_id=1, source_target_pairs={{0,1},{1,0},{2,3},{3,2},{4,5},{5,4},{6,7},{7,6},{8,9},{9,8},{10,11... | collective-permute-start | bytes 589832 | tf_op jit(solution)/shard_map/ppermute | solution.py:41
  20.8 1.7 %copy-start.4 = (f32[6]{0:T(128)S(1)}, f32[6]{0:T(128)}, u32[]{:S(2)}) copy-start(f32[6]{0:T(128)} %param.14) | copy-start | bytes 76
  20.8 1.7 %copy-start.5 = (f32[6]{0:T(128)S(1)}, f32[6]{0:T(128)}, u32[]{:S(2)}) copy-start(f32[6]{0:T(128)} %param.13) | copy-start | bytes 76
  21.8 11.7 %collective-permute-start.5 = (f32[768,128]{1,0:T(8,128)S(1)}, f32[768,128]{1,0:T(8,128)S(1)}, u32[]{:S(2)}, u32[]{:S(2)}) collective-permute-start(f32[768,128]{1,0:T(8,128)S(1)} %constant_dynamic-update-slice_fusion.refs_6_), channel_id=1, source_target_pairs={{0,2},{1,3},{2,0},{3,1},{4,6},{5,7},{6,4},{7,5},{8,10},{9,11},{10,... | collective-permute-start | bytes 1179656 | tf_op jit(solution)/shard_map/ppermute | solution.py:41
  43.3 7.6 %collective-permute-start.6 = (f32[48,128]{1,0:T(8,128)S(1)}, f32[48,128]{1,0:T(8,128)S(1)}, u32[]{:S(2)}, u32[]{:S(2)}) collective-permute-start(f32[48,128]{1,0:T(8,128)S(1)} %get-tuple-element.45), channel_id=1, source_target_pairs={{28,12},{0,16},{29,13},{1,17},{30,14},{2,18},{31,15},{3,19}} | collective-permute-start | bytes 73736 | tf_op jit(solution)/shard_map/ppermute | solution.py:742
  46.4 4.5 %collective-permute-start.7 = (f32[48,128]{1,0:T(8,128)S(1)}, f32[48,128]{1,0:T(8,128)S(1)}, u32[]{:S(2)}, u32[]{:S(2)}) collective-permute-start(f32[48,128]{1,0:T(8,128)S(1)} %get-tuple-element.45), channel_id=1, source_target_pairs={{4,12},{24,16},{5,13},{25,17},{6,14},{26,18},{7,15},{27,19}} | collective-permute-start | bytes 73736 | tf_op jit(solution)/shard_map/ppermute | solution.py:742
  47.1 3.8 %collective-permute-start.8 = (f32[48,128]{1,0:T(8,128)S(1)}, f32[48,128]{1,0:T(8,128)S(1)}, u32[]{:S(2)}, u32[]{:S(2)}) collective-permute-start(f32[48,128]{1,0:T(8,128)S(1)} %get-tuple-element.45), channel_id=1, source_target_pairs={{8,12},{20,16},{9,13},{21,17},{10,14},{22,18},{11,15},{23,19}} | collective-permute-start | bytes 73736 | tf_op jit(solution)/shard_map/ppermute | solution.py:742
  47.8 5.8 %collective-permute-start.9 = (f32[2,32,128]{2,1,0:T(8,128)S(1)}, f32[2,32,128]{2,1,0:T(8,128)S(1)}, u32[]{:S(2)}, u32[]{:S(2)}) collective-permute-start(f32[2,32,128]{2,1,0:T(8,128)S(1)} %get-tuple-element.46), channel_id=1, source_target_pairs={{4,0},{8,4},{12,8},{16,12},{20,16},{24,20},{28,24},{5,1},{9,5},{13... | collective-permute-start | bytes 98312 | tf_op jit(solution)/shard_map/ppermute | solution.py:45
  49.1 3.1 %collective-permute-start.10 = (f32[2,24,128]{2,1,0:T(8,128)S(1)}, f32[2,24,128]{2,1,0:T(8,128)S(1)}, u32[]{:S(2)}, u32[]{:S(2)}) collective-permute-start(f32[2,24,128]{2,1,0:T(8,128)S(1)} %get-tuple-element.47), channel_id=1, source_target_pairs={{1,0},{2,1},{3,2},{5,4},{6,5},{7,6},{9,8},{10,9},{11,10},{13,12},{... | collective-permute-start | bytes 73736 | tf_op jit(solution)/shard_map/ppermute | solution.py:45
